TPU v7x, 128 devices: a whole 4x4x4 slice. The times are simulated.
128 devices in a mesh: rows: 32 (over y, z, x_lo), cols: 4 (over x_hi, core).
Axes of the slice: x: 4 (x_hi: 2, x_lo: 2; x = x_hi * 2 + x_lo), y: 4, z: 4, core: 2. Of those that a mesh axis runs over, the one named last changes fastest.
Arguments:
- image: bfloat16 [1024, 192, 512], P('rows', None, 'cols'), may hold values from -6 to 6
- w_expand: bfloat16 [192, 768], replicated, may hold values from -0.4375 to 0.4375
- dw_kernel: bfloat16 [3, 3, 768], replicated, may hold values from -2 to 2
- w_project: bfloat16 [192, 768], replicated, may hold values from -0.21875 to 0.21875
- block_qkv: bfloat16 [192, 576], replicated, may hold values from -2 to 2
- block_out: bfloat16 [192, 192], replicated, may hold values from -0.4375 to 0.4375
- block_bias: float32 [6, 15, 15], replicated, may hold values from -4 to 4
- mlp_in: bfloat16 [192, 768], replicated, may hold values from -0.4375 to 0.4375
- mlp_out: bfloat16 [192, 768], replicated, may hold values from -0.21875 to 0.21875
- grid_qkv: bfloat16 [192, 576], replicated, may hold values from -2 to 2
- grid_out: bfloat16 [192, 192], replicated, may hold values from -0.4375 to 0.4375
- grid_bias: float32 [6, 15, 15], replicated, may hold values from -4 to 4
- mlp2_in: bfloat16 [192, 768], replicated, may hold values from -0.4375 to 0.4375
- mlp2_out: bfloat16 [192, 768], replicated, may hold values from -0.21875 to 0.21875
Outputs:
- result: bfloat16 [1024, 192, 512], P('rows', None, 'cols')
All inputs are finite; a program needn't handle non-finite values.
Results may differ from a plain program's by a relative error of at most 0.03.
Values may be sent and summed in bfloat16 or wider, within the bound.
No kernel may reach another device: no remote copies, remote signals or barrier semaphores. Data moves between devices by JAX's collectives and lax.ppermute only.
A program may use at most 128 MiB of HBM per device.

v0:
```python
import jax
import jax.numpy as jnp
from jax import lax
from jax.sharding import PartitionSpec as P

WIN = 8


def padded_2(cells, sides, width):
    for axis, dim in sides:
        count = lax.axis_size(axis)
        ends = count - 1
        head = lax.slice_in_dim(cells, 0, width, axis=dim)
        tail = lax.slice_in_dim(cells, cells.shape[dim] - width, cells.shape[dim], axis=dim)
        cells = jnp.concatenate(
            [
                lax.ppermute(tail, axis, [(i, (i + 1) % count) for i in range(ends)]),
                cells,
                lax.ppermute(head, axis, [((i + 1) % count, i) for i in range(ends)]),
            ],
            axis=dim,
        )
    return cells


def normalize(tokens):
    values = tokens.astype(jnp.float32)
    centre = values - jnp.mean(values, axis=-1, keepdims=True)
    spread = jnp.mean(centre * centre, axis=-1, keepdims=True)
    return (centre * lax.rsqrt(spread + 1e-05)).astype(jnp.bfloat16)


def relative_bias(table):
    span = table.shape[1]
    side = (span + 1) // 2
    place = jnp.arange(side * side, dtype=jnp.int32)
    row_of = place // side
    col_of = place % side
    index = (row_of[:, None] - row_of[None, :] + side - 1) * span + (
        col_of[:, None] - col_of[None, :] + side - 1
    )
    flat = table.reshape(table.shape[0], span * span)
    return jnp.take(flat, index, axis=1)


def attend(tokens, w_qkv, w_out, table):
    groups, count, width = tokens.shape
    heads = table.shape[0]
    size = width // heads
    normed = normalize(tokens)
    qkv = jnp.einsum("gtd,de->gte", normed, w_qkv, preferred_element_type=jnp.float32).astype(
        jnp.bfloat16
    )
    qkv = qkv.reshape(groups, count, 3, heads, size)
    scores = jnp.einsum(
        "gshe,gthe->ghst", qkv[:, :, 0], qkv[:, :, 1], preferred_element_type=jnp.float32
    )
    scores = scores * size ** (-0.5) + relative_bias(table)[None]
    weights = jax.nn.softmax(scores, axis=-1).astype(jnp.bfloat16)
    mixed = jnp.einsum(
        "ghst,gthe->gshe", weights, qkv[:, :, 2], preferred_element_type=jnp.float32
    ).astype(jnp.bfloat16)
    mixed = mixed.reshape(groups, count, width)
    added = jnp.einsum("gtd,de->gte", mixed, w_out, preferred_element_type=jnp.float32)
    return (tokens.astype(jnp.float32) + added).astype(jnp.bfloat16)


def feed(tokens, w_in, w_out):
    normed = normalize(tokens)
    hidden = jax.nn.gelu(jnp.dot(normed, w_in, preferred_element_type=jnp.float32)).astype(
        jnp.bfloat16
    )
    added = jnp.dot(hidden, w_out.T, preferred_element_type=jnp.float32)
    return (tokens.astype(jnp.float32) + added).astype(jnp.bfloat16)


def expand(values, w_expand):
    return jax.nn.gelu(jnp.dot(values, w_expand, preferred_element_type=jnp.float32)).astype(
        jnp.bfloat16
    )


def body(
    image,
    w_expand,
    dw_kernel,
    w_project,
    block_qkv,
    block_out,
    block_bias,
    mlp_in,
    mlp_out,
    grid_qkv,
    grid_out,
    grid_bias,
    mlp2_in,
    mlp2_out,
):
    rows_here, width, cols_here = image.shape
    cells = image.transpose(0, 2, 1)
    hidden_width = w_expand.shape[1]
    expanded = expand(cells.reshape(-1, width), w_expand).reshape(
        rows_here, cols_here, hidden_width
    )
    padded = padded_2(expanded, (("rows", 0), ("cols", 1)), 1)
    conv = jnp.zeros((rows_here, cols_here, hidden_width), jnp.float32)
    for shift_r in range(3):
        for shift_c in range(3):
            conv = conv + padded[
                shift_r : shift_r + rows_here, shift_c : shift_c + cols_here
            ].astype(jnp.float32) * dw_kernel[shift_r, shift_c].astype(jnp.float32)
    mobile = jax.nn.gelu(conv).astype(jnp.bfloat16)
    added = jnp.dot(
        mobile.reshape(-1, hidden_width), w_project.T, preferred_element_type=jnp.float32
    )
    stream = (cells.astype(jnp.float32) + added.reshape(rows_here, cols_here, width)).astype(
        jnp.bfloat16
    )
    tiles = stream.reshape(rows_here // WIN, WIN, cols_here // WIN, WIN, width).transpose(
        0, 2, 1, 3, 4
    )
    tiles = attend(tiles.reshape(-1, WIN * WIN, width), block_qkv, block_out, block_bias)
    stream = tiles.reshape(rows_here // WIN, cols_here // WIN, WIN, WIN, width).transpose(
        0, 2, 1, 3, 4
    )
    stream = feed(stream.reshape(-1, width), mlp_in, mlp_out)
    n_rows = lax.axis_size("rows")
    n_cols = lax.axis_size("cols")
    per_col = WIN // n_cols
    span = cols_here // WIN
    share = rows_here // n_rows
    spread = stream.reshape(rows_here, per_col, n_cols, span, width)
    arrived = lax.all_to_all(
        lax.all_to_all(spread, "rows", split_axis=0, concat_axis=0, tiled=True),
        "cols",
        split_axis=2,
        concat_axis=2,
        tiled=True,
    )
    members = arrived.reshape(WIN, n_rows // WIN, share, per_col, n_cols, span, width)
    groups = members.transpose(1, 2, 5, 0, 4, 3, 6).reshape(-1, WIN * WIN, width)
    groups = attend(groups, grid_qkv, grid_out, grid_bias)
    laid = groups.reshape(n_rows // WIN, share, span, WIN, n_cols, per_col, width)
    outgoing = laid.transpose(3, 0, 1, 5, 4, 2, 6).reshape(rows_here, per_col, n_cols, span, width)
    returned = lax.all_to_all(
        lax.all_to_all(outgoing, "rows", split_axis=0, concat_axis=0, tiled=True),
        "cols",
        split_axis=2,
        concat_axis=2,
        tiled=True,
    )
    final = feed(returned.reshape(-1, width), mlp2_in, mlp2_out)
    return final.reshape(rows_here, cols_here, width).transpose(0, 2, 1)


def solution(mesh):
    in_specs = (
        P("rows", None, "cols"),
        P(),
        P(),
        P(),
        P(),
        P(),
        P(),
        P(),
        P(),
        P(),
        P(),
        P(),
        P(),
        P(),
    )
    out_specs = P("rows", None, "cols")
    return jax.shard_map(body, mesh=mesh, in_specs=in_specs, out_specs=out_specs, check_vma=False)
```

profile of v0, /device:TPU:1, one launch (start us, length us, event | category | flops | bytes accessed | tf_op | source)
XLA Modules:
  0.0 388.5 jit_solution(15391036172750429495)
XLA Ops:
  1.0 5.8 %fusion.9 = bf16[4096,768]{1,0:T(8,128)(2,1)S(1)} fusion(bf16[192,768]{1,0:T(8,128)(2,1)S(1)} %copy-done, bf16[32,192,128]{2,1,0:T(8,128)(2,1)} %param.16), kind=kOutput, calls=%fused_computation.15 | convolution fusion | flops 1236271104 | bytes 8159232 | tf_op jit(solution)/shard_map/dot_general | solution.py:78
  10.2 3.9 %collective-permute-start = (bf16[1,128,768]{2,1,0:T(8,128)(2,1)}, bf16[1,128,768]{2,1,0:T(8,128)(2,1)S(1)}, u32[]{:S(2)}, u32[]{:S(2)}) collective-permute-start(bf16[1,128,768]{2,1,0:T(8,128)(2,1)} %get-tuple-element.19), channel_id=1, source_target_pairs={{0,4},{4,8},{8,12},{12,16},{16,20},{20,24},{24,28},{28,32},{32,36}... | collective-permute-start | bytes 589832 | tf_op jit(solution)/shard_map/ppermute | solution.py:17
  16.2 14.1 %gather_fusion = f32[4096,6]{1,0:T(8,128)} fusion(f32[6,225]{0,1:T(8,128)S(1)} %copy.165, s32[4096]{0:T(1024)S(1)} %broadcast_clamp_fusion), kind=kCustom, calls=%fused_computation.clone | custom fusion | bytes 212992 | tf_op jit(solution)/shard_map/jit(_take)/gather | solution.py:43
  33.2 14.1 %gather_fusion.1 = f32[4096,6]{1,0:T(8,128)} fusion(f32[6,225]{0,1:T(8,128)S(1)} %copy.186, s32[4096]{0:T(1024)S(1)} %broadcast_clamp_fusion), kind=kCustom, calls=%fused_computation.1.clone | custom fusion | bytes 212992 | tf_op jit(solution)/shard_map/jit(_take)/gather | solution.py:43
  52.4 5.2 %collective-permute-start.2 = (bf16[34,1,768]{2,1,0:T(2,128)(2,1)S(1)}, bf16[34,1,768]{2,1,0:T(2,128)(2,1)S(1)}, u32[]{:S(2)}, u32[]{:S(2)}) collective-permute-start(bf16[34,1,768]{2,1,0:T(2,128)(2,1)S(1)} %get-tuple-element.17), channel_id=1, source_target_pairs={{0,1},{1,2},{2,3},{4,5},{5,6},{6,7},{8,9},{9,10},{10,11},{12,13},{... | collective-permute-start | bytes 156680 | tf_op jit(solution)/shard_map/ppermute | solution.py:17
  60.1 4.9 %collective-permute-done.3 = bf16[34,1,768]{2,1,0:T(2,128)(2,1)S(1)} collective-permute-done((bf16[34,1,768]{2,1,0:T(2,128)(2,1)S(1)}, bf16[34,1,768]{2,1,0:T(2,128)(2,1)S(1)}, u32[]{:S(2)}, u32[]{:S(2)}) %collective-permute-start.3) | collective-permute-done | bytes 52256 | tf_op jit(solution)/shard_map/ppermute | solution.py:19
  65.1 3.6 maximum_maximum_fusion
  68.7 22.8 %fusion.84 = f32[32,128,192]{1,2,0:T(8,128)} fusion(bf16[32,128,768]{2,1,0:T(8,128)(2,1)S(1)} %bitcast.147, bf16[34,129,768]{2,1,0:T(8,128)(2,1)S(1)} %get-tuple-element.16, bf16[1,128,768]{2,1,0:T(8,128)(2,1)S(1)} %collective-permute-done.1, bf16[34,129,768]{2,1,0:T(8,128)(2,1)S(1)} %get-tuple-element.15, ...), kind=kOutput, calls=%fused_computation.103 | convolution fusion | flops 1327497216 | bytes 49483776 | tf_op jit(solution)/shard_map/dot_general | solution.py:113
  91.5 5.1 %copy.151 = f32[32,128,192]{2,1,0:T(8,128)} copy(f32[32,128,192]{1,2,0:T(8,128)} %fusion.84) | data formatting | bytes 6291456 | tf_op jit(solution)/shard_map/convert_element_type | solution.py:65
  99.8 4.9 %copy.152 = f32[4,16,8,8,192]{4,3,2,1,0:T(8,128)} copy(f32[4,16,8,8,192]{4,3,1,2,0:T(8,128)} %bitcast.136) | data formatting | bytes 6291456 | tf_op jit(solution)/shard_map/convert_element_type | solution.py:65
  108.3 5.7 %convolution_convert_fusion.1 = bf16[64,64,576]{2,1,0:T(8,128)(2,1)} fusion(f32[64,64,192]{2,1,0:T(8,128)} %bitcast.138, f32[64,64]{1,0:T(8,128)S(1)} %copy.159, f32[64,64]{1,0:T(8,128)S(1)} %copy.155, bf16[192,576]{1,0:T(8,128)(2,1)S(1)} %copy-done.7), kind=kOutput, calls=%fused_computation.91 | convolution fusion | flops 910688256 | bytes 8118272 | tf_op jit(solution)/shard_map/gtd,de->gte/dot_general | solution.py:51
  114.0 10.1 %copy.160 = bf16[64,64,576]{1,2,0:T(8,128)(2,1)} copy(bf16[64,64,576]{2,1,0:T(8,128)(2,1)} %convolution_convert_fusion.1) | data formatting | bytes 9437184 | tf_op jit(solution)/shard_map/convert_element_type | solution.py:51
  124.1 4.7 %fusion.67 = f32[64,6,64,64]{2,3,1,0:T(8,128)S(1)} fusion(bf16[64,64,3,6,32]{1,4,3,2,0:T(8,128)(2,1)} %bitcast.150), kind=kOutput, calls=%fused_computation.86 | convolution fusion | flops 100663296 | bytes 12582912 | tf_op jit(solution)/shard_map/gshe,gthe->ghst/dot_general | solution.py:55
  128.9 7.9 %fusion.113 = (f32[64,6,64]{2,1,0:T(8,128)S(1)}, f32[64,6,64,64]{2,3,1,0:T(8,128)}) fusion(f32[64,6,64,64]{2,3,1,0:T(8,128)S(1)} %fusion.67, f32[6,64,64]{1,2,0:T(8,128)S(1)} %get-tuple-element.22), kind=kOutput, calls=%fused_computation.161 | output fusion | flops 9437247 | bytes 12779520 | tf_op jit(solution)/shard_map/sub | solution.py:59
  136.8 7.4 %fusion.69 = bf16[64,6,32,64]{3,2,1,0:T(8,128)(2,1)S(1)} fusion(f32[64,6,64,64]{2,3,1,0:T(8,128)} %get-tuple-element.24, f32[64,6,64]{2,1,0:T(8,128)S(1)} %get-tuple-element.23, bf16[64,64,3,6,32]{1,4,3,2,0:T(8,128)(2,1)} %bitcast.151), kind=kOutput, calls=%fused_computation.93 | convolution fusion | flops 104595456 | bytes 17399808 | tf_op jit(solution)/shard_map/ghst,gthe->gshe/dot_general | solution.py:60
  150.2 3.7 copy.170
  154.0 8.2 %fusion.57 = bf16[4096,192]{0,1:T(8,128)(2,1)} fusion(f32[4096,192]{0,1:T(8,128)S(1)} %copy.170, bf16[192,768]{1,0:T(8,128)(2,1)} %param.24, bf16[192,768]{1,0:T(8,128)(2,1)} %param.23, f32[4096,192]{1,0:T(8,128)} %bitcast.155, f32[4096]{0:T(1024)S(1)} %rsqrt.47, f32[4096]{0:T(1024)S(1)} %div.68), kind=kOutput, calls=%fused_computation.64 | convolution fusion | flops 2448162816 | bytes 8486912 | tf_op jit(solution)/shard_map/dot_general | solution.py:73
  165.3 36.0 %all_to_all.20 = bf16[32,2,4,16,192]{4,3,2,1,0:T(8,128)(2,1)S(1)} all-to-all(bf16[32,2,4,16,192]{4,3,2,1,0:T(8,128)(2,1)S(1)} %bitcast.159), channel_id=1, replica_groups=mesh['rows'=32,'cols'=4] {'rows'}, dimensions={0} | all-to-all | bytes 3145728 | tf_op jit(solution)/shard_map/all_to_all | solution.py:134
  201.6 28.5 %all_to_all.21 = bf16[32,2,4,16,192]{4,3,1,0,2:T(8,128)(2,1)S(1)} all-to-all(bf16[32,2,4,16,192]{4,3,1,0,2:T(8,128)(2,1)S(1)} %copy.172), channel_id=1, replica_groups=mesh['rows'=32,'cols'=4] {'cols'}, dimensions={2} | all-to-all | bytes 3145728 | tf_op jit(solution)/shard_map/all_to_all | solution.py:133
  232.6 4.7 %fusion.112 = f32[4,16,8,4,2]{4,3,2,1,0:T(4,128)S(1)} fusion(f32[8,4,1,2,4,16,192]{6,5,3,1,0,4,2:T(8,128)S(1)} %convert.26), kind=kLoop, calls=%fused_computation.160 | loop fusion | flops 782336 | bytes 3162112 | tf_op jit(solution)/shard_map/reduce_sum | solution.py:28
  239.5 4.3 %copy.224 = f32[8,4,1,2,4,16,192]{6,3,4,0,5,1,2:T(2,128)} copy(bf16[8,4,1,2,4,16,192]{6,5,3,1,0,4,2:T(8,128)(2,1)S(1)} %bitcast.153) | data formatting | bytes 4718592 | tf_op jit(solution)/shard_map/convert_element_type | solution.py:65
  244.0 10.6 %multiply_reduce_fusion.1 = f32[4,16,8,4,2]{4,3,2,1,0:T(4,128)S(1)} fusion(f32[4,16,8,4,2]{4,3,2,1,0:T(4,128)S(1)} %copy.177, f32[8,4,1,2,4,16,192]{6,5,3,1,0,4,2:T(8,128)} %copy-done.4), kind=kLoop, calls=%fused_computation.76 | loop fusion | flops 2355200 | bytes 3178496 | tf_op jit(solution)/shard_map/reduce_sum | solution.py:29
  255.8 6.6 %reshape.275 = f32[64,64,192]{2,1,0:T(8,128)} reshape(f32[4,1,16,8,4,2,192]{6,5,4,3,2,0,1:T(2,128)} %bitcast.158) | data formatting | bytes 6291456 | tf_op jit(solution)/shard_map/convert_element_type | solution.py:65
  262.3 5.7 %convolution_convert_fusion = bf16[64,64,576]{2,1,0:T(8,128)(2,1)} fusion(f32[64,64,192]{2,1,0:T(8,128)} %reshape.275, f32[64,64]{1,0:T(8,128)S(1)} %copy.180, f32[64,64]{1,0:T(8,128)S(1)} %copy.176, bf16[192,576]{1,0:T(8,128)(2,1)S(1)} %copy-done.8), kind=kOutput, calls=%fused_computation.90 | convolution fusion | flops 910688256 | bytes 8118272 | tf_op jit(solution)/shard_map/gtd,de->gte/dot_general | solution.py:51
  268.0 10.1 %copy.181 = bf16[64,64,576]{1,2,0:T(8,128)(2,1)} copy(bf16[64,64,576]{2,1,0:T(8,128)(2,1)} %convolution_convert_fusion) | data formatting | bytes 9437184 | tf_op jit(solution)/shard_map/convert_element_type | solution.py:51
  278.1 4.8 %fusion.66 = f32[64,6,64,64]{2,3,1,0:T(8,128)S(1)} fusion(bf16[64,64,3,6,32]{1,4,3,2,0:T(8,128)(2,1)} %bitcast.148), kind=kOutput, calls=%fused_computation.82 | convolution fusion | flops 100663296 | bytes 12582912 | tf_op jit(solution)/shard_map/gshe,gthe->ghst/dot_general | solution.py:55
  282.9 7.8 %fusion.114 = (f32[64,6,64]{2,1,0:T(8,128)S(1)}, f32[64,6,64,64]{2,3,1,0:T(8,128)}) fusion(f32[64,6,64,64]{2,3,1,0:T(8,128)S(1)} %fusion.66, f32[6,64,64]{1,2,0:T(8,128)S(1)} %copy-done.6), kind=kOutput, calls=%fused_computation.162 | output fusion | flops 9437247 | bytes 12779520 | tf_op jit(solution)/shard_map/sub | solution.py:59
  290.7 7.5 %fusion.68 = bf16[64,6,32,64]{3,2,1,0:T(8,128)(2,1)S(1)} fusion(f32[64,6,64,64]{2,3,1,0:T(8,128)} %get-tuple-element.26, f32[64,6,64]{2,1,0:T(8,128)S(1)} %get-tuple-element.25, bf16[64,64,3,6,32]{1,4,3,2,0:T(8,128)(2,1)} %bitcast.149), kind=kOutput, calls=%fused_computation.92 | convolution fusion | flops 104595456 | bytes 17399808 | tf_op jit(solution)/shard_map/ghst,gthe->gshe/dot_general | solution.py:60
  305.4 31.1 %all_to_all.22 = bf16[32,2,4,16,192]{4,3,2,1,0:T(8,128)(2,1)S(1)} all-to-all(bf16[32,2,4,16,192]{4,3,2,1,0:T(8,128)(2,1)S(1)} %bitcast.160), channel_id=1, replica_groups=mesh['rows'=32,'cols'=4] {'rows'}, dimensions={0} | all-to-all | bytes 3145728 | tf_op jit(solution)/shard_map/all_to_all | solution.py:146
  336.8 30.9 %all_to_all.23 = bf16[32,2,4,16,192]{4,3,1,0,2:T(8,128)(2,1)S(1)} all-to-all(bf16[32,2,4,16,192]{4,3,1,0,2:T(8,128)(2,1)S(1)} %copy.191), channel_id=1, replica_groups=mesh['rows'=32,'cols'=4] {'cols'}, dimensions={2} | all-to-all | bytes 3145728 | tf_op jit(solution)/shard_map/all_to_all | solution.py:145
  373.3 3.7 copy.198
  377.0 8.3 %fusion.89 = bf16[24,32,8,128]{3,2,1,0:T(8,128)(2,1)} fusion(f32[4096,192]{0,1:T(8,128)S(1)} %copy.198, bf16[192,768]{1,0:T(8,128)(2,1)} %param.29, bf16[192,768]{1,0:T(8,128)(2,1)} %param.28, f32[4096,192]{1,0:T(8,128)} %bitcast.157, f32[4096]{0:T(1024)S(1)} %rsqrt.51, f32[4096]{0:T(1024)S(1)} %div.76), kind=kOutput, calls=%fused_computation.107 | convolution fusion | flops 2448162816 | bytes 8486912 | tf_op jit(solution)/shard_map/dot_general | solution.py:73
  (108 shorter events, 55.0 us)
Async XLA Ops:
  0.0 1.0 copy-start
  0.0 15.7 %copy-start.11 = (f32[6,15,15]{2,1,0:T(8,128)S(1)}, f32[6,15,15]{2,1,0:T(8,128)}, u32[]{:S(2)}) copy-start(f32[6,15,15]{2,1,0:T(8,128)} %param.22) | copy-start | bytes 16204
  0.0 15.8 %copy-start.12 = (f32[6,15,15]{2,1,0:T(8,128)S(1)}, f32[6,15,15]{2,1,0:T(8,128)}, u32[]{:S(2)}) copy-start(f32[6,15,15]{2,1,0:T(8,128)} %param.27) | copy-start | bytes 16204
  6.8 2.7 copy-start.5
  10.2 40.5 %collective-permute-start = (bf16[1,128,768]{2,1,0:T(8,128)(2,1)}, bf16[1,128,768]{2,1,0:T(8,128)(2,1)S(1)}, u32[]{:S(2)}, u32[]{:S(2)}) collective-permute-start(bf16[1,128,768]{2,1,0:T(8,128)(2,1)} %get-tuple-element.19), channel_id=1, source_target_pairs={{0,4},{4,8},{8,12},{12,16},{16,20},{20,24},{24,28},{28,32},{32,36}... | collective-permute-start | bytes 589832 | tf_op jit(solution)/shard_map/ppermute | solution.py:17
  14.1 36.5 %collective-permute-start.1 = (bf16[1,128,768]{2,1,0:T(8,128)(2,1)S(1)}, bf16[1,128,768]{2,1,0:T(8,128)(2,1)S(1)}, u32[]{:S(2)}, u32[]{:S(2)}) collective-permute-start(bf16[1,128,768]{2,1,0:T(8,128)(2,1)S(1)} %get-tuple-element.20), channel_id=1, source_target_pairs={{4,0},{8,4},{12,8},{16,12},{20,16},{24,20},{28,24},{32,28},{36,32}... | collective-permute-start | bytes 589832 | tf_op jit(solution)/shard_map/ppermute | solution.py:19
  30.3 34.7 %slice-start = ((s8[6291456]{0:T(1024)(128)(4,1)}), s8[2097152]{0:T(1024)(128)(4,1)S(1)}, s32[]{:S(2)}) async-start(s8[6291456]{0:T(1024)(128)(4,1)} %bitcast.144), calls=%async_computation.4 | async-start | bytes 4194304
  33.1 26.9 %copy-start.13 = (bf16[3,3,768]{2,1,0:T(4,128)(2,1)S(1)}, bf16[3,3,768]{2,1,0:T(4,128)(2,1)}, u32[]{:S(2)}) copy-start(bf16[3,3,768]{2,1,0:T(4,128)(2,1)} %param.18) | copy-start | bytes 41476
  49.9 15.2 %slice-start.1 = ((s8[6291456]{0:T(1024)(128)(4,1)}), s8[4194304]{0:T(1024)(128)(4,1)S(1)}, s32[]{:S(2)}) async-start(s8[6291456]{0:T(1024)(128)(4,1)} %bitcast.144), calls=%async_computation.5 | async-start | bytes 8388608
  52.4 7.8 %collective-permute-start.2 = (bf16[34,1,768]{2,1,0:T(2,128)(2,1)S(1)}, bf16[34,1,768]{2,1,0:T(2,128)(2,1)S(1)}, u32[]{:S(2)}, u32[]{:S(2)}) collective-permute-start(bf16[34,1,768]{2,1,0:T(2,128)(2,1)S(1)} %get-tuple-element.17), channel_id=1, source_target_pairs={{0,1},{1,2},{2,3},{4,5},{5,6},{6,7},{8,9},{9,10},{10,11},{12,13},{... | collective-permute-start | bytes 156680 | tf_op jit(solution)/shard_map/ppermute | solution.py:17
  57.6 7.5 %collective-permute-start.3 = (bf16[34,1,768]{2,1,0:T(2,128)(2,1)S(1)}, bf16[34,1,768]{2,1,0:T(2,128)(2,1)S(1)}, u32[]{:S(2)}, u32[]{:S(2)}) collective-permute-start(bf16[34,1,768]{2,1,0:T(2,128)(2,1)S(1)} %get-tuple-element.18), channel_id=1, source_target_pairs={{1,0},{2,1},{3,2},{5,4},{6,5},{7,6},{9,8},{10,9},{11,10},{13,12},{... | collective-permute-start | bytes 156680 | tf_op jit(solution)/shard_map/ppermute | solution.py:19
  60.1 8.6 %copy-start.14 = (bf16[192,768]{1,0:T(8,128)(2,1)S(1)}, bf16[192,768]{1,0:T(8,128)(2,1)}, u32[]{:S(2)}) copy-start(bf16[192,768]{1,0:T(8,128)(2,1)} %param.19) | copy-start | bytes 884740
  99.8 8.5 %copy-start.7 = (bf16[192,576]{1,0:T(8,128)(2,1)S(1)}, bf16[192,576]{1,0:T(8,128)(2,1)}, u32[]{:S(2)}) copy-start(bf16[192,576]{1,0:T(8,128)(2,1)} %param.20) | copy-start | bytes 663556
  136.8 7.4 %copy-start.2 = (f32[4,16,8,8,192]{4,3,2,1,0:T(8,128)S(1)}, f32[4,16,8,8,192]{4,3,2,1,0:T(8,128)}, u32[]{:S(2)}) copy-start(f32[4,16,8,8,192]{4,3,2,1,0:T(8,128)} %copy.152) | copy-start | bytes 9437188
  136.8 7.5 %copy-start.9 = (bf16[192,192]{1,0:T(8,128)(2,1)S(1)}, bf16[192,192]{1,0:T(8,128)(2,1)}, u32[]{:S(2)}) copy-start(bf16[192,192]{1,0:T(8,128)(2,1)} %param.21) | copy-start | bytes 221188
  230.7 2.0 copy-start.4
  254.6 7.8 %copy-start.8 = (bf16[192,576]{1,0:T(8,128)(2,1)S(1)}, bf16[192,576]{1,0:T(8,128)(2,1)}, u32[]{:S(2)}) copy-start(bf16[192,576]{1,0:T(8,128)(2,1)} %param.25) | copy-start | bytes 663556
  278.1 4.8 %copy-start.6 = (f32[6,64,64]{1,2,0:T(8,128)S(1)}, f32[6,64,64]{1,2,0:T(8,128)}, u32[]{:S(2)}) copy-start(f32[6,64,64]{1,2,0:T(8,128)} %get-tuple-element.21) | copy-start | bytes 294916
  290.7 7.5 %copy-start.3 = (f32[64,64,192]{2,1,0:T(8,128)S(1)}, f32[64,64,192]{2,1,0:T(8,128)}, u32[]{:S(2)}) copy-start(f32[64,64,192]{2,1,0:T(8,128)} %reshape.275) | copy-start | bytes 9437188
  290.7 7.5 %copy-start.10 = (bf16[192,192]{1,0:T(8,128)(2,1)S(1)}, bf16[192,192]{1,0:T(8,128)(2,1)}, u32[]{:S(2)}) copy-start(bf16[192,192]{1,0:T(8,128)(2,1)} %param.26) | copy-start | bytes 221188
  377.0 11.3 %copy-start.1 = (bf16[192,768]{1,0:T(8,128)(2,1)S(1)}, bf16[192,768]{1,0:T(8,128)(2,1)}, u32[]{:S(2)}) copy-start(bf16[192,768]{1,0:T(8,128)(2,1)} %param.17) | copy-start | bytes 884740
where the time goes:
time: 394 us; the launch traced here: 389 us
  blocking collectives  126 us (32%)
  local copies, waits for them, and re-layouts  111 us (28%)
  matrix products  84.6 us (21%)
  other arithmetic  48.1 us (12%)
  starting transfers between devices  12.9 us (3%)
  waiting for transfers between devices  4.94 us (1%)
    all_to_all x1, blocking collectives, body(): lax.all_to_all(spread, 'rows', split_axis=0, concat_axis=0, tiled=True)  36 us
    gather x4, local copies, waits for them, and re-layouts, relative_bias(): return jnp.take(flat, index, axis=1)  33.6 us
    all_to_all x1, blocking collectives, body(): lax.all_to_all(outgoing, 'rows', split_axis=0, concat_axis=0, tiled=True)  31.1 us
    all_to_all x1, blocking collectives, body(): lax.all_to_all(lax.all_to_all(outgoing, 'rows', split_axis=0, concat_axis...  30.9 us
    all_to_all x1, blocking collectives, body(): lax.all_to_all(lax.all_to_all(spread, 'rows', split_axis=0, concat_axis=0...  28.5 us
    dot_general x1, matrix products, body(): jnp.dot(mobile.reshape(-1, hidden_width), w_project.T, preferred_element_...  22.8 us
    convert_element_type x4, local copies, waits for them, and re-layouts, attend(): return (tokens.astype(jnp.float32) + added).astype(jnp.bfloat16)  20.8 us
    convert_element_type x2, local copies, waits for them, and re-layouts, attend(): jnp.einsum('gtd,de->gte', normed, w_qkv, preferred_element_type=jnp.float32)  20.2 us
  transfers between devices with their start and end apart: 4, of which 1 were waited for; matrix products, arithmetic and copies ran while one was open for 9% of the time, Pallas kernels for 0%

commit v1 on v0

v1 whole, which is shorter than its diff:
```python
import functools
import math

import jax
import jax.numpy as jnp
from jax import lax
from jax.experimental import pallas as pl
from jax.experimental.pallas import tpu as pltpu
from jax.sharding import Mesh, PartitionSpec as P

WIN = 8
D = 192
HID = 768
HEADS = 6
SIZE = 32
COLS = 128
TOKENS = 64
QUAD = 256
ROWS_CHUNK = 8
N_CALLS = 2
LOG2E = 1.4426950408889634
F32 = jnp.float32
BF16 = jnp.bfloat16
NN = (((1,), (0,)), ((), ()))
NT = (((1,), (1,)), ((), ()))
TN = (((0,), (0,)), ((), ()))


def dot(a, b, dims=NN):
    return lax.dot_general(a, b, dims, preferred_element_type=F32)


def gelu(x):
    c0 = math.sqrt(2.0 / math.pi)
    inner = x * (c0 + (c0 * 0.044715) * (x * x))
    half = 0.5 * x
    return half + half * jnp.tanh(inner)


def norm(x):
    centre = x - jnp.mean(x, axis=-1, keepdims=True)
    spread = jnp.mean(centre * centre, axis=-1, keepdims=True)
    return (centre * lax.rsqrt(spread + 1e-05)).astype(BF16)


def mlp(s, w_in, w_out):
    hidden = gelu(dot(norm(s), w_in)).astype(BF16)
    return s + dot(hidden, w_out, NT)


def head_rows(q, heads):
    lane = lax.broadcasted_iota(jnp.int32, q.shape, 1) // SIZE
    zero = jnp.zeros_like(q)
    return jnp.concatenate([jnp.where(lane == h, q, zero) for h in range(heads)], axis=0)


def softmax_keys(scores):
    top = jnp.max(scores, axis=0, keepdims=True)
    weights = jnp.exp2(scores - top)
    total = jnp.sum(weights, axis=0, keepdims=True)
    return (weights * (1.0 / total)).astype(BF16)


def head_pick(out, heads):
    lane = lax.broadcasted_iota(jnp.int32, (TOKENS, out.shape[1]), 1) // SIZE
    got = out[:TOKENS]
    for h in range(1, heads):
        got = jnp.where(lane == h, out[h * TOKENS : (h + 1) * TOKENS], got)
    return got


def attend(s, wq, wk, wv, w_out, bias):
    n = norm(s)
    q = (dot(n, wq) * (SIZE**-0.5 * LOG2E)).astype(BF16)
    k = dot(n, wk).astype(BF16)
    v = dot(n, wv).astype(BF16)
    mixed = []
    for g in range(s.shape[0] // TOKENS):
        at = slice(g * TOKENS, (g + 1) * TOKENS)
        qg, kg, vg = q[at], k[at], v[at]
        parts = []
        for lo, hi, h0, h1 in ((0, 128, 0, 4), (128, 192, 4, 6)):
            count = h1 - h0
            scores = dot(kg[:, lo:hi], head_rows(qg[:, lo:hi], count), NT)
            scores = scores + bias[:, h0 * TOKENS : h1 * TOKENS]
            out = dot(softmax_keys(scores), vg[:, lo:hi], TN)
            parts.append(head_pick(out, count))
        mixed.append(jnp.concatenate(parts, axis=1).astype(BF16))
    return s + dot(jnp.concatenate(mixed, axis=0), w_out)


def split_qkv(w_ref, wq, wk, wv):
    wq[...] = w_ref[:, 0:D]
    wk[...] = w_ref[:, D : 2 * D]
    wv[...] = w_ref[:, 2 * D : 3 * D]


def first_kernel(
    first, last,
    image, before, after, top, bottom, left, right,
    w_expand, dw, w_project, w_qkv, w_out, bias, w_in, w_back,
    out, expanded, stream, side, wq, wk, wv,
):
    step = pl.program_id(0)
    steps = pl.num_programs(0)
    split_qkv(w_qkv, wq, wk, wv)

    def expand(row, x):
        tokens = x.T
        expanded[row] = gelu(dot(tokens, w_expand[...]))
        return tokens

    above = before[0]
    if first:
        above = jnp.where(step == 0, top[0], above)
    expand(0, above)
    expand(1, image[0])

    start = pl.multiple_of(step * ROWS_CHUNK, 8)
    for index, halo in enumerate((left, right)):
        cells = gelu(dot(halo[pl.ds(start, 16), :].astype(BF16), w_expand[...]))
        tap = 2 * index
        total = jnp.zeros((8, HID), F32)
        for i in range(3):
            total = total + cells[i : i + 8] * dw[3 * i + tap : 3 * i + tap + 1, :]
        for r in range(8):
            side[index, r] = jnp.broadcast_to(total[r : r + 1], (8, HID))

    def row(r, carry):
        below = image[jnp.minimum(r + 1, ROWS_CHUNK - 1)]
        edge = after[0]
        if last:
            edge = jnp.where(step == steps - 1, bottom[0], edge)
        expand(r + 2, jnp.where(r == ROWS_CHUNK - 1, edge, below))
        place = lax.broadcasted_iota(jnp.int32, (8, 128), 0)
        mobile = []
        for block in range(HID // 128):
            lanes = slice(block * 128, (block + 1) * 128)
            e = [expanded[r + i, :, lanes] for i in range(3)]
            taps = [
                sum(e[i] * dw[3 * i + k : 3 * i + k + 1, lanes] for i in range(3))
                for k in range(3)
            ]
            head = pltpu.roll(taps[0], 1, 0)
            tail = pltpu.roll(taps[2], COLS - 1, 0)
            head = jnp.concatenate(
                [jnp.where(place == 0, side[0, r, :, lanes], head[:8]), head[8:]], axis=0
            )
            tail = jnp.concatenate(
                [tail[:-8], jnp.where(place == 7, side[1, r, :, lanes], tail[-8:])], axis=0
            )
            mobile.append(gelu(head + taps[1] + tail).astype(BF16))
        mobile = jnp.concatenate(mobile, axis=1)
        tokens = image[r].T.astype(F32) + dot(mobile, w_project[...], NT)
        stream[:, r] = tokens.reshape(COLS // WIN, WIN, D)
        return carry

    lax.fori_loop(0, ROWS_CHUNK, row, 0)

    def windows(index, carry):
        at = pl.ds(index * 4, 4)
        s = stream[at].reshape(QUAD, D)
        s = attend(s, wq[...], wk[...], wv[...], w_out[...], bias)
        s = mlp(s, w_in[...], w_back[...])
        stream[at] = s.reshape(4, WIN, WIN, D)
        return carry

    lax.fori_loop(0, COLS // WIN // 4, windows, 0)

    for r in range(ROWS_CHUNK):
        rows = stream[:, r].reshape(2, 4, 16, D).astype(BF16)
        out[0, pl.ds(4 * r, 4), 0:16, :] = rows[0, :, :, 0:128]
        out[0, pl.ds(4 * r, 4), 16:32, :] = rows[1, :, :, 0:128]
        out[0, pl.ds(4 * r, 4), 32:48, :] = jnp.concatenate(
            [rows[0, :, :, 128:], rows[1, :, :, 128:]], axis=-1
        )


def grid_kernel(inp, w_qkv, w_out, bias, out, lo, hi, wq, wk, wv):
    split_qkv(w_qkv, wq, wk, wv)

    def load(src, carry):
        at = pl.multiple_of(src * 32, 32)
        lo[pl.ds(at, 32), :] = inp[0, src, 0:32, :].astype(F32)
        both = inp[0, src, 32:48, :].astype(F32)
        hi[pl.ds(at, 16), :] = both
        hi[pl.ds(at + 16, 16), :] = pltpu.roll(both, 64, 1)
        return carry

    lax.fori_loop(0, 32, load, 0)

    def groups(index, carry):
        first = index * 4
        picks = [pl.ds(first + g, TOKENS, stride=16) for g in range(4)]
        s = jnp.concatenate(
            [jnp.concatenate([lo[at, :], hi[at, :][:, :64]], axis=1) for at in picks], axis=0
        )
        s = attend(s, wq[...], wk[...], wv[...], w_out[...], bias)
        for g, at in enumerate(picks):
            rows = s[g * TOKENS : (g + 1) * TOKENS]
            lo[at, :] = rows[:, :128]
            hi[at, :] = jnp.concatenate([rows[:, 128:], rows[:, 128:]], axis=1)
        return carry

    lax.fori_loop(0, 4, groups, 0)

    def store(src, carry):
        at = pl.multiple_of(src * 32, 32)
        out[0, src, 0:32, :] = lo[pl.ds(at, 32), :].astype(BF16)
        lane = lax.broadcasted_iota(jnp.int32, (16, 128), 1)
        out[0, src, 32:48, :] = jnp.where(
            lane < 64, hi[pl.ds(at, 16), :], hi[pl.ds(at + 16, 16), :]
        ).astype(BF16)
        return carry

    lax.fori_loop(0, 32, store, 0)


def last_kernel(inp, w_in, w_back, out):
    def rows(index, carry):
        for half in range(2):
            r = 2 * index + half
            got = inp[0, pl.ds(4 * r, 4)].astype(F32)
            low = [got[:, 0:16], got[:, 16:32]]
            both = got[:, 32:48]
            high = [both[:, :, :64], both[:, :, 64:]]
            s = jnp.concatenate(
                [
                    jnp.concatenate([low[i].reshape(64, 128), high[i].reshape(64, 64)], axis=1)
                    for i in range(2)
                ],
                axis=0,
            )
            out[r] = mlp(s, w_in[...], w_back[...]).astype(BF16).T
        return carry

    lax.fori_loop(0, ROWS_CHUNK // 2, rows, 0)


def whole(shape):
    return pl.BlockSpec(shape, lambda k: (0,) * len(shape))


def vm(limit):
    return pltpu.CompilerParams(vmem_limit_bytes=limit << 20, dimension_semantics=("arbitrary",))


def call_first(call, chunks, image, top, bottom, left, right, weights):
    steps = chunks
    base = call * chunks
    total = image.shape[0]
    first, last = call == 0, (base + chunks) * ROWS_CHUNK == total
    rows = pl.BlockSpec((ROWS_CHUNK, D, COLS), lambda k: (base + k, 0, 0))
    before = pl.BlockSpec(
        (1, D, COLS), lambda k: (jnp.maximum((base + k) * ROWS_CHUNK - 1, 0), 0, 0)
    )
    after = pl.BlockSpec(
        (1, D, COLS), lambda k: (jnp.minimum((base + k + 1) * ROWS_CHUNK, total - 1), 0, 0)
    )
    left = left[base * ROWS_CHUNK : base * ROWS_CHUNK + chunks * ROWS_CHUNK + 8]
    right = right[base * ROWS_CHUNK : base * ROWS_CHUNK + chunks * ROWS_CHUNK + 8]
    small = [top, bottom, left, right] + weights
    tokens = chunks * ROWS_CHUNK * COLS
    return pl.pallas_call(
        functools.partial(first_kernel, first, last),
        grid=(steps,),
        in_specs=[rows, before, after] + [whole(a.shape) for a in small],
        out_specs=pl.BlockSpec((1, 32, 48, 128), lambda k: (k, 0, 0, 0)),
        out_shape=jax.ShapeDtypeStruct((chunks, 32, 48, 128), BF16),
        scratch_shapes=[
            pltpu.VMEM((ROWS_CHUNK + 2, COLS, HID), F32),
            pltpu.VMEM((COLS // WIN, WIN, WIN, D), F32),
            pltpu.VMEM((2, 8, 8, HID), F32),
            pltpu.VMEM((D, D), BF16),
            pltpu.VMEM((D, D), BF16),
            pltpu.VMEM((D, D), BF16),
        ],
        compiler_params=vm(48),
        cost_estimate=pl.CostEstimate(
            flops=tokens * 2000000, bytes_accessed=tokens * 800, transcendentals=tokens * 2700
        ),
        name="first",
    )(image, image, image, *small)


def call_grid(arrived, weights):
    chunks = arrived.shape[0]
    tokens = chunks * ROWS_CHUNK * COLS
    block = pl.BlockSpec((1, 32, 48, 128), lambda k: (k, 0, 0, 0))
    return pl.pallas_call(
        grid_kernel,
        grid=(chunks,),
        in_specs=[block] + [whole(a.shape) for a in weights],
        out_specs=block,
        out_shape=jax.ShapeDtypeStruct(arrived.shape, BF16),
        scratch_shapes=[
            pltpu.VMEM((1024, 128), F32),
            pltpu.VMEM((1024, 128), F32),
            pltpu.VMEM((D, D), BF16),
            pltpu.VMEM((D, D), BF16),
            pltpu.VMEM((D, D), BF16),
        ],
        compiler_params=vm(32),
        cost_estimate=pl.CostEstimate(
            flops=tokens * 500000, bytes_accessed=tokens * 800, transcendentals=tokens * 400
        ),
        name="grid",
    )(arrived, *weights)


def call_last(returned, w_in, w_back):
    chunks = returned.shape[0]
    tokens = chunks * ROWS_CHUNK * COLS
    return pl.pallas_call(
        last_kernel,
        grid=(chunks,),
        in_specs=[
            pl.BlockSpec((1, 32, 48, 128), lambda k: (k, 0, 0, 0)),
            whole(w_in.shape),
            whole(w_back.shape),
        ],
        out_specs=pl.BlockSpec((ROWS_CHUNK, D, COLS), lambda k: (k, 0, 0)),
        out_shape=jax.ShapeDtypeStruct((chunks * ROWS_CHUNK, D, COLS), BF16),
        compiler_params=vm(32),
        cost_estimate=pl.CostEstimate(
            flops=tokens * 600000, bytes_accessed=tokens * 800, transcendentals=tokens * 800
        ),
        name="last",
    )(returned, w_in, w_back)


def bias_rows(table):
    span = 2 * WIN - 1
    cols = jnp.stack([table[:, :, 7 - v : 15 - v] for v in range(WIN)], axis=0)
    both = jnp.stack([cols[:, :, 7 - u : 15 - u, :] for u in range(WIN)], axis=0)
    return both.reshape(TOKENS, HEADS * TOKENS) * LOG2E


def shift(x, axis, count, step):
    if step > 0:
        pairs = [(i, i + 1) for i in range(count - 1)]
    else:
        pairs = [(i + 1, i) for i in range(count - 1)]
    return lax.ppermute(x, axis, pairs)


ROW_AXES = ("y", "zh", "zl", "xl")
COL_AXES = ("xh", "core")
GROUP = ("y", "zh", "xh", "core")


def body(
    image, w_expand, dw_kernel, w_project, block_qkv, block_out, block_bias, mlp_in, mlp_out,
    grid_qkv, grid_out, grid_bias, mlp2_in, mlp2_out,
):
    rows = image.shape[0]
    top = shift(image[rows - 1 :], ROW_AXES, 32, 1)
    bottom = shift(image[:1], ROW_AXES, 32, -1)
    ends = [
        jnp.concatenate([top[:, :, c], image[:, :, c], bottom[:, :, c]], axis=0)
        for c in (0, COLS - 1)
    ]
    left = shift(ends[1], COL_AXES, 4, 1)
    right = shift(ends[0], COL_AXES, 4, -1)
    left = jnp.pad(left.astype(F32), ((0, 6), (0, 0)))
    right = jnp.pad(right.astype(F32), ((0, 6), (0, 0)))
    bias1 = bias_rows(block_bias)
    bias2 = bias_rows(grid_bias)
    weights = [
        w_expand, dw_kernel.reshape(9, HID).astype(F32), w_project, block_qkv, block_out, bias1,
        mlp_in, mlp_out,
    ]
    chunks = rows // ROWS_CHUNK // N_CALLS
    outs = []
    for call in range(N_CALLS):
        sent = call_first(call, chunks, image, top, bottom, left, right, weights)
        arrived = lax.all_to_all(sent, GROUP, 1, 1, tiled=True)
        mixed = call_grid(arrived, [grid_qkv, grid_out, bias2])
        back = lax.all_to_all(mixed, GROUP, 1, 1, tiled=True)
        outs.append(call_last(back, mlp2_in, mlp2_out))
    return jnp.concatenate(outs, axis=0)


def solution(mesh):
    names = ("y", "zh", "zl", "xl", "xh", "core")
    fine = Mesh(mesh.devices.reshape(4, 2, 2, 2, 2, 2), names)
    spec = P(ROW_AXES, None, COL_AXES)
    return jax.shard_map(
        body, mesh=fine, in_specs=(spec,) + (P(),) * 13, out_specs=spec, check_vma=False
    )
```

time: 394 us -> 218 us (0.55); the launches traced: 389 us -> 216 us
  blocking collectives: 126 us -> 0 us
  Pallas kernels: 0 us -> 121 us
  local copies, waits for them, and re-layouts: 111 us -> 25.3 us
  matrix products: 84.6 us -> 0 us
  other arithmetic: 48.1 us -> 3.03 us
  starting transfers between devices: 12.9 us -> 51.6 us
  waiting for transfers between devices: 4.94 us -> 15.2 us
    all_to_all x4 -> x0, blocking collectives: 126 us -> none  [the longest x1 36 us: body(): lax.all_to_all(spread, 'rows', split_axis=0, concat_axis=0, tiled=True)]
    pallas_call x0 -> x6, Pallas kernels: none -> 121 us  [the longest x2 69 us: call_first(): pl.pallas_call(functools.partial(first_kernel, first, last), grid=(steps,...]
    dot_general x12 -> x0, matrix products: 84.6 us -> none  [the longest x1 22.8 us: body(): jnp.dot(mobile.reshape(-1, hidden_width), w_project.T, preferred_element_...]
    convert_element_type x11 -> x1, local copies, waits for them, and re-layouts: 56.6 us -> 0.02 us  [body(): dw_kernel.reshape(9, HID).astype(F32)]
    all_to_all x0 -> x4, starting transfers between devices: none -> 37.7 us  [the longest x2 19.7 us: body(): back = lax.all_to_all(mixed, GROUP, 1, 1, tiled=True)]
    gather x4 -> x0, local copies, waits for them, and re-layouts: 33.6 us -> none  [relative_bias(): return jnp.take(flat, index, axis=1)]
    reduce_sum x8 -> x0, other arithmetic: 25.2 us -> none  [the longest x4 16.3 us: normalize(): spread = jnp.mean(centre * centre, axis=-1, keepdims=True)]
    sub x2 -> x0, other arithmetic: 15.7 us -> none  [attend(): weights = jax.nn.softmax(scores, axis=-1).astype(jnp.bfloat16)]
  transfers between devices with their start and end apart: 4 -> 8, of which waited for: 1 -> 2; matrix products, arithmetic and copies ran while one was open for 9% -> 12% of each run, Pallas kernels for 0% -> 37%
where the time goes in v1:
time: 218 us; the launch traced here: 216 us
  Pallas kernels  121 us (56%)
  starting transfers between devices  51.6 us (24%)
  local copies, waits for them, and re-layouts  25.3 us (12%)
  waiting for transfers between devices  15.2 us (7%)
  other arithmetic  3.03 us (1%)
    pallas_call x2, Pallas kernels, call_first(): pl.pallas_call(functools.partial(first_kernel, first, last), grid=(steps,...  69 us
    pallas_call x2, Pallas kernels, call_grid(): pl.pallas_call(grid_kernel, grid=(chunks,), in_specs=[block] + [whole(a.s...  39.2 us
    all_to_all x2, starting transfers between devices, body(): back = lax.all_to_all(mixed, GROUP, 1, 1, tiled=True)  19.7 us
    all_to_all x2, starting transfers between devices, body(): arrived = lax.all_to_all(sent, GROUP, 1, 1, tiled=True)  17.9 us
    ppermute x4, starting transfers between devices, shift(): return lax.ppermute(x, axis, pairs)  13.9 us
    pallas_call x2, Pallas kernels, call_last(): pl.pallas_call(last_kernel, grid=(chunks,), in_specs=[pl.BlockSpec((1, 32...  12.6 us
    unnamed x62, local copies, waits for them, and re-layouts  12.3 us
    all_to_all x2, waiting for transfers between devices, body(): back = lax.all_to_all(mixed, GROUP, 1, 1, tiled=True)  10.6 us
  transfers between devices with their start and end apart: 8, of which 2 were waited for; matrix products, arithmetic and copies ran while one was open for 12% of the time, Pallas kernels for 37%

profile of v1, /device:TPU:1, one launch (start us, length us, event | category | flops | bytes accessed | tf_op | source)
XLA Modules:
  0.0 216.5 jit_solution(17363231441015342050)
XLA Ops:
  0.0 0.8 fusion.17
  0.8 1.3 collective-permute-start.1
  2.1 4.7 %collective-permute-start = (bf16[1,192,128]{2,1,0:T(8,128)(2,1)S(1)}, bf16[1,192,128]{2,1,0:T(8,128)(2,1)S(1)}, u32[]{:S(2)}, u32[]{:S(2)}) collective-permute-start(bf16[1,192,128]{2,1,0:T(8,128)(2,1)S(1)} %get-tuple-element.12), channel_id=1, source_target_pairs={{0,4},{4,8},{8,12},{12,16},{16,20},{20,24},{24,28},{28,32},{32,36}... | collective-permute-start | bytes 147464 | tf_op jit(solution)/shard_map/ppermute | solution.py:344
  6.9 4.4 %fusion.16 = (bf16[32,192,1]{2,1,0:T(8,128)(2,1)}, bf16[32,192,1]{2,1,0:T(8,128)(2,1)}) fusion(bf16[32,192,128]{2,1,0:T(8,128)(2,1)} %after.3), kind=kLoop, calls=%fused_computation.59 | loop fusion | bytes 49152 | tf_op jit(solution)/shard_map/slice | solution.py:360
  12.4 0.7 fusion.7
  15.7 0.8 mul.11.bias
  16.6 2.0 copy.30
  18.6 1.9 copy.29
  21.0 6.0 %collective-permute-start.2 = (bf16[34,192]{1,0:T(8,128)(2,1)S(1)}, bf16[34,192]{1,0:T(8,128)(2,1)S(1)}, u32[]{:S(2)}, u32[]{:S(2)}) collective-permute-start(bf16[34,192]{1,0:T(8,128)(2,1)S(1)} %pad_maximum_fusion.1), channel_id=1, source_target_pairs={{0,1},{1,2},{2,3},{4,5},{5,6},{6,7},{8,9},{9,10},{10,11},{12,13},{... | collective-permute-start | bytes 39176 | tf_op jit(solution)/shard_map/ppermute | solution.py:344
  27.0 1.9 collective-permute-start.3
  29.0 4.6 %collective-permute-done.3 = bf16[34,192]{1,0:T(8,128)(2,1)S(1)} collective-permute-done((bf16[34,192]{1,0:T(8,128)(2,1)S(1)}, bf16[34,192]{1,0:T(8,128)(2,1)S(1)}, u32[]{:S(2)}, u32[]{:S(2)}) %collective-permute-start.3) | collective-permute-done | bytes 13088 | tf_op jit(solution)/shard_map/ppermute | solution.py:344
  33.7 34.5 %first.3 = bf16[2,32,48,128]{3,2,1,0:T(8,128)(2,1)S(1)} custom-call(bf16[32,192,128]{2,1,0:T(8,128)(2,1)S(1)} %copy-done, bf16[32,192,128]{2,1,0:T(8,128)(2,1)S(1)} %copy-done, bf16[32,192,128]{2,1,0:T(8,128)(2,1)S(1)} %copy-done, bf16[1,192,128]{2,1,0:T(8,128)(2,1)S(1)} %collective-permute-done.top, bf16[1,192,128]{2,1,0:T(8,128)(2,1)S(1)} %collective-permute-done.1.bottom, ...), custom_call_target="tpu_custom_call" | custom-call | flops 4096000000 | bytes 1638400 | tf_op jit(solution)/shard_map/first/pallas_call | solution.py:264
  68.2 0.9 copy.25
  69.2 8.1 %all-to-all-start.2 = ((bf16[2,32,48,128]{3,2,0,1:T(8,128)(2,1)}), bf16[2,32,48,128]{3,2,0,1:T(8,128)(2,1)}, u32[]{:S(2)}, u32[]{:S(2)}) async-start(bf16[2,32,48,128]{3,2,0,1:T(8,128)(2,1)} %copy.25), calls=%async_computation.2 | async-start | bytes 1572864 | tf_op jit(solution)/shard_map/all_to_all | solution.py:377
  77.3 1.7 fusion.3
  79.0 1.7 fusion.2
  80.7 34.5 %first.2 = bf16[2,32,48,128]{3,2,1,0:T(8,128)(2,1)S(1)} custom-call(bf16[32,192,128]{2,1,0:T(8,128)(2,1)S(1)} %copy-done, bf16[32,192,128]{2,1,0:T(8,128)(2,1)S(1)} %copy-done, bf16[32,192,128]{2,1,0:T(8,128)(2,1)S(1)} %copy-done, bf16[1,192,128]{2,1,0:T(8,128)(2,1)S(1)} %collective-permute-done.top, bf16[1,192,128]{2,1,0:T(8,128)(2,1)S(1)} %collective-permute-done.1.bottom, ...), custom_call_target="tpu_custom_call" | custom-call | flops 4096000000 | bytes 1638400 | tf_op jit(solution)/shard_map/first/pallas_call | solution.py:264
  115.2 1.0 copy.21
  116.2 9.8 %all-to-all-start = ((bf16[2,32,48,128]{3,2,0,1:T(8,128)(2,1)}), bf16[2,32,48,128]{3,2,0,1:T(8,128)(2,1)S(1)}, u32[]{:S(2)}, u32[]{:S(2)}) async-start(bf16[2,32,48,128]{3,2,0,1:T(8,128)(2,1)} %copy.21), calls=%async_computation | async-start | bytes 1572864 | tf_op jit(solution)/shard_map/all_to_all | solution.py:377
  127.4 1.5 broadcast_multiply_fusion
  129.0 0.8 mul.13.bias
  129.8 1.2 copy.26.inp
  131.0 19.6 %grid.3 = bf16[2,32,48,128]{3,2,1,0:T(8,128)(2,1)S(1)} custom-call(bf16[2,32,48,128]{3,2,1,0:T(8,128)(2,1)S(1)} %copy.26.inp, bf16[192,576]{1,0:T(8,128)(2,1)S(1)} %copy-done.8, bf16[192,192]{1,0:T(8,128)(2,1)S(1)} %copy-done.10, f32[64,384]{1,0:T(8,128)S(1)} %mul.13.bias), custom_call_target="tpu_custom_call" | custom-call | flops 1024000000 | bytes 1638400 | tf_op jit(solution)/shard_map/grid/pallas_call | solution.py:290
  150.6 0.9 copy.27
  151.5 9.8 %all-to-all-start.3 = ((bf16[2,32,48,128]{3,2,0,1:T(8,128)(2,1)}), bf16[2,32,48,128]{3,2,0,1:T(8,128)(2,1)S(1)}, u32[]{:S(2)}, u32[]{:S(2)}) async-start(bf16[2,32,48,128]{3,2,0,1:T(8,128)(2,1)} %copy.27), calls=%async_computation.3 | async-start | bytes 1572864 | tf_op jit(solution)/shard_map/all_to_all | solution.py:379
  161.4 19.6 %grid.2 = bf16[2,32,48,128]{3,2,1,0:T(8,128)(2,1)S(1)} custom-call(bf16[2,32,48,128]{3,2,1,0:T(8,128)(2,1)S(1)} %copy.22.inp, bf16[192,576]{1,0:T(8,128)(2,1)S(1)} %copy-done.8, bf16[192,192]{1,0:T(8,128)(2,1)S(1)} %copy-done.10, f32[64,384]{1,0:T(8,128)S(1)} %mul.13.bias), custom_call_target="tpu_custom_call" | custom-call | flops 1024000000 | bytes 1638400 | tf_op jit(solution)/shard_map/grid/pallas_call | solution.py:290
  181.0 0.9 copy.23
  182.0 9.9 %all-to-all-start.1 = ((bf16[2,32,48,128]{3,2,0,1:T(8,128)(2,1)}), bf16[2,32,48,128]{3,2,0,1:T(8,128)(2,1)S(1)}, u32[]{:S(2)}, u32[]{:S(2)}) async-start(bf16[2,32,48,128]{3,2,0,1:T(8,128)(2,1)} %copy.23), calls=%async_computation.1 | async-start | bytes 1572864 | tf_op jit(solution)/shard_map/all_to_all | solution.py:379
  192.0 6.3 %last.3 = bf16[16,192,128]{2,1,0:T(8,128)(2,1)S(1)} custom-call(bf16[2,32,48,128]{3,2,1,0:T(8,128)(2,1)S(1)} %copy.28.inp, bf16[192,768]{1,0:T(8,128)(2,1)S(1)} %copy-done.5, bf16[192,768]{1,0:T(8,128)(2,1)S(1)} %copy-done.6), custom_call_target="tpu_custom_call" | custom-call | flops 1228800000 | bytes 1638400 | tf_op jit(solution)/shard_map/last/pallas_call | solution.py:314
  198.3 10.6 %all-to-all-done.1 = bf16[2,32,48,128]{3,2,0,1:T(8,128)(2,1)S(1)} async-done(((bf16[2,32,48,128]{3,2,0,1:T(8,128)(2,1)}), bf16[2,32,48,128]{3,2,0,1:T(8,128)(2,1)S(1)}, u32[]{:S(2)}, u32[]{:S(2)}) %all-to-all-start.1) | async-done | bytes 786464 | tf_op jit(solution)/shard_map/all_to_all | solution.py:379
  208.9 6.3 %last.2 = bf16[16,192,128]{2,1,0:T(8,128)(2,1)S(1)} custom-call(bf16[2,32,48,128]{3,2,1,0:T(8,128)(2,1)S(1)} %copy.24.inp, bf16[192,768]{1,0:T(8,128)(2,1)S(1)} %copy-done.5, bf16[192,768]{1,0:T(8,128)(2,1)S(1)} %copy-done.6), custom_call_target="tpu_custom_call" | custom-call | flops 1228800000 | bytes 1638400 | tf_op jit(solution)/shard_map/last/pallas_call | solution.py:314
  215.2 1.3 pad_maximum_fusion
  (86 shorter events, 5.7 us)
Async XLA Ops:
  0.8 19.7 %collective-permute-start.1 = (bf16[1,192,128]{2,1,0:T(8,128)(2,1)S(1)}, bf16[1,192,128]{2,1,0:T(8,128)(2,1)S(1)}, u32[]{:S(2)}, u32[]{:S(2)}) collective-permute-start(bf16[1,192,128]{2,1,0:T(8,128)(2,1)S(1)} %get-tuple-element.11), channel_id=1, source_target_pairs={{4,0},{8,4},{12,8},{16,12},{20,16},{24,20},{28,24},{32,28},{36,32}... | collective-permute-start | bytes 147464 | tf_op jit(solution)/shard_map/ppermute | solution.py:344
  2.1 9.1 %copy-start.13 = (f32[6,15,15]{2,1,0:T(8,128)S(1)}, f32[6,15,15]{2,1,0:T(8,128)}, u32[]{:S(2)}) copy-start(f32[6,15,15]{2,1,0:T(8,128)} %param.20) | copy-start | bytes 16204
  2.1 9.7 %copy-start.14 = (f32[6,15,15]{2,1,0:T(8,128)S(1)}, f32[6,15,15]{2,1,0:T(8,128)}, u32[]{:S(2)}) copy-start(f32[6,15,15]{2,1,0:T(8,128)} %param.25) | copy-start | bytes 16204
  2.1 18.6 %collective-permute-start = (bf16[1,192,128]{2,1,0:T(8,128)(2,1)S(1)}, bf16[1,192,128]{2,1,0:T(8,128)(2,1)S(1)}, u32[]{:S(2)}, u32[]{:S(2)}) collective-permute-start(bf16[1,192,128]{2,1,0:T(8,128)(2,1)S(1)} %get-tuple-element.12), channel_id=1, source_target_pairs={{0,4},{4,8},{8,12},{12,16},{16,20},{20,24},{24,28},{28,32},{32,36}... | collective-permute-start | bytes 147464 | tf_op jit(solution)/shard_map/ppermute | solution.py:344
  12.4 2.6 %copy-start.11 = (f32[8,6,15,8]{3,2,1,0:T(8,128)}, f32[8,6,15,8]{3,2,1,0:T(8,128)S(1)}, u32[]{:S(2)}) copy-start(f32[8,6,15,8]{3,2,1,0:T(8,128)S(1)} %constant_dynamic-update-slice_fusion.8) | copy-start | bytes 69124
  14.8 0.9 copy-start.15
  16.5 17.1 %copy-start = (bf16[32,192,128]{2,1,0:T(8,128)(2,1)S(1)}, bf16[32,192,128]{2,1,0:T(8,128)(2,1)}, u32[]{:S(2)}) copy-start(bf16[32,192,128]{2,1,0:T(8,128)(2,1)} %after.3) | copy-start | bytes 4718596
  16.5 17.1 %copy-start.1 = (bf16[192,768]{1,0:T(8,128)(2,1)S(1)}, bf16[192,768]{1,0:T(8,128)(2,1)}, u32[]{:S(2)}) copy-start(bf16[192,768]{1,0:T(8,128)(2,1)} %w_expand.3) | copy-start | bytes 884740
  16.5 17.1 %copy-start.2 = (bf16[192,768]{1,0:T(8,128)(2,1)S(1)}, bf16[192,768]{1,0:T(8,128)(2,1)}, u32[]{:S(2)}) copy-start(bf16[192,768]{1,0:T(8,128)(2,1)} %w_project.3) | copy-start | bytes 884740
  16.5 17.1 %copy-start.3 = (bf16[192,768]{1,0:T(8,128)(2,1)S(1)}, bf16[192,768]{1,0:T(8,128)(2,1)}, u32[]{:S(2)}) copy-start(bf16[192,768]{1,0:T(8,128)(2,1)} %w_in.6) | copy-start | bytes 884740
  16.6 17.1 %copy-start.4 = (bf16[192,768]{1,0:T(8,128)(2,1)S(1)}, bf16[192,768]{1,0:T(8,128)(2,1)}, u32[]{:S(2)}) copy-start(bf16[192,768]{1,0:T(8,128)(2,1)} %w_back.6) | copy-start | bytes 884740
  16.6 17.1 %copy-start.7 = (bf16[192,576]{1,0:T(8,128)(2,1)S(1)}, bf16[192,576]{1,0:T(8,128)(2,1)}, u32[]{:S(2)}) copy-start(bf16[192,576]{1,0:T(8,128)(2,1)} %w_qkv.6) | copy-start | bytes 663556
  16.6 17.1 %copy-start.9 = (bf16[192,192]{1,0:T(8,128)(2,1)S(1)}, bf16[192,192]{1,0:T(8,128)(2,1)}, u32[]{:S(2)}) copy-start(bf16[192,192]{1,0:T(8,128)(2,1)} %w_out.6) | copy-start | bytes 221188
  21.0 8.0 %collective-permute-start.2 = (bf16[34,192]{1,0:T(8,128)(2,1)S(1)}, bf16[34,192]{1,0:T(8,128)(2,1)S(1)}, u32[]{:S(2)}, u32[]{:S(2)}) collective-permute-start(bf16[34,192]{1,0:T(8,128)(2,1)S(1)} %pad_maximum_fusion.1), channel_id=1, source_target_pairs={{0,1},{1,2},{2,3},{4,5},{5,6},{6,7},{8,9},{9,10},{10,11},{12,13},{... | collective-permute-start | bytes 39176 | tf_op jit(solution)/shard_map/ppermute | solution.py:344
  27.0 6.6 %collective-permute-start.3 = (bf16[34,192]{1,0:T(8,128)(2,1)S(1)}, bf16[34,192]{1,0:T(8,128)(2,1)S(1)}, u32[]{:S(2)}, u32[]{:S(2)}) collective-permute-start(bf16[34,192]{1,0:T(8,128)(2,1)S(1)} %pad_maximum_fusion.2), channel_id=1, source_target_pairs={{1,0},{2,1},{3,2},{5,4},{6,5},{7,6},{9,8},{10,9},{11,10},{13,12},{... | collective-permute-start | bytes 39176 | tf_op jit(solution)/shard_map/ppermute | solution.py:344
  69.2 47.0 %all-to-all-start.2 = ((bf16[2,32,48,128]{3,2,0,1:T(8,128)(2,1)}), bf16[2,32,48,128]{3,2,0,1:T(8,128)(2,1)}, u32[]{:S(2)}, u32[]{:S(2)}) async-start(bf16[2,32,48,128]{3,2,0,1:T(8,128)(2,1)} %copy.25), calls=%async_computation.2 | async-start | bytes 1572864 | tf_op jit(solution)/shard_map/all_to_all | solution.py:377
  115.2 10.8 %copy-start.12 = (f32[8,6,15,8]{3,2,1,0:T(8,128)S(1)}, f32[8,6,15,8]{3,2,1,0:T(8,128)}, u32[]{:S(2)}) copy-start(f32[8,6,15,8]{3,2,1,0:T(8,128)} %copy-done.11) | copy-start | bytes 69124
  116.2 35.3 %all-to-all-start = ((bf16[2,32,48,128]{3,2,0,1:T(8,128)(2,1)}), bf16[2,32,48,128]{3,2,0,1:T(8,128)(2,1)S(1)}, u32[]{:S(2)}, u32[]{:S(2)}) async-start(bf16[2,32,48,128]{3,2,0,1:T(8,128)(2,1)} %copy.21), calls=%async_computation | async-start | bytes 1572864 | tf_op jit(solution)/shard_map/all_to_all | solution.py:377
  129.0 2.0 copy-start.8
  129.0 2.0 copy-start.10
  151.5 30.4 %all-to-all-start.3 = ((bf16[2,32,48,128]{3,2,0,1:T(8,128)(2,1)}), bf16[2,32,48,128]{3,2,0,1:T(8,128)(2,1)S(1)}, u32[]{:S(2)}, u32[]{:S(2)}) async-start(bf16[2,32,48,128]{3,2,0,1:T(8,128)(2,1)} %copy.27), calls=%async_computation.3 | async-start | bytes 1572864 | tf_op jit(solution)/shard_map/all_to_all | solution.py:379
  181.9 10.0 %copy-start.5 = (bf16[192,768]{1,0:T(8,128)(2,1)S(1)}, bf16[192,768]{1,0:T(8,128)(2,1)}, u32[]{:S(2)}) copy-start(bf16[192,768]{1,0:T(8,128)(2,1)} %w_in.7) | copy-start | bytes 884740
  181.9 10.0 %copy-start.6 = (bf16[192,768]{1,0:T(8,128)(2,1)S(1)}, bf16[192,768]{1,0:T(8,128)(2,1)}, u32[]{:S(2)}) copy-start(bf16[192,768]{1,0:T(8,128)(2,1)} %w_back.7) | copy-start | bytes 884740
  182.0 26.9 %all-to-all-start.1 = ((bf16[2,32,48,128]{3,2,0,1:T(8,128)(2,1)}), bf16[2,32,48,128]{3,2,0,1:T(8,128)(2,1)S(1)}, u32[]{:S(2)}, u32[]{:S(2)}) async-start(bf16[2,32,48,128]{3,2,0,1:T(8,128)(2,1)} %copy.23), calls=%async_computation.1 | async-start | bytes 1572864 | tf_op jit(solution)/shard_map/all_to_all | solution.py:379

commit v2 on v1

v2 whole, which is shorter than its diff:
```python
import functools
import math

import jax
import jax.numpy as jnp
from jax import lax
from jax.experimental import pallas as pl
from jax.experimental.pallas import tpu as pltpu
from jax.sharding import Mesh, PartitionSpec as P

WIN = 8
D = 192
HID = 768
HEADS = 6
SIZE = 32
COLS = 128
TOKENS = 64
CHUNK = 1024
ROWS_CHUNK = 8
TILES = 16
LAG = 3
CALLS = (2, 2)
LOG2E = 1.4426950408889634
F32 = jnp.float32
BF16 = jnp.bfloat16
NN = (((1,), (0,)), ((), ()))
NT = (((1,), (1,)), ((), ()))
TN = (((0,), (0,)), ((), ()))
C0 = math.sqrt(2.0 / math.pi)
C1 = 0.044715 * C0


def dot(a, b, dims=NN):
    return lax.dot_general(a, b, dims, preferred_element_type=F32)


def gelu(x):
    x = x.astype(BF16)
    inner = x * (BF16(C0) + BF16(C1) * (x * x))
    half = BF16(0.5) * x
    return half + half * jnp.tanh(inner)


def norm(s):
    centre = s - jnp.mean(s, axis=0, keepdims=True)
    spread = jnp.mean(centre * centre, axis=0, keepdims=True)
    return (centre * lax.rsqrt(spread + 1e-05)).astype(BF16)


def mlp(s, w_in_t, w_out):
    return s + dot(w_out, gelu(dot(w_in_t, norm(s))))


def softmax_keys(scores):
    top = jnp.max(scores, axis=0, keepdims=True)
    weights = jnp.exp2(scores - top)
    total = jnp.sum(weights, axis=0, keepdims=True)
    return (weights * (1.0 / total)).astype(BF16)


def attend(s, wq_t, wk, wv_t, w_out_t, bias):
    n = norm(s)
    q = dot(wq_t, n) * (SIZE**-0.5 * LOG2E)
    v = dot(wv_t, n).astype(BF16)
    k = dot(n, wk, TN).astype(BF16)
    left = lax.broadcasted_iota(jnp.int32, (1, 128), 1) < TOKENS
    keep = (lax.broadcasted_iota(jnp.int32, (TOKENS, 1), 0) < SIZE) == left
    zero = jnp.zeros((TOKENS, 128), BF16)
    tiles = s.shape[1] // 128
    ready = {}
    mixed = []

    def score(t):
        here = q[:, 128 * t : 128 * t + 128]
        swapped = pltpu.roll(here, TOKENS, 1).astype(BF16)
        here = here.astype(BF16)
        got = []
        for g in range(2):
            both = jnp.where(left, here, swapped) if g == 0 else jnp.where(left, swapped, here)
            keys = k[(2 * t + g) * TOKENS : (2 * t + g + 1) * TOKENS]
            b = [jnp.where(keep, both[64 * p : 64 * p + 64], zero) for p in range(3)]
            four = jnp.concatenate(
                [jnp.concatenate([b[0], zero], axis=1), jnp.concatenate([zero, b[1]], axis=1)],
                axis=0,
            )
            first = softmax_keys(dot(keys[:, :128], four) + bias[:, :256])
            last = softmax_keys(dot(keys[:, 128:], b[2]) + bias[:, 256:])
            got.append((first[:, :128], first[:, 128:], last))
        ready[t] = got

    def mix(t):
        got = ready.pop(t)
        values = v[:, 128 * t : 128 * t + 128]
        rows = []
        for p in range(3):
            pair = jnp.concatenate(
                [
                    jnp.concatenate([got[0][p], zero], axis=1),
                    jnp.concatenate([zero, got[1][p]], axis=1),
                ],
                axis=0,
            )
            out = dot(values[64 * p : 64 * p + 64], pair)
            a, b = out[:, :128], out[:, 128:]
            rows.append(jnp.where(left, a[:SIZE], pltpu.roll(b[:SIZE], TOKENS, 1)))
            rows.append(jnp.where(left, pltpu.roll(a[SIZE:], TOKENS, 1), b[SIZE:]))
        mixed.append(jnp.concatenate(rows, axis=0).astype(BF16))

    for t in range(tiles + LAG):
        if t < tiles:
            score(t)
        if t >= LAG:
            mix(t - LAG)
    return s + dot(w_out_t, jnp.concatenate(mixed, axis=1))


def prepare(w_qkv, w_out, table, wq_t, wk, wv_t, w_out_t, bias):
    wq_t[...] = w_qkv[:, 0:D].T
    wk[...] = w_qkv[:, D : 2 * D]
    wv_t[...] = w_qkv[:, 2 * D : 3 * D].T
    w_out_t[...] = w_out[...].T
    left = lax.broadcasted_iota(jnp.int32, (WIN, 128), 1) < TOKENS
    for u in range(WIN):
        for p in range(3):
            start = (7 - u) * WIN
            even = pltpu.roll(table[2 * p], (128 - start) % 128, 1)
            odd = pltpu.roll(table[2 * p + 1], (64 - start) % 128, 1)
            bias[u * WIN : (u + 1) * WIN, 128 * p : 128 * p + 128] = (
                jnp.where(left, even, odd) * LOG2E
            )


def gather_groups(lo, hi):
    parts = []
    for g in range(TILES):
        at = pl.ds(g, TOKENS, stride=TILES)
        parts.append(jnp.concatenate([lo[at, :], hi[at, :][:, :64]], axis=1))
    return jnp.concatenate(parts, axis=0).T


def first_kernel(
    first, last,
    image, before, after, top, bottom, left, right,
    w_expand, dw, w_project, w_qkv, w_out, table, w_in, w_back,
    out, expanded, mobile, tokens, lo, hi, place, wq_t, wk, wv_t, w_out_t, w_in_t, bias,
):
    step = pl.program_id(0)
    steps = pl.num_programs(0)
    start = pl.multiple_of(step * ROWS_CHUNK, 8)
    line = lax.broadcasted_iota(jnp.int32, (16, HID), 0)

    def laid(x):
        return dot(place[...], x, NT).astype(BF16)

    def expand(x, sides, rows):
        cells = gelu(dot(x, w_expand[...])).astype(F32)
        for i, r in enumerate(rows):
            e = cells[COLS * i : COLS * (i + 1)]
            expanded[r, 16:144, :] = e
            prev = pltpu.roll(e[112:128], 1, 0)
            expanded[r, 0:16, :] = jnp.where(line == 0, sides[0][r : r + 1], prev)
            follow = pltpu.roll(e[0:16], 15, 0)
            expanded[r, 144:160, :] = jnp.where(line == 15, sides[1][r : r + 1], follow)

    sides = [
        gelu(dot(halo[pl.ds(start, 16), :].astype(BF16), w_expand[...])).astype(F32)
        for halo in (left, right)
    ]

    @pl.when(step == 0)
    def _():
        prepare(w_qkv, w_out, table, wq_t, wk, wv_t, w_out_t, bias)
        w_in_t[...] = w_in[...].T
        row = lax.broadcasted_iota(jnp.int32, (COLS, COLS), 0)
        col = lax.broadcasted_iota(jnp.int32, (COLS, COLS), 1)
        place[...] = jnp.where(col == (row % 16) * 8 + row // 16, 1.0, 0.0).astype(BF16)
        above = top[0] if first else before[0]
        pair = jnp.concatenate([laid(above), laid(image[0])], axis=0)
        tokens[0:COLS, :] = pair[COLS:]
        expand(pair, sides, (0, 1))

    @pl.when(step > 0)
    def _():
        tokens[0:COLS, :] = tokens[8 * COLS : 9 * COLS, :]
        expanded[0:2] = expanded[8:10]

    below = after[0]
    if last:
        below = jnp.where(step == steps - 1, bottom[0], below)
    for r in range(1, ROWS_CHUNK):
        tokens[COLS * r : COLS * (r + 1), :] = laid(image[r])
    tokens[COLS * 8 : COLS * 9, :] = laid(below)
    for half in range(2):
        x = tokens[COLS * (1 + 4 * half) : COLS * (5 + 4 * half), :]
        expand(x, sides, range(2 + 4 * half, 6 + 4 * half))

    for r in range(ROWS_CHUNK):
        for block in range(HID // 128):
            lanes = slice(block * 128, (block + 1) * 128)
            conv = None
            for i in range(3):
                for k in range(3):
                    term = expanded[r + i, 16 * k : 16 * k + COLS, lanes] * dw[
                        3 * i + k : 3 * i + k + 1, lanes
                    ]
                    conv = term if conv is None else conv + term
            mobile[COLS * r : COLS * (r + 1), lanes] = gelu(conv)

    s = tokens[0:CHUNK, :].astype(F32) + dot(mobile[...], w_project[...], NT)
    lo[...] = s[:, :128]
    hi[:, :64] = s[:, 128:]
    s = gather_groups(lo, hi)
    s = attend(s, wq_t[...], wk[...], wv_t[...], w_out_t[...], bias)
    s = mlp(s, w_in_t[...], w_back[...]).T.reshape(TILES, WIN, WIN, D)
    for r in range(ROWS_CHUNK):
        rows = s[:, r].reshape(2, 4, 16, D)
        at = slice(4 * r, 4 * r + 4)
        out[at, 0, 0:16, :] = rows[0, :, :, 0:128].astype(BF16)
        out[at, 0, 16:32, :] = rows[1, :, :, 0:128].astype(BF16)
        out[at, 0, 32:48, :] = jnp.concatenate(
            [rows[0, :, :, 128:], rows[1, :, :, 128:]], axis=-1
        ).astype(BF16)


def grid_kernel(
    inp, w_qkv, w_out, table, out, lo, hi, wq_t, wk, wv_t, w_out_t, bias
):
    @pl.when(pl.program_id(0) == 0)
    def _():
        prepare(w_qkv, w_out, table, wq_t, wk, wv_t, w_out_t, bias)

    for src in range(32):
        lo[32 * src : 32 * src + 32, :] = inp[src, 0, 0:32, :].astype(F32)
        both = inp[src, 0, 32:48, :].astype(F32)
        hi[32 * src : 32 * src + 16, :] = both
        hi[32 * src + 16 : 32 * src + 32, :] = pltpu.roll(both, 64, 1)
    s = gather_groups(lo, hi)
    s = attend(s, wq_t[...], wk[...], wv_t[...], w_out_t[...], bias).T
    for g in range(TILES):
        at = pl.ds(g, TOKENS, stride=TILES)
        rows = s[g * TOKENS : (g + 1) * TOKENS]
        lo[at, :] = rows[:, :128]
        hi[at, :] = jnp.concatenate([rows[:, 128:], rows[:, 128:]], axis=1)
    left = lax.broadcasted_iota(jnp.int32, (16, 128), 1) < 64
    for src in range(32):
        out[src, 0, 0:32, :] = lo[32 * src : 32 * src + 32, :].astype(BF16)
        out[src, 0, 32:48, :] = jnp.where(
            left, hi[32 * src : 32 * src + 16, :], hi[32 * src + 16 : 32 * src + 32, :]
        ).astype(BF16)


def last_kernel(inp, w_in, w_back, *rest):
    out, w_in_t = rest[-2:]

    @pl.when(pl.program_id(0) == 0)
    def _():
        w_in_t[...] = w_in[...].T

    rows = []
    for r in range(ROWS_CHUNK):
        got = inp[4 * r : 4 * r + 4, 0].astype(F32)
        both = got[:, 32:48].reshape(64, 128)
        for i in range(2):
            low = got[:, 16 * i : 16 * i + 16].reshape(64, 128)
            rows.append(jnp.concatenate([low, both[:, 64 * i : 64 * i + 64]], axis=1))
    s = jnp.concatenate(rows, axis=0).T
    s = mlp(s, w_in_t[...], w_back[...]).astype(BF16)
    for r in range(ROWS_CHUNK):
        out[r] = s[:, COLS * r : COLS * (r + 1)]


def whole(shape):
    return pl.BlockSpec(shape, lambda k: (0,) * len(shape))


def vm(limit):
    return pltpu.CompilerParams(vmem_limit_bytes=limit << 20, dimension_semantics=("arbitrary",))


BLOCK = pl.BlockSpec((32, 1, 48, 128), lambda k: (0, k, 0, 0))
ATTEND_SCRATCH = [
    pltpu.VMEM((D, D), BF16),
    pltpu.VMEM((D, D), BF16),
    pltpu.VMEM((D, D), BF16),
    pltpu.VMEM((D, D), BF16),
]


def call_first(base, chunks, image, top, bottom, left, right, weights):
    total = image.shape[0]
    first, last = base == 0, (base + chunks) * ROWS_CHUNK == total
    rows = pl.BlockSpec((ROWS_CHUNK, D, COLS), lambda k: (base + k, 0, 0))
    before = pl.BlockSpec((1, D, COLS), lambda k: (max(base * ROWS_CHUNK - 1, 0), 0, 0))
    after = pl.BlockSpec(
        (1, D, COLS), lambda k: (jnp.minimum((base + k + 1) * ROWS_CHUNK, total - 1), 0, 0)
    )
    at = slice(base * ROWS_CHUNK, (base + chunks) * ROWS_CHUNK + 8)
    small = [top, bottom, left[at], right[at]] + weights
    tokens = chunks * CHUNK
    return pl.pallas_call(
        functools.partial(first_kernel, first, last),
        grid=(chunks,),
        in_specs=[rows, before, after] + [whole(a.shape) for a in small],
        out_specs=BLOCK,
        out_shape=jax.ShapeDtypeStruct((32, chunks, 48, 128), BF16),
        scratch_shapes=[
            pltpu.VMEM((ROWS_CHUNK + 2, 160, HID), F32),
            pltpu.VMEM((CHUNK, HID), BF16),
            pltpu.VMEM((9 * COLS, D), BF16),
            pltpu.VMEM((CHUNK, 128), F32),
            pltpu.VMEM((CHUNK, 128), F32),
            pltpu.VMEM((COLS, COLS), BF16),
        ]
        + ATTEND_SCRATCH
        + [pltpu.VMEM((HID, D), BF16), pltpu.VMEM((TOKENS, HEADS * TOKENS), F32)],
        compiler_params=vm(48),
        cost_estimate=pl.CostEstimate(
            flops=tokens * 2000000, bytes_accessed=tokens * 800, transcendentals=tokens * 2700
        ),
        name="first",
    )(image, image, image, *small)


def call_grid(arrived, weights):
    chunks = arrived.shape[1]
    tokens = chunks * CHUNK
    return pl.pallas_call(
        grid_kernel,
        grid=(chunks,),
        in_specs=[BLOCK] + [whole(a.shape) for a in weights],
        out_specs=BLOCK,
        out_shape=jax.ShapeDtypeStruct(arrived.shape, BF16),
        scratch_shapes=[pltpu.VMEM((CHUNK, 128), F32), pltpu.VMEM((CHUNK, 128), F32)]
        + ATTEND_SCRATCH
        + [pltpu.VMEM((TOKENS, HEADS * TOKENS), F32)],
        compiler_params=vm(32),
        cost_estimate=pl.CostEstimate(
            flops=tokens * 1000000, bytes_accessed=tokens * 800, transcendentals=tokens * 400
        ),
        name="grid",
    )(arrived, *weights)


def call_last(base, rows, returned, w_in, w_back, earlier):
    chunks = returned.shape[1]
    tokens = chunks * CHUNK
    operands = [returned, w_in, w_back]
    specs = [BLOCK, whole(w_in.shape), whole(w_back.shape)]
    aliases = {}
    if earlier is not None:
        operands.append(earlier)
        specs.append(pl.BlockSpec(memory_space=pl.ANY))
        aliases = {3: 0}
    return pl.pallas_call(
        last_kernel,
        grid=(chunks,),
        in_specs=specs,
        out_specs=pl.BlockSpec((ROWS_CHUNK, D, COLS), lambda k: (base + k, 0, 0)),
        out_shape=jax.ShapeDtypeStruct((rows, D, COLS), BF16),
        scratch_shapes=[pltpu.VMEM((HID, D), BF16)],
        input_output_aliases=aliases,
        compiler_params=vm(32),
        cost_estimate=pl.CostEstimate(
            flops=tokens * 1000000, bytes_accessed=tokens * 800, transcendentals=tokens * 800
        ),
        name="last",
    )(*operands)


def bias_tables(tables):
    cols = jnp.stack([tables[:, :, 7 - v : 15 - v] for v in range(WIN)], axis=1)
    return jnp.pad(cols.reshape(2 * HEADS, WIN, 15 * WIN), ((0, 0), (0, 0), (0, 8)))


def shift(x, axis, count, step):
    if step > 0:
        pairs = [(i, i + 1) for i in range(count - 1)]
    else:
        pairs = [(i + 1, i) for i in range(count - 1)]
    return lax.ppermute(x, axis, pairs)


ROW_AXES = ("y", "zh", "zl", "xl")
COL_AXES = ("xh", "core")
GROUP = ("y", "zh", "xh", "core")


def body(
    image, w_expand, dw_kernel, w_project, block_qkv, block_out, block_bias, mlp_in, mlp_out,
    grid_qkv, grid_out, grid_bias, mlp2_in, mlp2_out,
):
    rows = image.shape[0]
    top = shift(image[rows - 1 :], ROW_AXES, 32, 1)
    bottom = shift(image[:1], ROW_AXES, 32, -1)
    ends = [
        jnp.concatenate([top[:, :, c], image[:, :, c], bottom[:, :, c]], axis=0)
        for c in (0, COLS - 1)
    ]
    left = shift(ends[1], COL_AXES, 4, 1)
    right = shift(ends[0], COL_AXES, 4, -1)
    left = jnp.pad(left.astype(F32), ((0, 6), (0, 0)))
    right = jnp.pad(right.astype(F32), ((0, 6), (0, 0)))
    tables = bias_tables(jnp.concatenate([block_bias, grid_bias], axis=0))
    weights = [
        w_expand, dw_kernel.reshape(9, HID).astype(F32), w_project, block_qkv, block_out,
        tables[:HEADS], mlp_in, mlp_out,
    ]
    base = 0
    result = None
    for chunks in CALLS:
        sent = call_first(base, chunks, image, top, bottom, left, right, weights)
        arrived = lax.all_to_all(sent, GROUP, 0, 0, tiled=True)
        mixed = call_grid(arrived, [grid_qkv, grid_out, tables[HEADS:]])
        back = lax.all_to_all(mixed, GROUP, 0, 0, tiled=True)
        result = call_last(base, rows, back, mlp2_in, mlp2_out, result)
        base += chunks
    return result


def solution(mesh):
    names = ("y", "zh", "zl", "xl", "xh", "core")
    fine = Mesh(mesh.devices.reshape(4, 2, 2, 2, 2, 2), names)
    spec = P(ROW_AXES, None, COL_AXES)
    return jax.shard_map(
        body, mesh=fine, in_specs=(spec,) + (P(),) * 13, out_specs=spec, check_vma=False
    )
```

time: 218 us -> 146 us (0.67)
  Pallas kernels: 121 us -> 51.5 us
  waiting for transfers between devices: 15.2 us -> 39.7 us
  local copies, waits for them, and re-layouts: 25.3 us -> 12.7 us
  starting transfers between devices: 51.6 us -> 39.5 us
    pallas_call x6, Pallas kernels: 121 us -> 51.5 us  [the longest x2 32.9 us: call_first(): pl.pallas_call(functools.partial(first_kernel, first, last), grid=(chunks...]
    all_to_all x4, waiting for transfers between devices: 10.6 us -> 35.1 us  [the longest x2 24 us: body(): back = lax.all_to_all(mixed, GROUP, 0, 0, tiled=True)]
    all_to_all x4, starting transfers between devices: 37.7 us -> 25.6 us  [the longest x2 18 us: body(): arrived = lax.all_to_all(sent, GROUP, 0, 0, tiled=True)]
    unnamed x62 -> x39, local copies, waits for them, and re-layouts: 12.3 us -> 5.92 us
    pallas_call x4 -> x0, local copies, waits for them, and re-layouts: 3.79 us -> none  [the longest x2 1.91 us: call_first(): pl.pallas_call(functools.partial(first_kernel, first, last), grid=(steps,...]
  transfers between devices with their start and end apart: 8 -> 8, of which waited for: 2 -> 4; matrix products, arithmetic and copies ran while one was open for 12% -> 8% of each run, Pallas kernels for 37% -> 22%
where the time goes in v2:
time: 146 us; the launch traced here: 145 us
  Pallas kernels  51.5 us (35%)
  waiting for transfers between devices  39.7 us (27%)
  starting transfers between devices  39.5 us (27%)
  local copies, waits for them, and re-layouts  12.7 us (9%)
  other arithmetic  1.49 us (1%)
    pallas_call x2, Pallas kernels, call_first(): pl.pallas_call(functools.partial(first_kernel, first, last), grid=(chunks...  32.9 us
    all_to_all x2, waiting for transfers between devices, body(): back = lax.all_to_all(mixed, GROUP, 0, 0, tiled=True)  24 us
    all_to_all x2, starting transfers between devices, body(): arrived = lax.all_to_all(sent, GROUP, 0, 0, tiled=True)  18 us
    ppermute x4, starting transfers between devices, shift(): return lax.ppermute(x, axis, pairs)  13.9 us
    pallas_call x2, Pallas kernels, call_grid(): pl.pallas_call(grid_kernel, grid=(chunks,), in_specs=[BLOCK] + [whole(a.s...  11.8 us
    all_to_all x2, waiting for transfers between devices, body(): arrived = lax.all_to_all(sent, GROUP, 0, 0, tiled=True)  11 us
    all_to_all x2, starting transfers between devices, body(): back = lax.all_to_all(mixed, GROUP, 0, 0, tiled=True)  7.62 us
    pallas_call x2, Pallas kernels, call_last(): pl.pallas_call(last_kernel, grid=(chunks,), in_specs=specs, out_specs=pl....  6.8 us
  transfers between devices with their start and end apart: 8, of which 4 were waited for; matrix products, arithmetic and copies ran while one was open for 8% of the time, Pallas kernels for 22%

profile of v2, /device:TPU:1, one launch (start us, length us, event | category | flops | bytes accessed | tf_op | source)
XLA Modules:
  0.0 145.3 jit_solution(6206341543355199824)
XLA Ops:
  0.0 0.8 fusion.1
  0.8 1.3 collective-permute-start.1
  2.1 4.7 %collective-permute-start = (bf16[1,192,128]{2,1,0:T(8,128)(2,1)S(1)}, bf16[1,192,128]{2,1,0:T(8,128)(2,1)S(1)}, u32[]{:S(2)}, u32[]{:S(2)}) collective-permute-start(bf16[1,192,128]{2,1,0:T(8,128)(2,1)S(1)} %get-tuple-element.12), channel_id=1, source_target_pairs={{0,4},{4,8},{8,12},{12,16},{16,20},{20,24},{24,28},{28,32},{32,36}... | collective-permute-start | bytes 147464 | tf_op jit(solution)/shard_map/ppermute | solution.py:380
  6.9 4.3 %fusion = (bf16[32,192,1]{2,1,0:T(8,128)(2,1)}, bf16[32,192,1]{2,1,0:T(8,128)(2,1)}) fusion(bf16[32,192,128]{2,1,0:T(8,128)(2,1)} %after.3), kind=kLoop, calls=%fused_computation.12 | loop fusion | bytes 49152 | tf_op jit(solution)/shard_map/slice | solution.py:396
  11.2 0.2 fusion.2
  11.5 0.1 stack.43
  11.6 0.1 stack.42
  11.7 0.1 stack.41
  12.5 2.0 %copy.29 = bf16[32,192,1]{1,0,2:T(8,128)(2,1)S(1)} copy(bf16[32,192,1]{2,1,0:T(8,128)(2,1)} %get-tuple-element.9) | data formatting | bytes 24576
  14.5 1.9 %copy.28 = bf16[32,192,1]{1,0,2:T(8,128)(2,1)S(1)} copy(bf16[32,192,1]{2,1,0:T(8,128)(2,1)} %get-tuple-element.10) | data formatting | bytes 24576
  16.5 0.2 slice_reduce_fusion
  16.7 0.2 slice_reduce_fusion.1
  16.9 6.0 %collective-permute-start.2 = (bf16[34,192]{1,0:T(8,128)(2,1)S(1)}, bf16[34,192]{1,0:T(8,128)(2,1)S(1)}, u32[]{:S(2)}, u32[]{:S(2)}) collective-permute-start(bf16[34,192]{1,0:T(8,128)(2,1)S(1)} %pad_maximum_fusion), channel_id=1, source_target_pairs={{0,1},{1,2},{2,3},{4,5},{5,6},{6,7},{8,9},{9,10},{10,11},{12,13},{... | collective-permute-start | bytes 39176 | tf_op jit(solution)/shard_map/ppermute | solution.py:380
  23.0 1.9 %collective-permute-start.3 = (bf16[34,192]{1,0:T(8,128)(2,1)S(1)}, bf16[34,192]{1,0:T(8,128)(2,1)S(1)}, u32[]{:S(2)}, u32[]{:S(2)}) collective-permute-start(bf16[34,192]{1,0:T(8,128)(2,1)S(1)} %pad_maximum_fusion.1), channel_id=1, source_target_pairs={{1,0},{2,1},{3,2},{5,4},{6,5},{7,6},{9,8},{10,9},{11,10},{13,12},{... | collective-permute-start | bytes 39176 | tf_op jit(solution)/shard_map/ppermute | solution.py:380
  25.0 4.6 %collective-permute-done.3 = bf16[34,192]{1,0:T(8,128)(2,1)S(1)} collective-permute-done((bf16[34,192]{1,0:T(8,128)(2,1)S(1)}, bf16[34,192]{1,0:T(8,128)(2,1)S(1)}, u32[]{:S(2)}, u32[]{:S(2)}) %collective-permute-start.3) | collective-permute-done | bytes 13088 | tf_op jit(solution)/shard_map/ppermute | solution.py:380
  29.7 16.4 %first.3 = bf16[32,2,48,128]{3,2,1,0:T(8,128)(2,1)} custom-call(bf16[32,192,128]{2,1,0:T(8,128)(2,1)S(1)} %copy-done, bf16[32,192,128]{2,1,0:T(8,128)(2,1)S(1)} %copy-done, bf16[32,192,128]{2,1,0:T(8,128)(2,1)S(1)} %copy-done, bf16[1,192,128]{2,1,0:T(8,128)(2,1)S(1)} %collective-permute-done.top, bf16[1,192,128]{2,1,0:T(8,128)(2,1)S(1)} %collective-permute-done.1.bottom, ...), custom_call_target="tpu_custom_call" | custom-call | flops 4096000000 | bytes 1638400 | tf_op jit(solution)/shard_map/first/pallas_call | solution.py:300
  46.1 8.1 %all-to-all-start.2 = ((bf16[32,2,48,128]{3,2,1,0:T(8,128)(2,1)}), bf16[32,2,48,128]{3,2,1,0:T(8,128)(2,1)S(1)}, u32[]{:S(2)}, u32[]{:S(2)}) async-start(bf16[32,2,48,128]{3,2,1,0:T(8,128)(2,1)} %first.3), calls=%async_computation.2 | async-start | bytes 1572864 | tf_op jit(solution)/shard_map/all_to_all | solution.py:412
  54.2 0.7 convert_element_type.16
  54.9 0.7 convert_element_type.17
  55.7 1.0 copy-done.5
  56.6 0.9 copy-done.9
  57.6 16.5 %first.2 = bf16[32,2,48,128]{3,2,1,0:T(8,128)(2,1)} custom-call(bf16[32,192,128]{2,1,0:T(8,128)(2,1)S(1)} %copy-done, bf16[32,192,128]{2,1,0:T(8,128)(2,1)S(1)} %copy-done, bf16[32,192,128]{2,1,0:T(8,128)(2,1)S(1)} %copy-done, bf16[1,192,128]{2,1,0:T(8,128)(2,1)S(1)} %collective-permute-done.top, bf16[1,192,128]{2,1,0:T(8,128)(2,1)S(1)} %collective-permute-done.1.bottom, ...), custom_call_target="tpu_custom_call" | custom-call | flops 4096000000 | bytes 1638400 | tf_op jit(solution)/shard_map/first/pallas_call | solution.py:300
  74.0 9.9 %all-to-all-start = ((bf16[32,2,48,128]{3,2,1,0:T(8,128)(2,1)}), bf16[32,2,48,128]{3,2,1,0:T(8,128)(2,1)S(1)}, u32[]{:S(2)}, u32[]{:S(2)}) async-start(bf16[32,2,48,128]{3,2,1,0:T(8,128)(2,1)} %first.2), calls=%async_computation | async-start | bytes 1572864 | tf_op jit(solution)/shard_map/all_to_all | solution.py:412
  84.0 5.9 %grid.3 = bf16[32,2,48,128]{3,2,1,0:T(8,128)(2,1)} custom-call(bf16[32,2,48,128]{3,2,1,0:T(8,128)(2,1)S(1)} %all-to-all-done.2.inp, bf16[192,576]{1,0:T(8,128)(2,1)S(1)} %copy-done.10, bf16[192,192]{1,0:T(8,128)(2,1)S(1)} %copy-done.12, f32[6,8,128]{2,1,0:T(8,128)S(1)} %get-tuple-element.21.table), custom_call_target="tpu_custom_call" | custom-call | flops 2048000000 | bytes 1638400 | tf_op jit(solution)/shard_map/grid/pallas_call | solution.py:327
  89.9 11.0 %all-to-all-done.inp = bf16[32,2,48,128]{3,2,1,0:T(8,128)(2,1)S(1)} async-done(((bf16[32,2,48,128]{3,2,1,0:T(8,128)(2,1)}), bf16[32,2,48,128]{3,2,1,0:T(8,128)(2,1)S(1)}, u32[]{:S(2)}, u32[]{:S(2)}) %all-to-all-start) | async-done | bytes 786464 | tf_op jit(solution)/shard_map/all_to_all | solution.py:412
  100.9 3.9 %all-to-all-start.3 = ((bf16[32,2,48,128]{3,2,1,0:T(8,128)(2,1)}), bf16[32,2,48,128]{3,2,1,0:T(8,128)(2,1)S(1)}, u32[]{:S(2)}, u32[]{:S(2)}) async-start(bf16[32,2,48,128]{3,2,1,0:T(8,128)(2,1)} %grid.3), calls=%async_computation.3 | async-start | bytes 1572864 | tf_op jit(solution)/shard_map/all_to_all | solution.py:414
  104.9 5.9 %grid.2 = bf16[32,2,48,128]{3,2,1,0:T(8,128)(2,1)} custom-call(bf16[32,2,48,128]{3,2,1,0:T(8,128)(2,1)S(1)} %all-to-all-done.inp, bf16[192,576]{1,0:T(8,128)(2,1)S(1)} %copy-done.10, bf16[192,192]{1,0:T(8,128)(2,1)S(1)} %copy-done.12, f32[6,8,128]{2,1,0:T(8,128)S(1)} %get-tuple-element.21.table), custom_call_target="tpu_custom_call" | custom-call | flops 2048000000 | bytes 1638400 | tf_op jit(solution)/shard_map/grid/pallas_call | solution.py:327
  110.7 10.7 %all-to-all-done.3.inp = bf16[32,2,48,128]{3,2,1,0:T(8,128)(2,1)S(1)} async-done(((bf16[32,2,48,128]{3,2,1,0:T(8,128)(2,1)}), bf16[32,2,48,128]{3,2,1,0:T(8,128)(2,1)S(1)}, u32[]{:S(2)}, u32[]{:S(2)}) %all-to-all-start.3) | async-done | bytes 786464 | tf_op jit(solution)/shard_map/all_to_all | solution.py:414
  121.4 3.7 %all-to-all-start.1 = ((bf16[32,2,48,128]{3,2,1,0:T(8,128)(2,1)}), bf16[32,2,48,128]{3,2,1,0:T(8,128)(2,1)S(1)}, u32[]{:S(2)}, u32[]{:S(2)}) async-start(bf16[32,2,48,128]{3,2,1,0:T(8,128)(2,1)} %grid.2), calls=%async_computation.1 | async-start | bytes 1572864 | tf_op jit(solution)/shard_map/all_to_all | solution.py:414
  125.1 3.4 %last.2.rest_0_ = bf16[32,192,128]{2,1,0:T(8,128)(2,1)} custom-call(bf16[32,2,48,128]{3,2,1,0:T(8,128)(2,1)S(1)} %all-to-all-done.3.inp, bf16[192,768]{1,0:T(8,128)(2,1)S(1)} %copy-done.6, bf16[192,768]{1,0:T(8,128)(2,1)S(1)} %copy-done.7), custom_call_target="tpu_custom_call" | custom-call | flops 2048000000 | bytes 1638400 | tf_op jit(solution)/shard_map/last/pallas_call | solution.py:354
  128.5 13.3 %all-to-all-done.1.inp = bf16[32,2,48,128]{3,2,1,0:T(8,128)(2,1)S(1)} async-done(((bf16[32,2,48,128]{3,2,1,0:T(8,128)(2,1)}), bf16[32,2,48,128]{3,2,1,0:T(8,128)(2,1)S(1)}, u32[]{:S(2)}, u32[]{:S(2)}) %all-to-all-start.1) | async-done | bytes 786464 | tf_op jit(solution)/shard_map/all_to_all | solution.py:414
  141.9 3.4 %last.3 = bf16[32,192,128]{2,1,0:T(8,128)(2,1)} custom-call(bf16[32,2,48,128]{3,2,1,0:T(8,128)(2,1)S(1)} %all-to-all-done.1.inp, bf16[192,768]{1,0:T(8,128)(2,1)S(1)} %copy-done.6, bf16[192,768]{1,0:T(8,128)(2,1)S(1)} %copy-done.7, bf16[32,192,128]{2,1,0:T(8,128)(2,1)} %last.2.rest_0_), custom_call_target="tpu_custom_call", output_to_operand_aliasing={{}: (3, {})} | custom-call | flops 2048000000 | bytes 1638400 | tf_op jit(solution)/shard_map/last/pallas_call | solution.py:354
  (58 shorter events, 0.8 us)
Async XLA Ops:
  0.8 15.6 %collective-permute-start.1 = (bf16[1,192,128]{2,1,0:T(8,128)(2,1)S(1)}, bf16[1,192,128]{2,1,0:T(8,128)(2,1)S(1)}, u32[]{:S(2)}, u32[]{:S(2)}) collective-permute-start(bf16[1,192,128]{2,1,0:T(8,128)(2,1)S(1)} %get-tuple-element.11), channel_id=1, source_target_pairs={{4,0},{8,4},{12,8},{16,12},{20,16},{24,20},{28,24},{32,28},{36,32}... | collective-permute-start | bytes 147464 | tf_op jit(solution)/shard_map/ppermute | solution.py:380
  2.1 9.1 %copy-start.15 = (f32[6,15,15]{2,1,0:T(8,128)S(1)}, f32[6,15,15]{2,1,0:T(8,128)}, u32[]{:S(2)}) copy-start(f32[6,15,15]{2,1,0:T(8,128)} %param.20) | copy-start | bytes 16204
  2.1 9.1 %copy-start.16 = (f32[6,15,15]{2,1,0:T(8,128)S(1)}, f32[6,15,15]{2,1,0:T(8,128)}, u32[]{:S(2)}) copy-start(f32[6,15,15]{2,1,0:T(8,128)} %param.25) | copy-start | bytes 16204
  2.1 14.6 %collective-permute-start = (bf16[1,192,128]{2,1,0:T(8,128)(2,1)S(1)}, bf16[1,192,128]{2,1,0:T(8,128)(2,1)S(1)}, u32[]{:S(2)}, u32[]{:S(2)}) collective-permute-start(bf16[1,192,128]{2,1,0:T(8,128)(2,1)S(1)} %get-tuple-element.12), channel_id=1, source_target_pairs={{0,4},{4,8},{8,12},{12,16},{16,20},{20,24},{24,28},{28,32},{32,36}... | collective-permute-start | bytes 147464 | tf_op jit(solution)/shard_map/ppermute | solution.py:380
  12.4 12.6 %copy-start.17 = (bf16[3,3,768]{2,1,0:T(4,128)(2,1)S(1)}, bf16[3,3,768]{2,1,0:T(4,128)(2,1)}, u32[]{:S(2)}) copy-start(bf16[3,3,768]{2,1,0:T(4,128)(2,1)} %param.16) | copy-start | bytes 41476
  12.4 17.2 %copy-start = (bf16[32,192,128]{2,1,0:T(8,128)(2,1)S(1)}, bf16[32,192,128]{2,1,0:T(8,128)(2,1)}, u32[]{:S(2)}) copy-start(bf16[32,192,128]{2,1,0:T(8,128)(2,1)} %after.3) | copy-start | bytes 4718596
  12.4 17.2 %copy-start.1 = (bf16[192,768]{1,0:T(8,128)(2,1)S(1)}, bf16[192,768]{1,0:T(8,128)(2,1)}, u32[]{:S(2)}) copy-start(bf16[192,768]{1,0:T(8,128)(2,1)} %w_expand.3) | copy-start | bytes 884740
  12.4 17.2 %copy-start.2 = (bf16[192,768]{1,0:T(8,128)(2,1)S(1)}, bf16[192,768]{1,0:T(8,128)(2,1)}, u32[]{:S(2)}) copy-start(bf16[192,768]{1,0:T(8,128)(2,1)} %w_project.3) | copy-start | bytes 884740
  12.4 17.2 %copy-start.3 = (bf16[192,768]{1,0:T(8,128)(2,1)S(1)}, bf16[192,768]{1,0:T(8,128)(2,1)}, u32[]{:S(2)}) copy-start(bf16[192,768]{1,0:T(8,128)(2,1)} %w_in.5) | copy-start | bytes 884740
  12.4 17.2 %copy-start.4 = (bf16[192,768]{1,0:T(8,128)(2,1)S(1)}, bf16[192,768]{1,0:T(8,128)(2,1)}, u32[]{:S(2)}) copy-start(bf16[192,768]{1,0:T(8,128)(2,1)} %w_back.5) | copy-start | bytes 884740
  12.4 17.2 %copy-start.8 = (bf16[192,576]{1,0:T(8,128)(2,1)S(1)}, bf16[192,576]{1,0:T(8,128)(2,1)}, u32[]{:S(2)}) copy-start(bf16[192,576]{1,0:T(8,128)(2,1)} %w_qkv.6) | copy-start | bytes 663556
  12.4 17.2 %copy-start.11 = (bf16[192,192]{1,0:T(8,128)(2,1)S(1)}, bf16[192,192]{1,0:T(8,128)(2,1)}, u32[]{:S(2)}) copy-start(bf16[192,192]{1,0:T(8,128)(2,1)} %w_out.6) | copy-start | bytes 221188
  16.9 8.0 %collective-permute-start.2 = (bf16[34,192]{1,0:T(8,128)(2,1)S(1)}, bf16[34,192]{1,0:T(8,128)(2,1)S(1)}, u32[]{:S(2)}, u32[]{:S(2)}) collective-permute-start(bf16[34,192]{1,0:T(8,128)(2,1)S(1)} %pad_maximum_fusion), channel_id=1, source_target_pairs={{0,1},{1,2},{2,3},{4,5},{5,6},{6,7},{8,9},{9,10},{10,11},{12,13},{... | collective-permute-start | bytes 39176 | tf_op jit(solution)/shard_map/ppermute | solution.py:380
  23.0 6.6 %collective-permute-start.3 = (bf16[34,192]{1,0:T(8,128)(2,1)S(1)}, bf16[34,192]{1,0:T(8,128)(2,1)S(1)}, u32[]{:S(2)}, u32[]{:S(2)}) collective-permute-start(bf16[34,192]{1,0:T(8,128)(2,1)S(1)} %pad_maximum_fusion.1), channel_id=1, source_target_pairs={{1,0},{2,1},{3,2},{5,4},{6,5},{7,6},{9,8},{10,9},{11,10},{13,12},{... | collective-permute-start | bytes 39176 | tf_op jit(solution)/shard_map/ppermute | solution.py:380
  25.0 21.1 %copy-start.13 = (bf16[34,192]{1,0:T(8,128)(2,1)}, bf16[34,192]{1,0:T(8,128)(2,1)S(1)}, u32[]{:S(2)}) copy-start(bf16[34,192]{1,0:T(8,128)(2,1)S(1)} %collective-permute-done.2) | copy-start | bytes 39172
  29.6 16.5 %copy-start.14 = (bf16[34,192]{1,0:T(8,128)(2,1)}, bf16[34,192]{1,0:T(8,128)(2,1)S(1)}, u32[]{:S(2)}) copy-start(bf16[34,192]{1,0:T(8,128)(2,1)S(1)} %collective-permute-done.3) | copy-start | bytes 39172
  46.1 27.9 %all-to-all-start.2 = ((bf16[32,2,48,128]{3,2,1,0:T(8,128)(2,1)}), bf16[32,2,48,128]{3,2,1,0:T(8,128)(2,1)S(1)}, u32[]{:S(2)}, u32[]{:S(2)}) async-start(bf16[32,2,48,128]{3,2,1,0:T(8,128)(2,1)} %first.3), calls=%async_computation.2 | async-start | bytes 1572864 | tf_op jit(solution)/shard_map/all_to_all | solution.py:412
  55.7 1.0 copy-start.5
  56.6 0.9 copy-start.9
  74.0 10.0 %copy-start.10 = (bf16[192,576]{1,0:T(8,128)(2,1)S(1)}, bf16[192,576]{1,0:T(8,128)(2,1)}, u32[]{:S(2)}) copy-start(bf16[192,576]{1,0:T(8,128)(2,1)} %w_qkv.7) | copy-start | bytes 663556
  74.0 10.0 %copy-start.12 = (bf16[192,192]{1,0:T(8,128)(2,1)S(1)}, bf16[192,192]{1,0:T(8,128)(2,1)}, u32[]{:S(2)}) copy-start(bf16[192,192]{1,0:T(8,128)(2,1)} %w_out.7) | copy-start | bytes 221188
  74.0 26.9 %all-to-all-start = ((bf16[32,2,48,128]{3,2,1,0:T(8,128)(2,1)}), bf16[32,2,48,128]{3,2,1,0:T(8,128)(2,1)S(1)}, u32[]{:S(2)}, u32[]{:S(2)}) async-start(bf16[32,2,48,128]{3,2,1,0:T(8,128)(2,1)} %first.2), calls=%async_computation | async-start | bytes 1572864 | tf_op jit(solution)/shard_map/all_to_all | solution.py:412
  100.9 20.5 %all-to-all-start.3 = ((bf16[32,2,48,128]{3,2,1,0:T(8,128)(2,1)}), bf16[32,2,48,128]{3,2,1,0:T(8,128)(2,1)S(1)}, u32[]{:S(2)}, u32[]{:S(2)}) async-start(bf16[32,2,48,128]{3,2,1,0:T(8,128)(2,1)} %grid.3), calls=%async_computation.3 | async-start | bytes 1572864 | tf_op jit(solution)/shard_map/all_to_all | solution.py:414
  110.7 14.4 %copy-start.6 = (bf16[192,768]{1,0:T(8,128)(2,1)S(1)}, bf16[192,768]{1,0:T(8,128)(2,1)}, u32[]{:S(2)}) copy-start(bf16[192,768]{1,0:T(8,128)(2,1)} %w_in.7) | copy-start | bytes 884740
  110.7 14.4 %copy-start.7 = (bf16[192,768]{1,0:T(8,128)(2,1)S(1)}, bf16[192,768]{1,0:T(8,128)(2,1)}, u32[]{:S(2)}) copy-start(bf16[192,768]{1,0:T(8,128)(2,1)} %w_back.7) | copy-start | bytes 884740
  121.4 20.5 %all-to-all-start.1 = ((bf16[32,2,48,128]{3,2,1,0:T(8,128)(2,1)}), bf16[32,2,48,128]{3,2,1,0:T(8,128)(2,1)S(1)}, u32[]{:S(2)}, u32[]{:S(2)}) async-start(bf16[32,2,48,128]{3,2,1,0:T(8,128)(2,1)} %grid.2), calls=%async_computation.1 | async-start | bytes 1572864 | tf_op jit(solution)/shard_map/all_to_all | solution.py:414

commit v3 on v2

--- a/solution.py
+++ b/solution.py
@@ -19,7 +19,6 @@
 ROWS_CHUNK = 8
 TILES = 16
 LAG = 3
-CALLS = (2, 2)
 LOG2E = 1.4426950408889634
 F32 = jnp.float32
 BF16 = jnp.bfloat16
@@ -114,20 +113,40 @@
     return s + dot(w_out_t, jnp.concatenate(mixed, axis=1))
 
 
-def prepare(w_qkv, w_out, table, wq_t, wk, wv_t, w_out_t, bias):
+def bias_rows(table, padded, bias):
+    lane = lax.broadcasted_iota(jnp.int32, (16, 128), 1)
+    line = lax.broadcasted_iota(jnp.int32, (16, 128), 0)
+    spread = jnp.where(lane // WIN == line, 1.0, 0.0)
+    left = lax.broadcasted_iota(jnp.int32, (WIN, 128), 1) < TOKENS
+    padded[...] = jnp.zeros_like(padded)
+    heads = []
+    for h in range(HEADS):
+        padded[h, 0:15, 0:15] = table[h]
+        cells = lax.dot_general(
+            padded[h][:, :16], spread, TN, precision=lax.Precision.HIGHEST,
+            preferred_element_type=F32,
+        )
+        rows = [
+            jnp.sum(jnp.where(line == 7 - v + lane % WIN, cells, 0.0), axis=0, keepdims=True)
+            for v in range(WIN)
+        ]
+        heads.append(jnp.concatenate(rows, axis=0))
+    for u in range(WIN):
+        for p in range(3):
+            start = (7 - u) * WIN
+            even = pltpu.roll(heads[2 * p], (128 - start) % 128, 1)
+            odd = pltpu.roll(heads[2 * p + 1], (64 - start) % 128, 1)
+            bias[u * WIN : (u + 1) * WIN, 128 * p : 128 * p + 128] = (
+                jnp.where(left, even, odd) * LOG2E
+            )
+
+
+def prepare(w_qkv, w_out, table, wq_t, wk, wv_t, w_out_t, bias, padded):
     wq_t[...] = w_qkv[:, 0:D].T
     wk[...] = w_qkv[:, D : 2 * D]
     wv_t[...] = w_qkv[:, 2 * D : 3 * D].T
     w_out_t[...] = w_out[...].T
-    left = lax.broadcasted_iota(jnp.int32, (WIN, 128), 1) < TOKENS
-    for u in range(WIN):
-        for p in range(3):
-            start = (7 - u) * WIN
-            even = pltpu.roll(table[2 * p], (128 - start) % 128, 1)
-            odd = pltpu.roll(table[2 * p + 1], (64 - start) % 128, 1)
-            bias[u * WIN : (u + 1) * WIN, 128 * p : 128 * p + 128] = (
-                jnp.where(left, even, odd) * LOG2E
-            )
+    bias_rows(table, padded, bias)
 
 
 def gather_groups(lo, hi):
@@ -139,14 +158,12 @@
 
 
 def first_kernel(
-    first, last,
-    image, before, after, top, bottom, left, right,
-    w_expand, dw, w_project, w_qkv, w_out, table, w_in, w_back,
-    out, expanded, mobile, tokens, lo, hi, place, wq_t, wk, wv_t, w_out_t, w_in_t, bias,
+    edge, image, before, after, top, bottom, left, right,
+    w_expand, taps, w_project, w_qkv, w_out, table, w_in, w_back,
+    out, expanded, mobile, tokens, lo, hi, place, wq_t, wk, wv_t, w_out_t, w_in_t, bias, padded,
+    dw, side,
 ):
     step = pl.program_id(0)
-    steps = pl.num_programs(0)
-    start = pl.multiple_of(step * ROWS_CHUNK, 8)
     line = lax.broadcasted_iota(jnp.int32, (16, HID), 0)
 
     def laid(x):
@@ -162,31 +179,48 @@
             follow = pltpu.roll(e[0:16], 15, 0)
             expanded[r, 144:160, :] = jnp.where(line == 15, sides[1][r : r + 1], follow)
 
-    sides = [
-        gelu(dot(halo[pl.ds(start, 16), :].astype(BF16), w_expand[...])).astype(F32)
-        for halo in (left, right)
-    ]
-
     @pl.when(step == 0)
     def _():
-        prepare(w_qkv, w_out, table, wq_t, wk, wv_t, w_out_t, bias)
+        for i in range(3):
+            dw[3 * i : 3 * i + 3, :] = taps[i].astype(F32)
+        for i, halo in enumerate((left, right)):
+            side[i, 8:40, :] = gelu(dot(halo[...], w_expand[...])).astype(F32)
+            if edge:
+                for j, message in enumerate((top, bottom)):
+                    pair = message[D + 32 * i : D + 32 * i + 32, :]
+                    corner = jnp.concatenate([pair[0:16], pair[16:32, 0:64]], axis=1)
+                    ends = gelu(dot(corner, w_expand[...])).astype(F32)
+                    side[i, 40 * j : 40 * j + 8, :] = jnp.broadcast_to(ends[0:1], (8, HID))
+        prepare(w_qkv, w_out, table, wq_t, wk, wv_t, w_out_t, bias, padded)
         w_in_t[...] = w_in[...].T
         row = lax.broadcasted_iota(jnp.int32, (COLS, COLS), 0)
         col = lax.broadcasted_iota(jnp.int32, (COLS, COLS), 1)
         place[...] = jnp.where(col == (row % 16) * 8 + row // 16, 1.0, 0.0).astype(BF16)
-        above = top[0] if first else before[0]
+
+    order = (step + 1) if not edge else jnp.where(step == 0, 3, 0)
+    start = pl.multiple_of(order * ROWS_CHUNK, 8)
+    sides = [side[i, pl.ds(start, 24), :][7:23] for i in range(2)]
+
+    def begin():
+        above = before[0]
+        if edge:
+            above = jnp.where(step == 0, above, top[0:D, :])
         pair = jnp.concatenate([laid(above), laid(image[0])], axis=0)
         tokens[0:COLS, :] = pair[COLS:]
         expand(pair, sides, (0, 1))
 
-    @pl.when(step > 0)
-    def _():
-        tokens[0:COLS, :] = tokens[8 * COLS : 9 * COLS, :]
-        expanded[0:2] = expanded[8:10]
-
     below = after[0]
-    if last:
-        below = jnp.where(step == steps - 1, bottom[0], below)
+    if edge:
+        below = jnp.where(step == 0, bottom[0:D, :], below)
+        begin()
+    else:
+        pl.when(step == 0)(begin)
+
+        @pl.when(step > 0)
+        def _():
+            tokens[0:COLS, :] = tokens[8 * COLS : 9 * COLS, :]
+            expanded[0:2] = expanded[8:10]
+
     for r in range(1, ROWS_CHUNK):
         tokens[COLS * r : COLS * (r + 1), :] = laid(image[r])
     tokens[COLS * 8 : COLS * 9, :] = laid(below)
@@ -223,17 +257,23 @@
 
 
 def grid_kernel(
-    inp, w_qkv, w_out, table, out, lo, hi, wq_t, wk, wv_t, w_out_t, bias
+    one, two, w_qkv, w_out, table, out, lo, hi, wq_t, wk, wv_t, w_out_t, bias, padded
 ):
-    @pl.when(pl.program_id(0) == 0)
+    step = pl.program_id(0)
+
+    @pl.when(step == 0)
     def _():
-        prepare(w_qkv, w_out, table, wq_t, wk, wv_t, w_out_t, bias)
-
-    for src in range(32):
-        lo[32 * src : 32 * src + 32, :] = inp[src, 0, 0:32, :].astype(F32)
-        both = inp[src, 0, 32:48, :].astype(F32)
-        hi[32 * src : 32 * src + 16, :] = both
-        hi[32 * src + 16 : 32 * src + 32, :] = pltpu.roll(both, 64, 1)
+        prepare(w_qkv, w_out, table, wq_t, wk, wv_t, w_out_t, bias, padded)
+
+    def unpack(inp):
+        for src in range(32):
+            lo[32 * src : 32 * src + 32, :] = inp[src, 0, 0:32, :].astype(F32)
+            both = inp[src, 0, 32:48, :].astype(F32)
+            hi[32 * src : 32 * src + 16, :] = both
+            hi[32 * src + 16 : 32 * src + 32, :] = pltpu.roll(both, 64, 1)
+
+    pl.when(step < 2)(lambda: unpack(one))
+    pl.when(step >= 2)(lambda: unpack(two))
     s = gather_groups(lo, hi)
     s = attend(s, wq_t[...], wk[...], wv_t[...], w_out_t[...], bias).T
     for g in range(TILES):
@@ -249,9 +289,7 @@
         ).astype(BF16)
 
 
-def last_kernel(inp, w_in, w_back, *rest):
-    out, w_in_t = rest[-2:]
-
+def last_kernel(inp, w_in, w_back, out, w_in_t):
     @pl.when(pl.program_id(0) == 0)
     def _():
         w_in_t[...] = w_in[...].T
@@ -269,6 +307,29 @@
         out[r] = s[:, COLS * r : COLS * (r + 1)]
 
 
+def pack_kernel(lowest, highest, left, right, down, up):
+    for r, cells, out in ((left.shape[0] - 1, lowest, down), (0, highest, up)):
+        out[0:D, :] = cells[0]
+        for i, halo in enumerate((left, right)):
+            cell = halo[r : r + 1, :].astype(F32)
+            high = jnp.concatenate([cell[:, 128:], cell[:, 128:]], axis=1)
+            at = D + 32 * i
+            out[at : at + 16, :] = jnp.broadcast_to(cell[:, :128], (16, 128)).astype(BF16)
+            out[at + 16 : at + 32, :] = jnp.broadcast_to(high, (16, 128)).astype(BF16)
+
+
+def edge_kernel(image, out):
+    rows = image.shape[0]
+    row = lax.broadcasted_iota(jnp.int32, (2 * rows, COLS * rows), 0)
+    col = lax.broadcasted_iota(jnp.int32, (2 * rows, COLS * rows), 1)
+    wanted = jnp.where(row < rows, row * COLS, (row - rows) * COLS + COLS - 1)
+    pick = jnp.where(col == wanted, 1.0, 0.0).astype(BF16)
+    cells = jnp.concatenate([image[r] for r in range(rows)], axis=1)
+    got = dot(pick, cells, NT).astype(BF16)
+    out[0] = got[:rows]
+    out[1] = got[rows:]
+
+
 def whole(shape):
     return pl.BlockSpec(shape, lambda k: (0,) * len(shape))
 
@@ -286,19 +347,55 @@
 ]
 
 
-def call_first(base, chunks, image, top, bottom, left, right, weights):
+def call_edge(image):
+    rows = image.shape[0]
+    return pl.pallas_call(
+        edge_kernel,
+        out_shape=jax.ShapeDtypeStruct((2, rows, D), BF16),
+        compiler_params=pltpu.CompilerParams(vmem_limit_bytes=32 << 20),
+        cost_estimate=pl.CostEstimate(flops=4000000, bytes_accessed=1600000, transcendentals=0),
+        name="edge",
+    )(image)
+
+
+def call_pack(image, left, right):
+    shape = jax.ShapeDtypeStruct((D + 64, COLS), BF16)
+    rows = image.shape[0]
+    return pl.pallas_call(
+        pack_kernel,
+        grid=(1,),
+        in_specs=[
+            pl.BlockSpec((1, D, COLS), lambda k: (rows - 1, 0, 0)),
+            pl.BlockSpec((1, D, COLS), lambda k: (0, 0, 0)),
+            whole(left.shape),
+            whole(right.shape),
+        ],
+        out_specs=(whole(shape.shape), whole(shape.shape)),
+        out_shape=(shape, shape),
+        compiler_params=pltpu.CompilerParams(vmem_limit_bytes=32 << 20),
+        cost_estimate=pl.CostEstimate(flops=40000, bytes_accessed=200000, transcendentals=0),
+        name="pack",
+    )(image, image, left, right)
+
+
+def call_first(edge, image, halos, weights):
+    chunks = 2
     total = image.shape[0]
-    first, last = base == 0, (base + chunks) * ROWS_CHUNK == total
-    rows = pl.BlockSpec((ROWS_CHUNK, D, COLS), lambda k: (base + k, 0, 0))
-    before = pl.BlockSpec((1, D, COLS), lambda k: (max(base * ROWS_CHUNK - 1, 0), 0, 0))
+
+    def chunk(k):
+        return 3 - 3 * k if edge else 1 + k
+
+    rows = pl.BlockSpec((ROWS_CHUNK, D, COLS), lambda k: (chunk(k), 0, 0))
+    before = pl.BlockSpec(
+        (1, D, COLS), lambda k: (jnp.maximum(chunk(k) * ROWS_CHUNK - 1, 0), 0, 0)
+    )
     after = pl.BlockSpec(
-        (1, D, COLS), lambda k: (jnp.minimum((base + k + 1) * ROWS_CHUNK, total - 1), 0, 0)
+        (1, D, COLS), lambda k: (jnp.minimum((chunk(k) + 1) * ROWS_CHUNK, total - 1), 0, 0)
     )
-    at = slice(base * ROWS_CHUNK, (base + chunks) * ROWS_CHUNK + 8)
-    small = [top, bottom, left[at], right[at]] + weights
+    small = halos + weights
     tokens = chunks * CHUNK
     return pl.pallas_call(
-        functools.partial(first_kernel, first, last),
+        functools.partial(first_kernel, edge),
         grid=(chunks,),
         in_specs=[rows, before, after] + [whole(a.shape) for a in small],
         out_specs=BLOCK,
@@ -312,8 +409,14 @@
             pltpu.VMEM((COLS, COLS), BF16),
         ]
         + ATTEND_SCRATCH
-        + [pltpu.VMEM((HID, D), BF16), pltpu.VMEM((TOKENS, HEADS * TOKENS), F32)],
-        compiler_params=vm(48),
+        + [
+            pltpu.VMEM((HID, D), BF16),
+            pltpu.VMEM((TOKENS, HEADS * TOKENS), F32),
+            pltpu.VMEM((HEADS, 16, 128), F32),
+            pltpu.VMEM((9, HID), F32),
+            pltpu.VMEM((2, 48, HID), F32),
+        ],
+        compiler_params=vm(60 if edge else 48),
         cost_estimate=pl.CostEstimate(
             flops=tokens * 2000000, bytes_accessed=tokens * 800, transcendentals=tokens * 2700
         ),
@@ -321,55 +424,47 @@
     )(image, image, image, *small)
 
 
-def call_grid(arrived, weights):
-    chunks = arrived.shape[1]
+def call_grid(one, two, weights):
+    chunks = one.shape[1] + two.shape[1]
     tokens = chunks * CHUNK
+    shape = (32, 1, 48, 128)
     return pl.pallas_call(
         grid_kernel,
         grid=(chunks,),
-        in_specs=[BLOCK] + [whole(a.shape) for a in weights],
+        in_specs=[
+            pl.BlockSpec(shape, lambda k: (0, jnp.minimum(k, 1), 0, 0)),
+            pl.BlockSpec(shape, lambda k: (0, jnp.maximum(k - 2, 0), 0, 0)),
+        ]
+        + [whole(a.shape) for a in weights],
         out_specs=BLOCK,
-        out_shape=jax.ShapeDtypeStruct(arrived.shape, BF16),
+        out_shape=jax.ShapeDtypeStruct((32, chunks, 48, 128), BF16),
         scratch_shapes=[pltpu.VMEM((CHUNK, 128), F32), pltpu.VMEM((CHUNK, 128), F32)]
         + ATTEND_SCRATCH
-        + [pltpu.VMEM((TOKENS, HEADS * TOKENS), F32)],
-        compiler_params=vm(32),
+        + [pltpu.VMEM((TOKENS, HEADS * TOKENS), F32), pltpu.VMEM((HEADS, 16, 128), F32)],
+        compiler_params=vm(48),
         cost_estimate=pl.CostEstimate(
             flops=tokens * 1000000, bytes_accessed=tokens * 800, transcendentals=tokens * 400
         ),
         name="grid",
-    )(arrived, *weights)
-
-
-def call_last(base, rows, returned, w_in, w_back, earlier):
+    )(one, two, *weights)
+
+
+def call_last(returned, w_in, w_back):
     chunks = returned.shape[1]
     tokens = chunks * CHUNK
-    operands = [returned, w_in, w_back]
-    specs = [BLOCK, whole(w_in.shape), whole(w_back.shape)]
-    aliases = {}
-    if earlier is not None:
-        operands.append(earlier)
-        specs.append(pl.BlockSpec(memory_space=pl.ANY))
-        aliases = {3: 0}
     return pl.pallas_call(
         last_kernel,
         grid=(chunks,),
-        in_specs=specs,
-        out_specs=pl.BlockSpec((ROWS_CHUNK, D, COLS), lambda k: (base + k, 0, 0)),
-        out_shape=jax.ShapeDtypeStruct((rows, D, COLS), BF16),
+        in_specs=[BLOCK, whole(w_in.shape), whole(w_back.shape)],
+        out_specs=pl.BlockSpec((ROWS_CHUNK, D, COLS), lambda k: (lax.rem(k + 1, chunks), 0, 0)),
+        out_shape=jax.ShapeDtypeStruct((chunks * ROWS_CHUNK, D, COLS), BF16),
         scratch_shapes=[pltpu.VMEM((HID, D), BF16)],
-        input_output_aliases=aliases,
-        compiler_params=vm(32),
+        compiler_params=vm(48),
         cost_estimate=pl.CostEstimate(
             flops=tokens * 1000000, bytes_accessed=tokens * 800, transcendentals=tokens * 800
         ),
         name="last",
-    )(*operands)
-
-
-def bias_tables(tables):
-    cols = jnp.stack([tables[:, :, 7 - v : 15 - v] for v in range(WIN)], axis=1)
-    return jnp.pad(cols.reshape(2 * HEADS, WIN, 15 * WIN), ((0, 0), (0, 0), (0, 8)))
+    )(returned, w_in, w_back)
 
 
 def shift(x, axis, count, step):
@@ -389,32 +484,23 @@
     image, w_expand, dw_kernel, w_project, block_qkv, block_out, block_bias, mlp_in, mlp_out,
     grid_qkv, grid_out, grid_bias, mlp2_in, mlp2_out,
 ):
-    rows = image.shape[0]
-    top = shift(image[rows - 1 :], ROW_AXES, 32, 1)
-    bottom = shift(image[:1], ROW_AXES, 32, -1)
-    ends = [
-        jnp.concatenate([top[:, :, c], image[:, :, c], bottom[:, :, c]], axis=0)
-        for c in (0, COLS - 1)
+    edges = call_edge(image)
+    left = shift(edges[1], COL_AXES, 4, 1)
+    right = shift(edges[0], COL_AXES, 4, -1)
+    down, up = call_pack(image, left, right)
+    top = shift(down, ROW_AXES, 32, 1)
+    bottom = shift(up, ROW_AXES, 32, -1)
+    weights = [
+        w_expand, dw_kernel, w_project, block_qkv, block_out, block_bias, mlp_in, mlp_out
     ]
-    left = shift(ends[1], COL_AXES, 4, 1)
-    right = shift(ends[0], COL_AXES, 4, -1)
-    left = jnp.pad(left.astype(F32), ((0, 6), (0, 0)))
-    right = jnp.pad(right.astype(F32), ((0, 6), (0, 0)))
-    tables = bias_tables(jnp.concatenate([block_bias, grid_bias], axis=0))
-    weights = [
-        w_expand, dw_kernel.reshape(9, HID).astype(F32), w_project, block_qkv, block_out,
-        tables[:HEADS], mlp_in, mlp_out,
-    ]
-    base = 0
-    result = None
-    for chunks in CALLS:
-        sent = call_first(base, chunks, image, top, bottom, left, right, weights)
-        arrived = lax.all_to_all(sent, GROUP, 0, 0, tiled=True)
-        mixed = call_grid(arrived, [grid_qkv, grid_out, tables[HEADS:]])
-        back = lax.all_to_all(mixed, GROUP, 0, 0, tiled=True)
-        result = call_last(base, rows, back, mlp2_in, mlp2_out, result)
-        base += chunks
-    return result
+    inner = call_first(False, image, [down, up, left, right], weights)
+    inner, top, bottom = lax.optimization_barrier((inner, top, bottom))
+    one = lax.all_to_all(inner, GROUP, 0, 0, tiled=True)
+    outer = call_first(True, image, [top, bottom, left, right], weights)
+    two = lax.all_to_all(outer, GROUP, 0, 0, tiled=True)
+    mixed = call_grid(one, two, [grid_qkv, grid_out, grid_bias])
+    back = lax.all_to_all(mixed, GROUP, 0, 0, tiled=True)
+    return call_last(back, mlp2_in, mlp2_out)
 
 
 def solution(mesh):

time: 146 us -> 137 us (0.938)
  blocking collectives: 0 us -> 55.7 us
  waiting for transfers between devices: 39.7 us -> 0.84 us
  starting transfers between devices: 39.5 us -> 26.5 us
  local copies, waits for them, and re-layouts: 12.7 us -> 1.51 us
  other arithmetic: 1.49 us -> 0 us
    all_to_all x0 -> x2, blocking collectives: none -> 55.7 us  [the longest x1 28.8 us: body(): back = lax.all_to_all(mixed, GROUP, 0, 0, tiled=True)]
    all_to_all x4 -> x1, waiting for transfers between devices: 35.1 us -> 0.01 us  [body(): one = lax.all_to_all(inner, GROUP, 0, 0, tiled=True)]
    all_to_all x4 -> x1, starting transfers between devices: 25.6 us -> 14 us  [body(): one = lax.all_to_all(inner, GROUP, 0, 0, tiled=True)]
    slice x10 -> x0, local copies, waits for them, and re-layouts: 5.81 us -> none  [the longest x1 4.35 us: body(): image[:, :, c]]
    unnamed x39 -> x38, local copies, waits for them, and re-layouts: 5.92 us -> 1.51 us
    ppermute x4, waiting for transfers between devices: 4.6 us -> 0.84 us  [shift(): return lax.ppermute(x, axis, pairs)]
    convert_element_type x2 -> x0, other arithmetic: 1.47 us -> none  [the longest x1 0.73 us: body(): left = jnp.pad(left.astype(F32), ((0, 6), (0, 0)))]
  transfers between devices with their start and end apart: 8 -> 5, of which waited for: 4 -> 1; matrix products, arithmetic and copies ran while one was open for 8% -> 0% of each run, Pallas kernels for 22% -> 25%
where the time goes in v3:
time: 137 us
  blocking collectives  55.7 us (41%)
  Pallas kernels  51.8 us (38%)
  starting transfers between devices  26.5 us (19%)
  local copies, waits for them, and re-layouts  1.51 us (1%)
    pallas_call x2, Pallas kernels, call_first(): pl.pallas_call(functools.partial(first_kernel, edge), grid=(chunks,), in_...  34.8 us
    all_to_all x1, blocking collectives, body(): back = lax.all_to_all(mixed, GROUP, 0, 0, tiled=True)  28.8 us
    all_to_all x1, blocking collectives, body(): two = lax.all_to_all(outer, GROUP, 0, 0, tiled=True)  26.9 us
    all_to_all x1, starting transfers between devices, body(): one = lax.all_to_all(inner, GROUP, 0, 0, tiled=True)  14 us
    ppermute x4, starting transfers between devices, shift(): return lax.ppermute(x, axis, pairs)  12.6 us
    pallas_call x1, Pallas kernels, call_grid(): pl.pallas_call(grid_kernel, grid=(chunks,), in_specs=[pl.BlockSpec(shape,...  10.4 us
    pallas_call x1, Pallas kernels, call_last(): pl.pallas_call(last_kernel, grid=(chunks,), in_specs=[BLOCK, whole(w_in.s...  5.9 us
  transfers between devices with their start and end apart: 5, of which 1 were waited for; matrix products, arithmetic and copies ran while one was open for 0% of the time, Pallas kernels for 25%

profile of v3, /device:TPU:1, one launch (start us, length us, event | category | flops | bytes accessed | tf_op | source)
XLA Modules:
  0.0 136.7 jit_solution(11647507554592614894)
XLA Ops:
  0.0 1.4 %copy-done = bf16[32,192,128]{2,1,0:T(8,128)(2,1)S(1)} copy-done((bf16[32,192,128]{2,1,0:T(8,128)(2,1)S(1)}, bf16[32,192,128]{2,1,0:T(8,128)(2,1)}, u32[]{:S(2)}) %copy-start) | copy-done | bytes 1572888
  1.4 0.6 edge.1
  2.0 3.3 %collective-permute-start.1 = (bf16[32,192]{1,0:T(8,128)(2,1)S(1)}, bf16[32,192]{1,0:T(8,128)(2,1)S(1)}, u32[]{:S(2)}, u32[]{:S(2)}) collective-permute-start(bf16[32,192]{1,0:T(8,128)(2,1)S(1)} %get-tuple-element.15), channel_id=1, source_target_pairs={{1,0},{2,1},{3,2},{5,4},{6,5},{7,6},{9,8},{10,9},{11,10},{13,12},{... | collective-permute-start | bytes 36872 | tf_op jit(solution)/shard_map/ppermute | solution.py:475
  5.4 0.0 copy-start.1
  5.4 0.0 copy-start.4
  5.4 0.0 copy-start.5
  5.4 0.0 copy-start.6
  5.4 0.0 copy-start.7
  5.4 0.0 copy-start.10
  5.4 0.0 copy-start.12
  5.5 0.0 copy-start.14
  5.5 0.0 copy-start.16
  5.5 4.9 %collective-permute-start = (bf16[32,192]{1,0:T(8,128)(2,1)S(1)}, bf16[32,192]{1,0:T(8,128)(2,1)S(1)}, u32[]{:S(2)}, u32[]{:S(2)}) collective-permute-start(bf16[32,192]{1,0:T(8,128)(2,1)S(1)} %get-tuple-element.16), channel_id=1, source_target_pairs={{0,1},{1,2},{2,3},{4,5},{5,6},{6,7},{8,9},{9,10},{10,11},{12,13},{... | collective-permute-start | bytes 36872 | tf_op jit(solution)/shard_map/ppermute | solution.py:475
  10.4 0.0 collective-permute-done.1.right
  10.4 0.8 collective-permute-done.left
  11.2 0.1 pack.1
  11.3 3.0 %collective-permute-start.2 = (bf16[256,128]{1,0:T(8,128)(2,1)S(1)}, bf16[256,128]{1,0:T(8,128)(2,1)S(1)}, u32[]{:S(2)}, u32[]{:S(2)}) collective-permute-start(bf16[256,128]{1,0:T(8,128)(2,1)S(1)} %get-tuple-element.10.top), channel_id=1, source_target_pairs={{0,4},{4,8},{8,12},{12,16},{16,20},{20,24},{24,28},{28,32},{32,36}... | collective-permute-start | bytes 196616 | tf_op jit(solution)/shard_map/ppermute | solution.py:475
  14.4 1.3 collective-permute-start.3
  15.8 16.7 %first.2 = bf16[32,2,48,128]{3,2,1,0:T(8,128)(2,1)} custom-call(bf16[32,192,128]{2,1,0:T(8,128)(2,1)S(1)} %copy-done.1, bf16[32,192,128]{2,1,0:T(8,128)(2,1)S(1)} %copy-done.1, bf16[32,192,128]{2,1,0:T(8,128)(2,1)S(1)} %copy-done.1, bf16[256,128]{1,0:T(8,128)(2,1)S(1)} %get-tuple-element.10.top, bf16[256,128]{1,0:T(8,128)(2,1)S(1)} %get-tuple-element.11.bottom, ...), custom_call_target="tpu_custom_call" | custom-call | flops 4096000000 | bytes 1638400 | tf_op jit(solution)/shard_map/first/pallas_call | solution.py:397
  32.5 0.0 collective-permute-done.2.top
  32.5 0.0 collective-permute-done.3.bottom
  32.5 14.0 %all-to-all-start = ((bf16[32,2,48,128]{3,2,1,0:T(8,128)(2,1)}), bf16[32,2,48,128]{3,2,1,0:T(8,128)(2,1)S(1)}, u32[]{:S(2)}, u32[]{:S(2)}) async-start(bf16[32,2,48,128]{3,2,1,0:T(8,128)(2,1)} %first.2), calls=%async_computation | async-start | bytes 1572864 | tf_op jit(solution)/shard_map/all_to_all | solution.py:498
  46.5 18.1 %first.3 = bf16[32,2,48,128]{3,2,1,0:T(8,128)(2,1)} custom-call(bf16[32,192,128]{2,1,0:T(8,128)(2,1)} %after.3, bf16[32,192,128]{2,1,0:T(8,128)(2,1)} %after.3, bf16[32,192,128]{2,1,0:T(8,128)(2,1)} %after.3, bf16[256,128]{1,0:T(8,128)(2,1)} %copy-done.17, bf16[256,128]{1,0:T(8,128)(2,1)} %copy-done.18, bf16[32,192]{1,0:T(8,128)(2,1)} %copy-done.3, ...), custom_call_target="tpu_custom_call" | custom-call | flops 4096000000 | bytes 1638400 | tf_op jit(solution)/shard_map/first/pallas_call | solution.py:397
  64.6 0.0 copy-start.13
  64.6 0.0 copy-start.15
  64.6 0.0 all-to-all-done.one
  64.6 26.9 %all_to_all.15.two = bf16[32,2,48,128]{3,2,1,0:T(8,128)(2,1)S(1)} all-to-all(bf16[32,2,48,128]{3,2,1,0:T(8,128)(2,1)} %first.3), channel_id=1, replica_groups=mesh['y'=4,'zh'=2,'zl'=2,'xl'=2,'xh'=2,'core'=2] {'y','zh','xh','core'}, dimensions={0} | all-to-all | bytes 1572864 | tf_op jit(solution)/shard_map/all_to_all | solution.py:500
  91.5 10.4 %grid.1 = bf16[32,4,48,128]{3,2,1,0:T(8,128)(2,1)S(1)} custom-call(bf16[32,2,48,128]{3,2,1,0:T(8,128)(2,1)S(1)} %all-to-all-done.one, bf16[32,2,48,128]{3,2,1,0:T(8,128)(2,1)S(1)} %all_to_all.15.two, bf16[192,576]{1,0:T(8,128)(2,1)S(1)} %copy-done.11, bf16[192,192]{1,0:T(8,128)(2,1)S(1)} %copy-done.13, f32[6,15,15]{2,1,0:T(8,128)S(1)} %copy-done.15), custom_call_target="tpu_custom_call" | custom-call | flops 4096000000 | bytes 3276800 | tf_op jit(solution)/shard_map/grid/pallas_call | solution.py:431
  101.9 0.0 copy-start.8
  101.9 0.0 copy-start.9
  102.0 28.8 %all_to_all.16.inp = bf16[32,4,48,128]{3,2,1,0:T(8,128)(2,1)S(1)} all-to-all(bf16[32,4,48,128]{3,2,1,0:T(8,128)(2,1)S(1)} %grid.1), channel_id=1, replica_groups=mesh['y'=4,'zh'=2,'zl'=2,'xl'=2,'xh'=2,'core'=2] {'y','zh','xh','core'}, dimensions={0} | all-to-all | bytes 3145728 | tf_op jit(solution)/shard_map/all_to_all | solution.py:502
  130.8 5.9 %last.1 = bf16[32,192,128]{2,1,0:T(8,128)(2,1)} custom-call(bf16[32,4,48,128]{3,2,1,0:T(8,128)(2,1)S(1)} %all_to_all.16.inp, bf16[192,768]{1,0:T(8,128)(2,1)S(1)} %copy-done.8, bf16[192,768]{1,0:T(8,128)(2,1)S(1)} %copy-done.9), custom_call_target="tpu_custom_call" | custom-call | flops 4096000000 | bytes 3276800 | tf_op jit(solution)/shard_map/last/pallas_call | solution.py:455
  (25 shorter events, 0.1 us)
Async XLA Ops:
  0.0 1.4 %copy-start = (bf16[32,192,128]{2,1,0:T(8,128)(2,1)S(1)}, bf16[32,192,128]{2,1,0:T(8,128)(2,1)}, u32[]{:S(2)}) copy-start(bf16[32,192,128]{2,1,0:T(8,128)(2,1)} %after.3) | copy-start | bytes 4718596
  2.0 8.4 %collective-permute-start.1 = (bf16[32,192]{1,0:T(8,128)(2,1)S(1)}, bf16[32,192]{1,0:T(8,128)(2,1)S(1)}, u32[]{:S(2)}, u32[]{:S(2)}) collective-permute-start(bf16[32,192]{1,0:T(8,128)(2,1)S(1)} %get-tuple-element.15), channel_id=1, source_target_pairs={{1,0},{2,1},{3,2},{5,4},{6,5},{7,6},{9,8},{10,9},{11,10},{13,12},{... | collective-permute-start | bytes 36872 | tf_op jit(solution)/shard_map/ppermute | solution.py:475
  5.4 10.3 %copy-start.1 = (bf16[32,192,128]{2,1,0:T(8,128)(2,1)S(1)}, bf16[32,192,128]{2,1,0:T(8,128)(2,1)}, u32[]{:S(2)}) copy-start(bf16[32,192,128]{2,1,0:T(8,128)(2,1)} %after.3) | copy-start | bytes 4718596
  5.4 10.3 %copy-start.4 = (bf16[192,768]{1,0:T(8,128)(2,1)S(1)}, bf16[192,768]{1,0:T(8,128)(2,1)}, u32[]{:S(2)}) copy-start(bf16[192,768]{1,0:T(8,128)(2,1)} %w_expand.3) | copy-start | bytes 884740
  5.4 10.3 %copy-start.5 = (bf16[192,768]{1,0:T(8,128)(2,1)S(1)}, bf16[192,768]{1,0:T(8,128)(2,1)}, u32[]{:S(2)}) copy-start(bf16[192,768]{1,0:T(8,128)(2,1)} %w_project.3) | copy-start | bytes 884740
  5.4 10.3 %copy-start.6 = (bf16[192,768]{1,0:T(8,128)(2,1)S(1)}, bf16[192,768]{1,0:T(8,128)(2,1)}, u32[]{:S(2)}) copy-start(bf16[192,768]{1,0:T(8,128)(2,1)} %w_in.4) | copy-start | bytes 884740
  5.4 10.3 %copy-start.7 = (bf16[192,768]{1,0:T(8,128)(2,1)S(1)}, bf16[192,768]{1,0:T(8,128)(2,1)}, u32[]{:S(2)}) copy-start(bf16[192,768]{1,0:T(8,128)(2,1)} %w_back.4) | copy-start | bytes 884740
  5.4 10.3 %copy-start.10 = (bf16[192,576]{1,0:T(8,128)(2,1)S(1)}, bf16[192,576]{1,0:T(8,128)(2,1)}, u32[]{:S(2)}) copy-start(bf16[192,576]{1,0:T(8,128)(2,1)} %w_qkv.4) | copy-start | bytes 663556
  5.4 10.3 %copy-start.12 = (bf16[192,192]{1,0:T(8,128)(2,1)S(1)}, bf16[192,192]{1,0:T(8,128)(2,1)}, u32[]{:S(2)}) copy-start(bf16[192,192]{1,0:T(8,128)(2,1)} %w_out.4) | copy-start | bytes 221188
  5.5 10.3 %copy-start.14 = (f32[6,15,15]{2,1,0:T(8,128)S(1)}, f32[6,15,15]{2,1,0:T(8,128)}, u32[]{:S(2)}) copy-start(f32[6,15,15]{2,1,0:T(8,128)} %table.4) | copy-start | bytes 16204
  5.5 10.3 %copy-start.16 = (bf16[3,3,768]{2,1,0:T(4,128)(2,1)S(1)}, bf16[3,3,768]{2,1,0:T(4,128)(2,1)}, u32[]{:S(2)}) copy-start(bf16[3,3,768]{2,1,0:T(4,128)(2,1)} %taps.3) | copy-start | bytes 41476
  5.5 5.8 %collective-permute-start = (bf16[32,192]{1,0:T(8,128)(2,1)S(1)}, bf16[32,192]{1,0:T(8,128)(2,1)S(1)}, u32[]{:S(2)}, u32[]{:S(2)}) collective-permute-start(bf16[32,192]{1,0:T(8,128)(2,1)S(1)} %get-tuple-element.16), channel_id=1, source_target_pairs={{0,1},{1,2},{2,3},{4,5},{5,6},{6,7},{8,9},{9,10},{10,11},{12,13},{... | collective-permute-start | bytes 36872 | tf_op jit(solution)/shard_map/ppermute | solution.py:475
  10.4 5.3 %copy-start.2 = (bf16[32,192]{1,0:T(8,128)(2,1)}, bf16[32,192]{1,0:T(8,128)(2,1)S(1)}, u32[]{:S(2)}) copy-start(bf16[32,192]{1,0:T(8,128)(2,1)S(1)} %collective-permute-done.1.right) | copy-start | bytes 36868
  11.2 4.4 %copy-start.3 = (bf16[32,192]{1,0:T(8,128)(2,1)}, bf16[32,192]{1,0:T(8,128)(2,1)S(1)}, u32[]{:S(2)}) copy-start(bf16[32,192]{1,0:T(8,128)(2,1)S(1)} %collective-permute-done.left) | copy-start | bytes 36868
  11.3 21.1 %collective-permute-start.2 = (bf16[256,128]{1,0:T(8,128)(2,1)S(1)}, bf16[256,128]{1,0:T(8,128)(2,1)S(1)}, u32[]{:S(2)}, u32[]{:S(2)}) collective-permute-start(bf16[256,128]{1,0:T(8,128)(2,1)S(1)} %get-tuple-element.10.top), channel_id=1, source_target_pairs={{0,4},{4,8},{8,12},{12,16},{16,20},{20,24},{24,28},{28,32},{32,36}... | collective-permute-start | bytes 196616 | tf_op jit(solution)/shard_map/ppermute | solution.py:475
  14.4 18.1 %collective-permute-start.3 = (bf16[256,128]{1,0:T(8,128)(2,1)S(1)}, bf16[256,128]{1,0:T(8,128)(2,1)S(1)}, u32[]{:S(2)}, u32[]{:S(2)}) collective-permute-start(bf16[256,128]{1,0:T(8,128)(2,1)S(1)} %get-tuple-element.11.bottom), channel_id=1, source_target_pairs={{4,0},{8,4},{12,8},{16,12},{20,16},{24,20},{28,24},{32,28},{36,32}... | collective-permute-start | bytes 196616 | tf_op jit(solution)/shard_map/ppermute | solution.py:475
  32.5 14.0 %copy-start.17 = (bf16[256,128]{1,0:T(8,128)(2,1)}, bf16[256,128]{1,0:T(8,128)(2,1)S(1)}, u32[]{:S(2)}) copy-start(bf16[256,128]{1,0:T(8,128)(2,1)S(1)} %collective-permute-done.2.top) | copy-start | bytes 196612
  32.5 14.0 %copy-start.18 = (bf16[256,128]{1,0:T(8,128)(2,1)}, bf16[256,128]{1,0:T(8,128)(2,1)S(1)}, u32[]{:S(2)}) copy-start(bf16[256,128]{1,0:T(8,128)(2,1)S(1)} %collective-permute-done.3.bottom) | copy-start | bytes 196612
  32.5 32.1 %all-to-all-start = ((bf16[32,2,48,128]{3,2,1,0:T(8,128)(2,1)}), bf16[32,2,48,128]{3,2,1,0:T(8,128)(2,1)S(1)}, u32[]{:S(2)}, u32[]{:S(2)}) async-start(bf16[32,2,48,128]{3,2,1,0:T(8,128)(2,1)} %first.2), calls=%async_computation | async-start | bytes 1572864 | tf_op jit(solution)/shard_map/all_to_all | solution.py:498
  64.6 26.9 %copy-start.11 = (bf16[192,576]{1,0:T(8,128)(2,1)S(1)}, bf16[192,576]{1,0:T(8,128)(2,1)}, u32[]{:S(2)}) copy-start(bf16[192,576]{1,0:T(8,128)(2,1)} %w_qkv.5) | copy-start | bytes 663556
  64.6 26.9 %copy-start.13 = (bf16[192,192]{1,0:T(8,128)(2,1)S(1)}, bf16[192,192]{1,0:T(8,128)(2,1)}, u32[]{:S(2)}) copy-start(bf16[192,192]{1,0:T(8,128)(2,1)} %w_out.5) | copy-start | bytes 221188
  64.6 26.9 %copy-start.15 = (f32[6,15,15]{2,1,0:T(8,128)S(1)}, f32[6,15,15]{2,1,0:T(8,128)}, u32[]{:S(2)}) copy-start(f32[6,15,15]{2,1,0:T(8,128)} %table.5) | copy-start | bytes 16204
  101.9 28.8 %copy-start.8 = (bf16[192,768]{1,0:T(8,128)(2,1)S(1)}, bf16[192,768]{1,0:T(8,128)(2,1)}, u32[]{:S(2)}) copy-start(bf16[192,768]{1,0:T(8,128)(2,1)} %w_in.5) | copy-start | bytes 884740
  101.9 28.8 %copy-start.9 = (bf16[192,768]{1,0:T(8,128)(2,1)S(1)}, bf16[192,768]{1,0:T(8,128)(2,1)}, u32[]{:S(2)}) copy-start(bf16[192,768]{1,0:T(8,128)(2,1)} %w_back.5) | copy-start | bytes 884740

commit v4 on v3

--- a/solution.py
+++ b/solution.py
@@ -256,24 +256,18 @@
         ).astype(BF16)
 
 
-def grid_kernel(
-    one, two, w_qkv, w_out, table, out, lo, hi, wq_t, wk, wv_t, w_out_t, bias, padded
-):
-    step = pl.program_id(0)
-
-    @pl.when(step == 0)
+def grid_kernel(inp, w_qkv, w_out, table, *rest):
+    out, lo, hi, wq_t, wk, wv_t, w_out_t, bias, padded = rest[-9:]
+
+    @pl.when(pl.program_id(0) == 0)
     def _():
         prepare(w_qkv, w_out, table, wq_t, wk, wv_t, w_out_t, bias, padded)
 
-    def unpack(inp):
-        for src in range(32):
-            lo[32 * src : 32 * src + 32, :] = inp[src, 0, 0:32, :].astype(F32)
-            both = inp[src, 0, 32:48, :].astype(F32)
-            hi[32 * src : 32 * src + 16, :] = both
-            hi[32 * src + 16 : 32 * src + 32, :] = pltpu.roll(both, 64, 1)
-
-    pl.when(step < 2)(lambda: unpack(one))
-    pl.when(step >= 2)(lambda: unpack(two))
+    for src in range(32):
+        lo[32 * src : 32 * src + 32, :] = inp[src, 0, 0:32, :].astype(F32)
+        both = inp[src, 0, 32:48, :].astype(F32)
+        hi[32 * src : 32 * src + 16, :] = both
+        hi[32 * src + 16 : 32 * src + 32, :] = pltpu.roll(both, 64, 1)
     s = gather_groups(lo, hi)
     s = attend(s, wq_t[...], wk[...], wv_t[...], w_out_t[...], bias).T
     for g in range(TILES):
@@ -424,29 +418,32 @@
     )(image, image, image, *small)
 
 
-def call_grid(one, two, weights):
-    chunks = one.shape[1] + two.shape[1]
+def call_grid(base, total, arrived, weights, earlier):
+    chunks = arrived.shape[1]
     tokens = chunks * CHUNK
-    shape = (32, 1, 48, 128)
+    operands = [arrived] + weights
+    specs = [BLOCK] + [whole(a.shape) for a in weights]
+    aliases = {}
+    if earlier is not None:
+        aliases = {len(operands): 0}
+        operands.append(earlier)
+        specs.append(pl.BlockSpec(memory_space=pl.ANY))
     return pl.pallas_call(
         grid_kernel,
         grid=(chunks,),
-        in_specs=[
-            pl.BlockSpec(shape, lambda k: (0, jnp.minimum(k, 1), 0, 0)),
-            pl.BlockSpec(shape, lambda k: (0, jnp.maximum(k - 2, 0), 0, 0)),
-        ]
-        + [whole(a.shape) for a in weights],
-        out_specs=BLOCK,
-        out_shape=jax.ShapeDtypeStruct((32, chunks, 48, 128), BF16),
+        in_specs=specs,
+        out_specs=pl.BlockSpec((32, 1, 48, 128), lambda k: (0, base + k, 0, 0)),
+        out_shape=jax.ShapeDtypeStruct((32, total, 48, 128), BF16),
         scratch_shapes=[pltpu.VMEM((CHUNK, 128), F32), pltpu.VMEM((CHUNK, 128), F32)]
         + ATTEND_SCRATCH
         + [pltpu.VMEM((TOKENS, HEADS * TOKENS), F32), pltpu.VMEM((HEADS, 16, 128), F32)],
+        input_output_aliases=aliases,
         compiler_params=vm(48),
         cost_estimate=pl.CostEstimate(
             flops=tokens * 1000000, bytes_accessed=tokens * 800, transcendentals=tokens * 400
         ),
         name="grid",
-    )(one, two, *weights)
+    )(*operands)
 
 
 def call_last(returned, w_in, w_back):
@@ -498,7 +495,9 @@
     one = lax.all_to_all(inner, GROUP, 0, 0, tiled=True)
     outer = call_first(True, image, [top, bottom, left, right], weights)
     two = lax.all_to_all(outer, GROUP, 0, 0, tiled=True)
-    mixed = call_grid(one, two, [grid_qkv, grid_out, grid_bias])
+    weights = [grid_qkv, grid_out, grid_bias]
+    mixed = call_grid(0, 4, one, weights, None)
+    mixed = call_grid(2, 4, two, weights, mixed)
     back = lax.all_to_all(mixed, GROUP, 0, 0, tiled=True)
     return call_last(back, mlp2_in, mlp2_out)
 

time: 137 us -> 132 us (0.964)
  blocking collectives: 55.7 us -> 28.8 us
  waiting for transfers between devices: 0.84 us -> 12.4 us
  starting transfers between devices: 26.5 us -> 36.5 us
    all_to_all x1 -> x0, blocking collectives: 26.9 us -> none  [body(): two = lax.all_to_all(outer, GROUP, 0, 0, tiled=True)]
    all_to_all x0 -> x1, waiting for transfers between devices: none -> 11.6 us  [body(): two = lax.all_to_all(outer, GROUP, 0, 0, tiled=True)]
    all_to_all x0 -> x1, starting transfers between devices: none -> 9.95 us  [body(): two = lax.all_to_all(outer, GROUP, 0, 0, tiled=True)]
    pallas_call x1 -> x2, Pallas kernels: 10.4 us -> 10.6 us  [call_grid(): pl.pallas_call(grid_kernel, grid=(chunks,), in_specs=specs, out_specs=pl....]
  transfers between devices with their start and end apart: 5 -> 6, of which waited for: 1 -> 2; matrix products, arithmetic and copies ran while one was open for 0% -> 0% of each run, Pallas kernels for 25% -> 30%
where the time goes in v4:
time: 132 us
  Pallas kernels  52 us (39%)
  starting transfers between devices  36.5 us (28%)
  blocking collectives  28.8 us (22%)
  waiting for transfers between devices  12.4 us (9%)
  local copies, waits for them, and re-layouts  1.51 us (1%)
    pallas_call x2, Pallas kernels, call_first(): pl.pallas_call(functools.partial(first_kernel, edge), grid=(chunks,), in_...  34.7 us
    all_to_all x1, blocking collectives, body(): back = lax.all_to_all(mixed, GROUP, 0, 0, tiled=True)  28.8 us
    all_to_all x1, starting transfers between devices, body(): one = lax.all_to_all(inner, GROUP, 0, 0, tiled=True)  14 us
    ppermute x4, starting transfers between devices, shift(): return lax.ppermute(x, axis, pairs)  12.6 us
    all_to_all x1, waiting for transfers between devices, body(): two = lax.all_to_all(outer, GROUP, 0, 0, tiled=True)  11.6 us
    pallas_call x2, Pallas kernels, call_grid(): pl.pallas_call(grid_kernel, grid=(chunks,), in_specs=specs, out_specs=pl....  10.6 us
    all_to_all x1, starting transfers between devices, body(): two = lax.all_to_all(outer, GROUP, 0, 0, tiled=True)  9.95 us
    pallas_call x1, Pallas kernels, call_last(): pl.pallas_call(last_kernel, grid=(chunks,), in_specs=[BLOCK, whole(w_in.s...  5.9 us
  transfers between devices with their start and end apart: 6, of which 2 were waited for; matrix products, arithmetic and copies ran while one was open for 0% of the time, Pallas kernels for 30%

profile of v4, /device:TPU:1, one launch (start us, length us, event | category | flops | bytes accessed | tf_op | source)
XLA Modules:
  0.0 131.5 jit_solution(5532056419947142153)
XLA Ops:
  0.0 1.4 %copy-done = bf16[32,192,128]{2,1,0:T(8,128)(2,1)S(1)} copy-done((bf16[32,192,128]{2,1,0:T(8,128)(2,1)S(1)}, bf16[32,192,128]{2,1,0:T(8,128)(2,1)}, u32[]{:S(2)}) %copy-start) | copy-done | bytes 1572888
  1.4 0.6 edge.1
  2.0 3.3 %collective-permute-start.1 = (bf16[32,192]{1,0:T(8,128)(2,1)S(1)}, bf16[32,192]{1,0:T(8,128)(2,1)S(1)}, u32[]{:S(2)}, u32[]{:S(2)}) collective-permute-start(bf16[32,192]{1,0:T(8,128)(2,1)S(1)} %get-tuple-element.15), channel_id=1, source_target_pairs={{1,0},{2,1},{3,2},{5,4},{6,5},{7,6},{9,8},{10,9},{11,10},{13,12},{... | collective-permute-start | bytes 36872 | tf_op jit(solution)/shard_map/ppermute | solution.py:472
  5.4 0.0 copy-start.1
  5.4 0.0 copy-start.4
  5.4 0.0 copy-start.5
  5.4 0.0 copy-start.6
  5.4 0.0 copy-start.7
  5.4 0.0 copy-start.10
  5.4 0.0 copy-start.12
  5.5 0.0 copy-start.14
  5.5 0.0 copy-start.16
  5.5 4.9 %collective-permute-start = (bf16[32,192]{1,0:T(8,128)(2,1)S(1)}, bf16[32,192]{1,0:T(8,128)(2,1)S(1)}, u32[]{:S(2)}, u32[]{:S(2)}) collective-permute-start(bf16[32,192]{1,0:T(8,128)(2,1)S(1)} %get-tuple-element.16), channel_id=1, source_target_pairs={{0,1},{1,2},{2,3},{4,5},{5,6},{6,7},{8,9},{9,10},{10,11},{12,13},{... | collective-permute-start | bytes 36872 | tf_op jit(solution)/shard_map/ppermute | solution.py:472
  10.4 0.8 collective-permute-done.left
  11.2 0.1 pack.1
  11.3 3.0 %collective-permute-start.2 = (bf16[256,128]{1,0:T(8,128)(2,1)S(1)}, bf16[256,128]{1,0:T(8,128)(2,1)S(1)}, u32[]{:S(2)}, u32[]{:S(2)}) collective-permute-start(bf16[256,128]{1,0:T(8,128)(2,1)S(1)} %get-tuple-element.10.top), channel_id=1, source_target_pairs={{0,4},{4,8},{8,12},{12,16},{16,20},{20,24},{24,28},{28,32},{32,36}... | collective-permute-start | bytes 196616 | tf_op jit(solution)/shard_map/ppermute | solution.py:472
  14.4 1.3 collective-permute-start.3
  15.8 16.7 %first.2 = bf16[32,2,48,128]{3,2,1,0:T(8,128)(2,1)} custom-call(bf16[32,192,128]{2,1,0:T(8,128)(2,1)S(1)} %copy-done.1, bf16[32,192,128]{2,1,0:T(8,128)(2,1)S(1)} %copy-done.1, bf16[32,192,128]{2,1,0:T(8,128)(2,1)S(1)} %copy-done.1, bf16[256,128]{1,0:T(8,128)(2,1)S(1)} %get-tuple-element.10.top, bf16[256,128]{1,0:T(8,128)(2,1)S(1)} %get-tuple-element.11.bottom, ...), custom_call_target="tpu_custom_call" | custom-call | flops 4096000000 | bytes 1638400 | tf_op jit(solution)/shard_map/first/pallas_call | solution.py:391
  32.5 0.0 collective-permute-done.3.bottom
  32.5 14.0 %all-to-all-start.1 = ((bf16[32,2,48,128]{3,2,1,0:T(8,128)(2,1)}), bf16[32,2,48,128]{3,2,1,0:T(8,128)(2,1)S(1)}, u32[]{:S(2)}, u32[]{:S(2)}) async-start(bf16[32,2,48,128]{3,2,1,0:T(8,128)(2,1)} %first.2), calls=%async_computation.1 | async-start | bytes 1572864 | tf_op jit(solution)/shard_map/all_to_all | solution.py:495
  46.5 18.0 %first.3 = bf16[32,2,48,128]{3,2,1,0:T(8,128)(2,1)} custom-call(bf16[32,192,128]{2,1,0:T(8,128)(2,1)} %after.3, bf16[32,192,128]{2,1,0:T(8,128)(2,1)} %after.3, bf16[32,192,128]{2,1,0:T(8,128)(2,1)} %after.3, bf16[256,128]{1,0:T(8,128)(2,1)} %copy-done.17, bf16[256,128]{1,0:T(8,128)(2,1)} %copy-done.18, bf16[32,192]{1,0:T(8,128)(2,1)} %copy-done.3, ...), custom_call_target="tpu_custom_call" | custom-call | flops 4096000000 | bytes 1638400 | tf_op jit(solution)/shard_map/first/pallas_call | solution.py:391
  64.5 0.0 copy-start.13
  64.6 0.0 copy-start.15
  64.6 0.0 all-to-all-done.1.inp
  64.6 10.0 %all-to-all-start = ((bf16[32,2,48,128]{3,2,1,0:T(8,128)(2,1)}), bf16[32,2,48,128]{3,2,1,0:T(8,128)(2,1)S(1)}, u32[]{:S(2)}, u32[]{:S(2)}) async-start(bf16[32,2,48,128]{3,2,1,0:T(8,128)(2,1)} %first.3), calls=%async_computation | async-start | bytes 1572864 | tf_op jit(solution)/shard_map/all_to_all | solution.py:497
  74.6 5.3 %grid.2.rest_0_ = bf16[32,4,48,128]{3,2,1,0:T(8,128)(2,1)S(1)} custom-call(bf16[32,2,48,128]{3,2,1,0:T(8,128)(2,1)S(1)} %all-to-all-done.1.inp, bf16[192,576]{1,0:T(8,128)(2,1)S(1)} %copy-done.11, bf16[192,192]{1,0:T(8,128)(2,1)S(1)} %copy-done.13, f32[6,15,15]{2,1,0:T(8,128)S(1)} %copy-done.15), custom_call_target="tpu_custom_call" | custom-call | flops 2048000000 | bytes 1638400 | tf_op jit(solution)/shard_map/grid/pallas_call | solution.py:431
  79.9 11.6 %all-to-all-done.inp = bf16[32,2,48,128]{3,2,1,0:T(8,128)(2,1)S(1)} async-done(((bf16[32,2,48,128]{3,2,1,0:T(8,128)(2,1)}), bf16[32,2,48,128]{3,2,1,0:T(8,128)(2,1)S(1)}, u32[]{:S(2)}, u32[]{:S(2)}) %all-to-all-start) | async-done | bytes 786464 | tf_op jit(solution)/shard_map/all_to_all | solution.py:497
  91.5 5.3 %grid.3 = bf16[32,4,48,128]{3,2,1,0:T(8,128)(2,1)S(1)} custom-call(bf16[32,2,48,128]{3,2,1,0:T(8,128)(2,1)S(1)} %all-to-all-done.inp, bf16[192,576]{1,0:T(8,128)(2,1)S(1)} %copy-done.11, bf16[192,192]{1,0:T(8,128)(2,1)S(1)} %copy-done.13, f32[6,15,15]{2,1,0:T(8,128)S(1)} %copy-done.15, ...), custom_call_target="tpu_custom_call", output_to_operand_aliasing={{}: (4, {})} | custom-call | flops 2048000000 | bytes 1638400 | tf_op jit(solution)/shard_map/grid/pallas_call | solution.py:431
  96.8 0.0 copy-start.8
  96.8 0.0 copy-start.9
  96.8 28.8 %all_to_all.15.inp = bf16[32,4,48,128]{3,2,1,0:T(8,128)(2,1)S(1)} all-to-all(bf16[32,4,48,128]{3,2,1,0:T(8,128)(2,1)S(1)} %grid.3), channel_id=1, replica_groups=mesh['y'=4,'zh'=2,'zl'=2,'xl'=2,'xh'=2,'core'=2] {'y','zh','xh','core'}, dimensions={0} | all-to-all | bytes 3145728 | tf_op jit(solution)/shard_map/all_to_all | solution.py:501
  125.7 5.9 %last.1 = bf16[32,192,128]{2,1,0:T(8,128)(2,1)} custom-call(bf16[32,4,48,128]{3,2,1,0:T(8,128)(2,1)S(1)} %all_to_all.15.inp, bf16[192,768]{1,0:T(8,128)(2,1)S(1)} %copy-done.8, bf16[192,768]{1,0:T(8,128)(2,1)S(1)} %copy-done.9), custom_call_target="tpu_custom_call" | custom-call | flops 4096000000 | bytes 3276800 | tf_op jit(solution)/shard_map/last/pallas_call | solution.py:452
  (27 shorter events, 0.1 us)
Async XLA Ops:
  0.0 1.4 %copy-start = (bf16[32,192,128]{2,1,0:T(8,128)(2,1)S(1)}, bf16[32,192,128]{2,1,0:T(8,128)(2,1)}, u32[]{:S(2)}) copy-start(bf16[32,192,128]{2,1,0:T(8,128)(2,1)} %after.3) | copy-start | bytes 4718596
  2.0 8.4 %collective-permute-start.1 = (bf16[32,192]{1,0:T(8,128)(2,1)S(1)}, bf16[32,192]{1,0:T(8,128)(2,1)S(1)}, u32[]{:S(2)}, u32[]{:S(2)}) collective-permute-start(bf16[32,192]{1,0:T(8,128)(2,1)S(1)} %get-tuple-element.15), channel_id=1, source_target_pairs={{1,0},{2,1},{3,2},{5,4},{6,5},{7,6},{9,8},{10,9},{11,10},{13,12},{... | collective-permute-start | bytes 36872 | tf_op jit(solution)/shard_map/ppermute | solution.py:472
  5.4 10.3 %copy-start.1 = (bf16[32,192,128]{2,1,0:T(8,128)(2,1)S(1)}, bf16[32,192,128]{2,1,0:T(8,128)(2,1)}, u32[]{:S(2)}) copy-start(bf16[32,192,128]{2,1,0:T(8,128)(2,1)} %after.3) | copy-start | bytes 4718596
  5.4 10.3 %copy-start.4 = (bf16[192,768]{1,0:T(8,128)(2,1)S(1)}, bf16[192,768]{1,0:T(8,128)(2,1)}, u32[]{:S(2)}) copy-start(bf16[192,768]{1,0:T(8,128)(2,1)} %w_expand.3) | copy-start | bytes 884740
  5.4 10.3 %copy-start.5 = (bf16[192,768]{1,0:T(8,128)(2,1)S(1)}, bf16[192,768]{1,0:T(8,128)(2,1)}, u32[]{:S(2)}) copy-start(bf16[192,768]{1,0:T(8,128)(2,1)} %w_project.3) | copy-start | bytes 884740
  5.4 10.3 %copy-start.6 = (bf16[192,768]{1,0:T(8,128)(2,1)S(1)}, bf16[192,768]{1,0:T(8,128)(2,1)}, u32[]{:S(2)}) copy-start(bf16[192,768]{1,0:T(8,128)(2,1)} %w_in.4) | copy-start | bytes 884740
  5.4 10.3 %copy-start.7 = (bf16[192,768]{1,0:T(8,128)(2,1)S(1)}, bf16[192,768]{1,0:T(8,128)(2,1)}, u32[]{:S(2)}) copy-start(bf16[192,768]{1,0:T(8,128)(2,1)} %w_back.4) | copy-start | bytes 884740
  5.4 10.3 %copy-start.10 = (bf16[192,576]{1,0:T(8,128)(2,1)S(1)}, bf16[192,576]{1,0:T(8,128)(2,1)}, u32[]{:S(2)}) copy-start(bf16[192,576]{1,0:T(8,128)(2,1)} %w_qkv.5) | copy-start | bytes 663556
  5.4 10.3 %copy-start.12 = (bf16[192,192]{1,0:T(8,128)(2,1)S(1)}, bf16[192,192]{1,0:T(8,128)(2,1)}, u32[]{:S(2)}) copy-start(bf16[192,192]{1,0:T(8,128)(2,1)} %w_out.5) | copy-start | bytes 221188
  5.5 10.3 %copy-start.14 = (f32[6,15,15]{2,1,0:T(8,128)S(1)}, f32[6,15,15]{2,1,0:T(8,128)}, u32[]{:S(2)}) copy-start(f32[6,15,15]{2,1,0:T(8,128)} %table.5) | copy-start | bytes 16204
  5.5 10.3 %copy-start.16 = (bf16[3,3,768]{2,1,0:T(4,128)(2,1)S(1)}, bf16[3,3,768]{2,1,0:T(4,128)(2,1)}, u32[]{:S(2)}) copy-start(bf16[3,3,768]{2,1,0:T(4,128)(2,1)} %taps.3) | copy-start | bytes 41476
  5.5 5.8 %collective-permute-start = (bf16[32,192]{1,0:T(8,128)(2,1)S(1)}, bf16[32,192]{1,0:T(8,128)(2,1)S(1)}, u32[]{:S(2)}, u32[]{:S(2)}) collective-permute-start(bf16[32,192]{1,0:T(8,128)(2,1)S(1)} %get-tuple-element.16), channel_id=1, source_target_pairs={{0,1},{1,2},{2,3},{4,5},{5,6},{6,7},{8,9},{9,10},{10,11},{12,13},{... | collective-permute-start | bytes 36872 | tf_op jit(solution)/shard_map/ppermute | solution.py:472
  10.4 5.3 %copy-start.2 = (bf16[32,192]{1,0:T(8,128)(2,1)}, bf16[32,192]{1,0:T(8,128)(2,1)S(1)}, u32[]{:S(2)}) copy-start(bf16[32,192]{1,0:T(8,128)(2,1)S(1)} %collective-permute-done.1.right) | copy-start | bytes 36868
  11.2 4.4 %copy-start.3 = (bf16[32,192]{1,0:T(8,128)(2,1)}, bf16[32,192]{1,0:T(8,128)(2,1)S(1)}, u32[]{:S(2)}) copy-start(bf16[32,192]{1,0:T(8,128)(2,1)S(1)} %collective-permute-done.left) | copy-start | bytes 36868
  11.3 21.2 %collective-permute-start.2 = (bf16[256,128]{1,0:T(8,128)(2,1)S(1)}, bf16[256,128]{1,0:T(8,128)(2,1)S(1)}, u32[]{:S(2)}, u32[]{:S(2)}) collective-permute-start(bf16[256,128]{1,0:T(8,128)(2,1)S(1)} %get-tuple-element.10.top), channel_id=1, source_target_pairs={{0,4},{4,8},{8,12},{12,16},{16,20},{20,24},{24,28},{28,32},{32,36}... | collective-permute-start | bytes 196616 | tf_op jit(solution)/shard_map/ppermute | solution.py:472
  14.4 18.1 %collective-permute-start.3 = (bf16[256,128]{1,0:T(8,128)(2,1)S(1)}, bf16[256,128]{1,0:T(8,128)(2,1)S(1)}, u32[]{:S(2)}, u32[]{:S(2)}) collective-permute-start(bf16[256,128]{1,0:T(8,128)(2,1)S(1)} %get-tuple-element.11.bottom), channel_id=1, source_target_pairs={{4,0},{8,4},{12,8},{16,12},{20,16},{24,20},{28,24},{32,28},{36,32}... | collective-permute-start | bytes 196616 | tf_op jit(solution)/shard_map/ppermute | solution.py:472
  32.5 14.0 %copy-start.17 = (bf16[256,128]{1,0:T(8,128)(2,1)}, bf16[256,128]{1,0:T(8,128)(2,1)S(1)}, u32[]{:S(2)}) copy-start(bf16[256,128]{1,0:T(8,128)(2,1)S(1)} %collective-permute-done.2.top) | copy-start | bytes 196612
  32.5 14.0 %copy-start.18 = (bf16[256,128]{1,0:T(8,128)(2,1)}, bf16[256,128]{1,0:T(8,128)(2,1)S(1)}, u32[]{:S(2)}) copy-start(bf16[256,128]{1,0:T(8,128)(2,1)S(1)} %collective-permute-done.3.bottom) | copy-start | bytes 196612
  32.5 32.1 %all-to-all-start.1 = ((bf16[32,2,48,128]{3,2,1,0:T(8,128)(2,1)}), bf16[32,2,48,128]{3,2,1,0:T(8,128)(2,1)S(1)}, u32[]{:S(2)}, u32[]{:S(2)}) async-start(bf16[32,2,48,128]{3,2,1,0:T(8,128)(2,1)} %first.2), calls=%async_computation.1 | async-start | bytes 1572864 | tf_op jit(solution)/shard_map/all_to_all | solution.py:495
  64.5 10.0 %copy-start.11 = (bf16[192,576]{1,0:T(8,128)(2,1)S(1)}, bf16[192,576]{1,0:T(8,128)(2,1)}, u32[]{:S(2)}) copy-start(bf16[192,576]{1,0:T(8,128)(2,1)} %w_qkv.7) | copy-start | bytes 663556
  64.5 10.0 %copy-start.13 = (bf16[192,192]{1,0:T(8,128)(2,1)S(1)}, bf16[192,192]{1,0:T(8,128)(2,1)}, u32[]{:S(2)}) copy-start(bf16[192,192]{1,0:T(8,128)(2,1)} %w_out.7) | copy-start | bytes 221188
  64.6 10.0 %copy-start.15 = (f32[6,15,15]{2,1,0:T(8,128)S(1)}, f32[6,15,15]{2,1,0:T(8,128)}, u32[]{:S(2)}) copy-start(f32[6,15,15]{2,1,0:T(8,128)} %table.7) | copy-start | bytes 16204
  64.6 26.9 %all-to-all-start = ((bf16[32,2,48,128]{3,2,1,0:T(8,128)(2,1)}), bf16[32,2,48,128]{3,2,1,0:T(8,128)(2,1)S(1)}, u32[]{:S(2)}, u32[]{:S(2)}) async-start(bf16[32,2,48,128]{3,2,1,0:T(8,128)(2,1)} %first.3), calls=%async_computation | async-start | bytes 1572864 | tf_op jit(solution)/shard_map/all_to_all | solution.py:497
  96.8 28.8 %copy-start.8 = (bf16[192,768]{1,0:T(8,128)(2,1)S(1)}, bf16[192,768]{1,0:T(8,128)(2,1)}, u32[]{:S(2)}) copy-start(bf16[192,768]{1,0:T(8,128)(2,1)} %w_in.5) | copy-start | bytes 884740
  96.8 28.8 %copy-start.9 = (bf16[192,768]{1,0:T(8,128)(2,1)S(1)}, bf16[192,768]{1,0:T(8,128)(2,1)}, u32[]{:S(2)}) copy-start(bf16[192,768]{1,0:T(8,128)(2,1)} %w_back.5) | copy-start | bytes 884740

commit v5 on v4

--- a/solution.py
+++ b/solution.py
@@ -482,8 +482,14 @@
     grid_qkv, grid_out, grid_bias, mlp2_in, mlp2_out,
 ):
     edges = call_edge(image)
-    left = shift(edges[1], COL_AXES, 4, 1)
-    right = shift(edges[0], COL_AXES, 4, -1)
+    here = lax.axis_index(COL_AXES)
+    place = lax.broadcasted_iota(jnp.int32, (4, 1, 1), 0)
+    none = jnp.zeros((), BF16)
+    out = jnp.where(place == here + 1, edges[1][None], none)
+    out = jnp.where(place == here - 1, edges[0][None], out)
+    got = lax.all_to_all(out, COL_AXES, 0, 0, tiled=True)
+    left = jnp.sum(jnp.where(place == here - 1, got, none), axis=0)
+    right = jnp.sum(jnp.where(place == here + 1, got, none), axis=0)
     down, up = call_pack(image, left, right)
     top = shift(down, ROW_AXES, 32, 1)
     bottom = shift(up, ROW_AXES, 32, -1)

time: 132 us -> 131 us (level)
  starting transfers between devices: 36.5 us -> 25.6 us
  blocking collectives: 28.8 us -> 39.2 us
    all_to_all x0 -> x1, blocking collectives: none -> 10.4 us  [body(): got = lax.all_to_all(out, COL_AXES, 0, 0, tiled=True)]
    ppermute x4 -> x2, starting transfers between devices: 12.6 us -> 3.63 us  [shift(): return lax.ppermute(x, axis, pairs)]
    all_to_all x1, starting transfers between devices: 14 us -> 12 us  [body(): one = lax.all_to_all(inner, GROUP, 0, 0, tiled=True)]
  transfers between devices with their start and end apart: 6 -> 4, of which waited for: 2 -> 1; matrix products, arithmetic and copies ran while one was open for 0% -> 0% of each run, Pallas kernels for 30% -> 31%
where the time goes in v5:
time: 131 us; the launch traced here: 130 us
  Pallas kernels  52 us (40%)
  blocking collectives  39.2 us (30%)
  starting transfers between devices  25.6 us (20%)
  waiting for transfers between devices  11.6 us (9%)
  local copies, waits for them, and re-layouts  1.51 us (1%)
    pallas_call x2, Pallas kernels, call_first(): pl.pallas_call(functools.partial(first_kernel, edge), grid=(chunks,), in_...  34.8 us
    all_to_all x1, blocking collectives, body(): back = lax.all_to_all(mixed, GROUP, 0, 0, tiled=True)  28.8 us
    all_to_all x1, starting transfers between devices, body(): one = lax.all_to_all(inner, GROUP, 0, 0, tiled=True)  12 us
    all_to_all x1, waiting for transfers between devices, body(): two = lax.all_to_all(outer, GROUP, 0, 0, tiled=True)  11.6 us
    pallas_call x2, Pallas kernels, call_grid(): pl.pallas_call(grid_kernel, grid=(chunks,), in_specs=specs, out_specs=pl....  10.6 us
    all_to_all x1, blocking collectives, body(): got = lax.all_to_all(out, COL_AXES, 0, 0, tiled=True)  10.4 us
    all_to_all x1, starting transfers between devices, body(): two = lax.all_to_all(outer, GROUP, 0, 0, tiled=True)  9.95 us
    pallas_call x1, Pallas kernels, call_last(): pl.pallas_call(last_kernel, grid=(chunks,), in_specs=[BLOCK, whole(w_in.s...  5.9 us
  transfers between devices with their start and end apart: 4, of which 1 were waited for; matrix products, arithmetic and copies ran while one was open for 0% of the time, Pallas kernels for 31%

profile of v5, /device:TPU:1, one launch (start us, length us, event | category | flops | bytes accessed | tf_op | source)
XLA Modules:
  0.0 130.4 jit_solution(12560186268533685646)
XLA Ops:
  0.0 1.4 %copy-done = bf16[32,192,128]{2,1,0:T(8,128)(2,1)S(1)} copy-done((bf16[32,192,128]{2,1,0:T(8,128)(2,1)S(1)}, bf16[32,192,128]{2,1,0:T(8,128)(2,1)}, u32[]{:S(2)}) %copy-start) | copy-done | bytes 1572888
  1.4 0.6 edge.1
  2.1 0.1 select_select_fusion
  2.1 10.4 %all_to_all.20 = bf16[4,32,192]{2,1,0:T(8,128)(2,1)S(1)} all-to-all(bf16[4,32,192]{2,1,0:T(8,128)(2,1)S(1)} %select_select_fusion), channel_id=1, replica_groups=mesh['y'=4,'zh'=2,'zl'=2,'xl'=2,'xh'=2,'core'=2] {'xh','core'}, dimensions={0} | all-to-all | bytes 98304 | tf_op jit(solution)/shard_map/all_to_all | solution.py:490
  12.5 0.1 select_reduce_fusion
  12.6 0.0 copy-start.1
  12.6 0.0 copy-start.4
  12.6 0.0 copy-start.5
  12.7 0.0 copy-start.6
  12.7 0.0 copy-start.7
  12.7 0.0 copy-start.10
  12.7 0.0 copy-start.12
  12.7 0.0 copy-start.14
  12.7 0.0 copy-start.16
  12.7 0.1 pack.1
  12.8 2.3 %collective-permute-start = (bf16[256,128]{1,0:T(8,128)(2,1)S(1)}, bf16[256,128]{1,0:T(8,128)(2,1)S(1)}, u32[]{:S(2)}, u32[]{:S(2)}) collective-permute-start(bf16[256,128]{1,0:T(8,128)(2,1)S(1)} %get-tuple-element.10.top), channel_id=1, source_target_pairs={{0,4},{4,8},{8,12},{12,16},{16,20},{20,24},{24,28},{28,32},{32,36}... | collective-permute-start | bytes 196616 | tf_op jit(solution)/shard_map/ppermute | solution.py:472
  15.2 1.3 collective-permute-start.1
  16.6 16.7 %first.2 = bf16[32,2,48,128]{3,2,1,0:T(8,128)(2,1)} custom-call(bf16[32,192,128]{2,1,0:T(8,128)(2,1)S(1)} %copy-done.1, bf16[32,192,128]{2,1,0:T(8,128)(2,1)S(1)} %copy-done.1, bf16[32,192,128]{2,1,0:T(8,128)(2,1)S(1)} %copy-done.1, bf16[256,128]{1,0:T(8,128)(2,1)S(1)} %get-tuple-element.10.top, bf16[256,128]{1,0:T(8,128)(2,1)S(1)} %get-tuple-element.11.bottom, ...), custom_call_target="tpu_custom_call" | custom-call | flops 4096000000 | bytes 1638400 | tf_op jit(solution)/shard_map/first/pallas_call | solution.py:391
  33.3 0.0 collective-permute-done.top
  33.3 12.0 %all-to-all-start.2 = ((bf16[32,2,48,128]{3,2,1,0:T(8,128)(2,1)}), bf16[32,2,48,128]{3,2,1,0:T(8,128)(2,1)S(1)}, u32[]{:S(2)}, u32[]{:S(2)}) async-start(bf16[32,2,48,128]{3,2,1,0:T(8,128)(2,1)} %first.2), calls=%async_computation.2 | async-start | bytes 1572864 | tf_op jit(solution)/shard_map/all_to_all | solution.py:501
  45.4 18.0 %first.3 = bf16[32,2,48,128]{3,2,1,0:T(8,128)(2,1)} custom-call(bf16[32,192,128]{2,1,0:T(8,128)(2,1)} %after.3, bf16[32,192,128]{2,1,0:T(8,128)(2,1)} %after.3, bf16[32,192,128]{2,1,0:T(8,128)(2,1)} %after.3, bf16[256,128]{1,0:T(8,128)(2,1)} %copy-done.17, bf16[256,128]{1,0:T(8,128)(2,1)} %copy-done.18, bf16[32,192]{1,0:T(8,128)(2,1)} %copy-done.3, ...), custom_call_target="tpu_custom_call" | custom-call | flops 4096000000 | bytes 1638400 | tf_op jit(solution)/shard_map/first/pallas_call | solution.py:391
  63.4 0.0 copy-start.13
  63.4 0.0 copy-start.15
  63.4 0.0 all-to-all-done.2.inp
  63.5 10.0 %all-to-all-start.1 = ((bf16[32,2,48,128]{3,2,1,0:T(8,128)(2,1)}), bf16[32,2,48,128]{3,2,1,0:T(8,128)(2,1)S(1)}, u32[]{:S(2)}, u32[]{:S(2)}) async-start(bf16[32,2,48,128]{3,2,1,0:T(8,128)(2,1)} %first.3), calls=%async_computation.1 | async-start | bytes 1572864 | tf_op jit(solution)/shard_map/all_to_all | solution.py:503
  73.4 5.3 %grid.2.rest_0_ = bf16[32,4,48,128]{3,2,1,0:T(8,128)(2,1)S(1)} custom-call(bf16[32,2,48,128]{3,2,1,0:T(8,128)(2,1)S(1)} %all-to-all-done.2.inp, bf16[192,576]{1,0:T(8,128)(2,1)S(1)} %copy-done.11, bf16[192,192]{1,0:T(8,128)(2,1)S(1)} %copy-done.13, f32[6,15,15]{2,1,0:T(8,128)S(1)} %copy-done.15), custom_call_target="tpu_custom_call" | custom-call | flops 2048000000 | bytes 1638400 | tf_op jit(solution)/shard_map/grid/pallas_call | solution.py:431
  78.8 11.6 %all-to-all-done.1.inp = bf16[32,2,48,128]{3,2,1,0:T(8,128)(2,1)S(1)} async-done(((bf16[32,2,48,128]{3,2,1,0:T(8,128)(2,1)}), bf16[32,2,48,128]{3,2,1,0:T(8,128)(2,1)S(1)}, u32[]{:S(2)}, u32[]{:S(2)}) %all-to-all-start.1) | async-done | bytes 786464 | tf_op jit(solution)/shard_map/all_to_all | solution.py:503
  90.4 5.3 %grid.3 = bf16[32,4,48,128]{3,2,1,0:T(8,128)(2,1)S(1)} custom-call(bf16[32,2,48,128]{3,2,1,0:T(8,128)(2,1)S(1)} %all-to-all-done.1.inp, bf16[192,576]{1,0:T(8,128)(2,1)S(1)} %copy-done.11, bf16[192,192]{1,0:T(8,128)(2,1)S(1)} %copy-done.13, f32[6,15,15]{2,1,0:T(8,128)S(1)} %copy-done.15, ...), custom_call_target="tpu_custom_call", output_to_operand_aliasing={{}: (4, {})} | custom-call | flops 2048000000 | bytes 1638400 | tf_op jit(solution)/shard_map/grid/pallas_call | solution.py:431
  95.7 0.0 copy-start.8
  95.7 0.0 copy-start.9
  95.7 28.8 %all_to_all.21.inp = bf16[32,4,48,128]{3,2,1,0:T(8,128)(2,1)S(1)} all-to-all(bf16[32,4,48,128]{3,2,1,0:T(8,128)(2,1)S(1)} %grid.3), channel_id=1, replica_groups=mesh['y'=4,'zh'=2,'zl'=2,'xl'=2,'xh'=2,'core'=2] {'y','zh','xh','core'}, dimensions={0} | all-to-all | bytes 3145728 | tf_op jit(solution)/shard_map/all_to_all | solution.py:507
  124.5 5.9 %last.1 = bf16[32,192,128]{2,1,0:T(8,128)(2,1)} custom-call(bf16[32,4,48,128]{3,2,1,0:T(8,128)(2,1)S(1)} %all_to_all.21.inp, bf16[192,768]{1,0:T(8,128)(2,1)S(1)} %copy-done.8, bf16[192,768]{1,0:T(8,128)(2,1)S(1)} %copy-done.9), custom_call_target="tpu_custom_call" | custom-call | flops 4096000000 | bytes 3276800 | tf_op jit(solution)/shard_map/last/pallas_call | solution.py:452
  (27 shorter events, 0.1 us)
Async XLA Ops:
  0.0 1.4 %copy-start = (bf16[32,192,128]{2,1,0:T(8,128)(2,1)S(1)}, bf16[32,192,128]{2,1,0:T(8,128)(2,1)}, u32[]{:S(2)}) copy-start(bf16[32,192,128]{2,1,0:T(8,128)(2,1)} %after.3) | copy-start | bytes 4718596
  12.6 3.9 %copy-start.2 = (bf16[32,192]{1,0:T(8,128)(2,1)}, bf16[32,192]{1,0:T(8,128)(2,1)S(1)}, u32[]{:S(2)}) copy-start(bf16[32,192]{1,0:T(8,128)(2,1)S(1)} %get-tuple-element.15.right) | copy-start | bytes 36868
  12.6 3.9 %copy-start.3 = (bf16[32,192]{1,0:T(8,128)(2,1)}, bf16[32,192]{1,0:T(8,128)(2,1)S(1)}, u32[]{:S(2)}) copy-start(bf16[32,192]{1,0:T(8,128)(2,1)S(1)} %get-tuple-element.16.left) | copy-start | bytes 36868
  12.6 3.9 %copy-start.1 = (bf16[32,192,128]{2,1,0:T(8,128)(2,1)S(1)}, bf16[32,192,128]{2,1,0:T(8,128)(2,1)}, u32[]{:S(2)}) copy-start(bf16[32,192,128]{2,1,0:T(8,128)(2,1)} %after.3) | copy-start | bytes 4718596
  12.6 3.9 %copy-start.4 = (bf16[192,768]{1,0:T(8,128)(2,1)S(1)}, bf16[192,768]{1,0:T(8,128)(2,1)}, u32[]{:S(2)}) copy-start(bf16[192,768]{1,0:T(8,128)(2,1)} %w_expand.3) | copy-start | bytes 884740
  12.6 3.9 %copy-start.5 = (bf16[192,768]{1,0:T(8,128)(2,1)S(1)}, bf16[192,768]{1,0:T(8,128)(2,1)}, u32[]{:S(2)}) copy-start(bf16[192,768]{1,0:T(8,128)(2,1)} %w_project.3) | copy-start | bytes 884740
  12.7 3.9 %copy-start.6 = (bf16[192,768]{1,0:T(8,128)(2,1)S(1)}, bf16[192,768]{1,0:T(8,128)(2,1)}, u32[]{:S(2)}) copy-start(bf16[192,768]{1,0:T(8,128)(2,1)} %w_in.4) | copy-start | bytes 884740
  12.7 3.9 %copy-start.7 = (bf16[192,768]{1,0:T(8,128)(2,1)S(1)}, bf16[192,768]{1,0:T(8,128)(2,1)}, u32[]{:S(2)}) copy-start(bf16[192,768]{1,0:T(8,128)(2,1)} %w_back.4) | copy-start | bytes 884740
  12.7 3.9 %copy-start.10 = (bf16[192,576]{1,0:T(8,128)(2,1)S(1)}, bf16[192,576]{1,0:T(8,128)(2,1)}, u32[]{:S(2)}) copy-start(bf16[192,576]{1,0:T(8,128)(2,1)} %w_qkv.5) | copy-start | bytes 663556
  12.7 3.8 %copy-start.12 = (bf16[192,192]{1,0:T(8,128)(2,1)S(1)}, bf16[192,192]{1,0:T(8,128)(2,1)}, u32[]{:S(2)}) copy-start(bf16[192,192]{1,0:T(8,128)(2,1)} %w_out.5) | copy-start | bytes 221188
  12.7 3.8 %copy-start.14 = (f32[6,15,15]{2,1,0:T(8,128)S(1)}, f32[6,15,15]{2,1,0:T(8,128)}, u32[]{:S(2)}) copy-start(f32[6,15,15]{2,1,0:T(8,128)} %table.5) | copy-start | bytes 16204
  12.7 3.8 %copy-start.16 = (bf16[3,3,768]{2,1,0:T(4,128)(2,1)S(1)}, bf16[3,3,768]{2,1,0:T(4,128)(2,1)}, u32[]{:S(2)}) copy-start(bf16[3,3,768]{2,1,0:T(4,128)(2,1)} %taps.3) | copy-start | bytes 41476
  12.8 20.5 %collective-permute-start = (bf16[256,128]{1,0:T(8,128)(2,1)S(1)}, bf16[256,128]{1,0:T(8,128)(2,1)S(1)}, u32[]{:S(2)}, u32[]{:S(2)}) collective-permute-start(bf16[256,128]{1,0:T(8,128)(2,1)S(1)} %get-tuple-element.10.top), channel_id=1, source_target_pairs={{0,4},{4,8},{8,12},{12,16},{16,20},{20,24},{24,28},{28,32},{32,36}... | collective-permute-start | bytes 196616 | tf_op jit(solution)/shard_map/ppermute | solution.py:472
  15.2 18.1 %collective-permute-start.1 = (bf16[256,128]{1,0:T(8,128)(2,1)S(1)}, bf16[256,128]{1,0:T(8,128)(2,1)S(1)}, u32[]{:S(2)}, u32[]{:S(2)}) collective-permute-start(bf16[256,128]{1,0:T(8,128)(2,1)S(1)} %get-tuple-element.11.bottom), channel_id=1, source_target_pairs={{4,0},{8,4},{12,8},{16,12},{20,16},{24,20},{28,24},{32,28},{36,32}... | collective-permute-start | bytes 196616 | tf_op jit(solution)/shard_map/ppermute | solution.py:472
  33.3 12.1 %copy-start.17 = (bf16[256,128]{1,0:T(8,128)(2,1)}, bf16[256,128]{1,0:T(8,128)(2,1)S(1)}, u32[]{:S(2)}) copy-start(bf16[256,128]{1,0:T(8,128)(2,1)S(1)} %collective-permute-done.top) | copy-start | bytes 196612
  33.3 12.1 %copy-start.18 = (bf16[256,128]{1,0:T(8,128)(2,1)}, bf16[256,128]{1,0:T(8,128)(2,1)S(1)}, u32[]{:S(2)}) copy-start(bf16[256,128]{1,0:T(8,128)(2,1)S(1)} %collective-permute-done.1.bottom) | copy-start | bytes 196612
  33.3 30.1 %all-to-all-start.2 = ((bf16[32,2,48,128]{3,2,1,0:T(8,128)(2,1)}), bf16[32,2,48,128]{3,2,1,0:T(8,128)(2,1)S(1)}, u32[]{:S(2)}, u32[]{:S(2)}) async-start(bf16[32,2,48,128]{3,2,1,0:T(8,128)(2,1)} %first.2), calls=%async_computation.2 | async-start | bytes 1572864 | tf_op jit(solution)/shard_map/all_to_all | solution.py:501
  63.4 10.0 %copy-start.11 = (bf16[192,576]{1,0:T(8,128)(2,1)S(1)}, bf16[192,576]{1,0:T(8,128)(2,1)}, u32[]{:S(2)}) copy-start(bf16[192,576]{1,0:T(8,128)(2,1)} %w_qkv.7) | copy-start | bytes 663556
  63.4 10.0 %copy-start.13 = (bf16[192,192]{1,0:T(8,128)(2,1)S(1)}, bf16[192,192]{1,0:T(8,128)(2,1)}, u32[]{:S(2)}) copy-start(bf16[192,192]{1,0:T(8,128)(2,1)} %w_out.7) | copy-start | bytes 221188
  63.4 10.0 %copy-start.15 = (f32[6,15,15]{2,1,0:T(8,128)S(1)}, f32[6,15,15]{2,1,0:T(8,128)}, u32[]{:S(2)}) copy-start(f32[6,15,15]{2,1,0:T(8,128)} %table.7) | copy-start | bytes 16204
  63.5 26.9 %all-to-all-start.1 = ((bf16[32,2,48,128]{3,2,1,0:T(8,128)(2,1)}), bf16[32,2,48,128]{3,2,1,0:T(8,128)(2,1)S(1)}, u32[]{:S(2)}, u32[]{:S(2)}) async-start(bf16[32,2,48,128]{3,2,1,0:T(8,128)(2,1)} %first.3), calls=%async_computation.1 | async-start | bytes 1572864 | tf_op jit(solution)/shard_map/all_to_all | solution.py:503
  95.7 28.8 %copy-start.8 = (bf16[192,768]{1,0:T(8,128)(2,1)S(1)}, bf16[192,768]{1,0:T(8,128)(2,1)}, u32[]{:S(2)}) copy-start(bf16[192,768]{1,0:T(8,128)(2,1)} %w_in.5) | copy-start | bytes 884740
  95.7 28.8 %copy-start.9 = (bf16[192,768]{1,0:T(8,128)(2,1)S(1)}, bf16[192,768]{1,0:T(8,128)(2,1)}, u32[]{:S(2)}) copy-start(bf16[192,768]{1,0:T(8,128)(2,1)} %w_back.5) | copy-start | bytes 884740

commit v6 on v5

--- a/solution.py
+++ b/solution.py
@@ -290,12 +290,12 @@
 
     rows = []
     for r in range(ROWS_CHUNK):
-        got = inp[4 * r : 4 * r + 4, 0].astype(F32)
+        got = inp[4 * r : 4 * r + 4, 0]
         both = got[:, 32:48].reshape(64, 128)
         for i in range(2):
             low = got[:, 16 * i : 16 * i + 16].reshape(64, 128)
             rows.append(jnp.concatenate([low, both[:, 64 * i : 64 * i + 64]], axis=1))
-    s = jnp.concatenate(rows, axis=0).T
+    s = jnp.concatenate(rows, axis=0).T.astype(F32)
     s = mlp(s, w_in_t[...], w_back[...]).astype(BF16)
     for r in range(ROWS_CHUNK):
         out[r] = s[:, COLS * r : COLS * (r + 1)]

time: 131 us -> 131 us (level)
  no operation moved by 1% of the time
where the time goes in v6:
time: 131 us; the launch traced here: 130 us
  Pallas kernels  51.9 us (40%)
  blocking collectives  39.2 us (30%)
  starting transfers between devices  25.6 us (20%)
  waiting for transfers between devices  11.6 us (9%)
  local copies, waits for them, and re-layouts  1.51 us (1%)
    pallas_call x2, Pallas kernels, call_first(): pl.pallas_call(functools.partial(first_kernel, edge), grid=(chunks,), in_...  34.8 us
    all_to_all x1, blocking collectives, body(): back = lax.all_to_all(mixed, GROUP, 0, 0, tiled=True)  28.8 us
    all_to_all x1, starting transfers between devices, body(): one = lax.all_to_all(inner, GROUP, 0, 0, tiled=True)  12 us
    all_to_all x1, waiting for transfers between devices, body(): two = lax.all_to_all(outer, GROUP, 0, 0, tiled=True)  11.6 us
    pallas_call x2, Pallas kernels, call_grid(): pl.pallas_call(grid_kernel, grid=(chunks,), in_specs=specs, out_specs=pl....  10.6 us
    all_to_all x1, blocking collectives, body(): got = lax.all_to_all(out, COL_AXES, 0, 0, tiled=True)  10.4 us
    all_to_all x1, starting transfers between devices, body(): two = lax.all_to_all(outer, GROUP, 0, 0, tiled=True)  9.95 us
    pallas_call x1, Pallas kernels, call_last(): pl.pallas_call(last_kernel, grid=(chunks,), in_specs=[BLOCK, whole(w_in.s...  5.8 us
  transfers between devices with their start and end apart: 4, of which 1 were waited for; matrix products, arithmetic and copies ran while one was open for 0% of the time, Pallas kernels for 31%

profile of v6, /device:TPU:1, one launch (start us, length us, event | category | flops | bytes accessed | tf_op | source)
XLA Modules:
  0.0 130.3 jit_solution(14342468065320597559)
XLA Ops:
  0.0 1.4 %copy-done = bf16[32,192,128]{2,1,0:T(8,128)(2,1)S(1)} copy-done((bf16[32,192,128]{2,1,0:T(8,128)(2,1)S(1)}, bf16[32,192,128]{2,1,0:T(8,128)(2,1)}, u32[]{:S(2)}) %copy-start) | copy-done | bytes 1572888
  1.4 0.6 edge.1
  2.1 0.1 select_select_fusion
  2.1 10.4 %all_to_all.20 = bf16[4,32,192]{2,1,0:T(8,128)(2,1)S(1)} all-to-all(bf16[4,32,192]{2,1,0:T(8,128)(2,1)S(1)} %select_select_fusion), channel_id=1, replica_groups=mesh['y'=4,'zh'=2,'zl'=2,'xl'=2,'xh'=2,'core'=2] {'xh','core'}, dimensions={0} | all-to-all | bytes 98304 | tf_op jit(solution)/shard_map/all_to_all | solution.py:490
  12.5 0.1 select_reduce_fusion
  12.6 0.0 copy-start.1
  12.6 0.0 copy-start.4
  12.6 0.0 copy-start.5
  12.7 0.0 copy-start.6
  12.7 0.0 copy-start.7
  12.7 0.0 copy-start.10
  12.7 0.0 copy-start.12
  12.7 0.0 copy-start.14
  12.7 0.0 copy-start.16
  12.7 0.1 pack.1
  12.8 2.3 %collective-permute-start = (bf16[256,128]{1,0:T(8,128)(2,1)S(1)}, bf16[256,128]{1,0:T(8,128)(2,1)S(1)}, u32[]{:S(2)}, u32[]{:S(2)}) collective-permute-start(bf16[256,128]{1,0:T(8,128)(2,1)S(1)} %get-tuple-element.10.top), channel_id=1, source_target_pairs={{0,4},{4,8},{8,12},{12,16},{16,20},{20,24},{24,28},{28,32},{32,36}... | collective-permute-start | bytes 196616 | tf_op jit(solution)/shard_map/ppermute | solution.py:472
  15.2 1.3 collective-permute-start.1
  16.6 16.7 %first.2 = bf16[32,2,48,128]{3,2,1,0:T(8,128)(2,1)} custom-call(bf16[32,192,128]{2,1,0:T(8,128)(2,1)S(1)} %copy-done.1, bf16[32,192,128]{2,1,0:T(8,128)(2,1)S(1)} %copy-done.1, bf16[32,192,128]{2,1,0:T(8,128)(2,1)S(1)} %copy-done.1, bf16[256,128]{1,0:T(8,128)(2,1)S(1)} %get-tuple-element.10.top, bf16[256,128]{1,0:T(8,128)(2,1)S(1)} %get-tuple-element.11.bottom, ...), custom_call_target="tpu_custom_call" | custom-call | flops 4096000000 | bytes 1638400 | tf_op jit(solution)/shard_map/first/pallas_call | solution.py:391
  33.3 0.0 collective-permute-done.top
  33.3 12.0 %all-to-all-start.2 = ((bf16[32,2,48,128]{3,2,1,0:T(8,128)(2,1)}), bf16[32,2,48,128]{3,2,1,0:T(8,128)(2,1)S(1)}, u32[]{:S(2)}, u32[]{:S(2)}) async-start(bf16[32,2,48,128]{3,2,1,0:T(8,128)(2,1)} %first.2), calls=%async_computation.2 | async-start | bytes 1572864 | tf_op jit(solution)/shard_map/all_to_all | solution.py:501
  45.4 18.0 %first.3 = bf16[32,2,48,128]{3,2,1,0:T(8,128)(2,1)} custom-call(bf16[32,192,128]{2,1,0:T(8,128)(2,1)} %after.3, bf16[32,192,128]{2,1,0:T(8,128)(2,1)} %after.3, bf16[32,192,128]{2,1,0:T(8,128)(2,1)} %after.3, bf16[256,128]{1,0:T(8,128)(2,1)} %copy-done.17, bf16[256,128]{1,0:T(8,128)(2,1)} %copy-done.18, bf16[32,192]{1,0:T(8,128)(2,1)} %copy-done.3, ...), custom_call_target="tpu_custom_call" | custom-call | flops 4096000000 | bytes 1638400 | tf_op jit(solution)/shard_map/first/pallas_call | solution.py:391
  63.4 0.0 copy-start.13
  63.4 0.0 copy-start.15
  63.4 0.0 all-to-all-done.2.inp
  63.5 10.0 %all-to-all-start.1 = ((bf16[32,2,48,128]{3,2,1,0:T(8,128)(2,1)}), bf16[32,2,48,128]{3,2,1,0:T(8,128)(2,1)S(1)}, u32[]{:S(2)}, u32[]{:S(2)}) async-start(bf16[32,2,48,128]{3,2,1,0:T(8,128)(2,1)} %first.3), calls=%async_computation.1 | async-start | bytes 1572864 | tf_op jit(solution)/shard_map/all_to_all | solution.py:503
  73.4 5.3 %grid.2.rest_0_ = bf16[32,4,48,128]{3,2,1,0:T(8,128)(2,1)S(1)} custom-call(bf16[32,2,48,128]{3,2,1,0:T(8,128)(2,1)S(1)} %all-to-all-done.2.inp, bf16[192,576]{1,0:T(8,128)(2,1)S(1)} %copy-done.11, bf16[192,192]{1,0:T(8,128)(2,1)S(1)} %copy-done.13, f32[6,15,15]{2,1,0:T(8,128)S(1)} %copy-done.15), custom_call_target="tpu_custom_call" | custom-call | flops 2048000000 | bytes 1638400 | tf_op jit(solution)/shard_map/grid/pallas_call | solution.py:431
  78.8 11.6 %all-to-all-done.1.inp = bf16[32,2,48,128]{3,2,1,0:T(8,128)(2,1)S(1)} async-done(((bf16[32,2,48,128]{3,2,1,0:T(8,128)(2,1)}), bf16[32,2,48,128]{3,2,1,0:T(8,128)(2,1)S(1)}, u32[]{:S(2)}, u32[]{:S(2)}) %all-to-all-start.1) | async-done | bytes 786464 | tf_op jit(solution)/shard_map/all_to_all | solution.py:503
  90.4 5.3 %grid.3 = bf16[32,4,48,128]{3,2,1,0:T(8,128)(2,1)S(1)} custom-call(bf16[32,2,48,128]{3,2,1,0:T(8,128)(2,1)S(1)} %all-to-all-done.1.inp, bf16[192,576]{1,0:T(8,128)(2,1)S(1)} %copy-done.11, bf16[192,192]{1,0:T(8,128)(2,1)S(1)} %copy-done.13, f32[6,15,15]{2,1,0:T(8,128)S(1)} %copy-done.15, ...), custom_call_target="tpu_custom_call", output_to_operand_aliasing={{}: (4, {})} | custom-call | flops 2048000000 | bytes 1638400 | tf_op jit(solution)/shard_map/grid/pallas_call | solution.py:431
  95.7 0.0 copy-start.8
  95.7 0.0 copy-start.9
  95.7 28.8 %all_to_all.21.inp = bf16[32,4,48,128]{3,2,1,0:T(8,128)(2,1)S(1)} all-to-all(bf16[32,4,48,128]{3,2,1,0:T(8,128)(2,1)S(1)} %grid.3), channel_id=1, replica_groups=mesh['y'=4,'zh'=2,'zl'=2,'xl'=2,'xh'=2,'core'=2] {'y','zh','xh','core'}, dimensions={0} | all-to-all | bytes 3145728 | tf_op jit(solution)/shard_map/all_to_all | solution.py:507
  124.5 5.8 %last.1 = bf16[32,192,128]{2,1,0:T(8,128)(2,1)} custom-call(bf16[32,4,48,128]{3,2,1,0:T(8,128)(2,1)S(1)} %all_to_all.21.inp, bf16[192,768]{1,0:T(8,128)(2,1)S(1)} %copy-done.8, bf16[192,768]{1,0:T(8,128)(2,1)S(1)} %copy-done.9), custom_call_target="tpu_custom_call" | custom-call | flops 4096000000 | bytes 3276800 | tf_op jit(solution)/shard_map/last/pallas_call | solution.py:452
  (27 shorter events, 0.1 us)
Async XLA Ops:
  0.0 1.4 %copy-start = (bf16[32,192,128]{2,1,0:T(8,128)(2,1)S(1)}, bf16[32,192,128]{2,1,0:T(8,128)(2,1)}, u32[]{:S(2)}) copy-start(bf16[32,192,128]{2,1,0:T(8,128)(2,1)} %after.3) | copy-start | bytes 4718596
  12.6 3.9 %copy-start.2 = (bf16[32,192]{1,0:T(8,128)(2,1)}, bf16[32,192]{1,0:T(8,128)(2,1)S(1)}, u32[]{:S(2)}) copy-start(bf16[32,192]{1,0:T(8,128)(2,1)S(1)} %get-tuple-element.15.right) | copy-start | bytes 36868
  12.6 3.9 %copy-start.3 = (bf16[32,192]{1,0:T(8,128)(2,1)}, bf16[32,192]{1,0:T(8,128)(2,1)S(1)}, u32[]{:S(2)}) copy-start(bf16[32,192]{1,0:T(8,128)(2,1)S(1)} %get-tuple-element.16.left) | copy-start | bytes 36868
  12.6 3.9 %copy-start.1 = (bf16[32,192,128]{2,1,0:T(8,128)(2,1)S(1)}, bf16[32,192,128]{2,1,0:T(8,128)(2,1)}, u32[]{:S(2)}) copy-start(bf16[32,192,128]{2,1,0:T(8,128)(2,1)} %after.3) | copy-start | bytes 4718596
  12.6 3.9 %copy-start.4 = (bf16[192,768]{1,0:T(8,128)(2,1)S(1)}, bf16[192,768]{1,0:T(8,128)(2,1)}, u32[]{:S(2)}) copy-start(bf16[192,768]{1,0:T(8,128)(2,1)} %w_expand.3) | copy-start | bytes 884740
  12.6 3.9 %copy-start.5 = (bf16[192,768]{1,0:T(8,128)(2,1)S(1)}, bf16[192,768]{1,0:T(8,128)(2,1)}, u32[]{:S(2)}) copy-start(bf16[192,768]{1,0:T(8,128)(2,1)} %w_project.3) | copy-start | bytes 884740
  12.7 3.9 %copy-start.6 = (bf16[192,768]{1,0:T(8,128)(2,1)S(1)}, bf16[192,768]{1,0:T(8,128)(2,1)}, u32[]{:S(2)}) copy-start(bf16[192,768]{1,0:T(8,128)(2,1)} %w_in.4) | copy-start | bytes 884740
  12.7 3.9 %copy-start.7 = (bf16[192,768]{1,0:T(8,128)(2,1)S(1)}, bf16[192,768]{1,0:T(8,128)(2,1)}, u32[]{:S(2)}) copy-start(bf16[192,768]{1,0:T(8,128)(2,1)} %w_back.4) | copy-start | bytes 884740
  12.7 3.9 %copy-start.10 = (bf16[192,576]{1,0:T(8,128)(2,1)S(1)}, bf16[192,576]{1,0:T(8,128)(2,1)}, u32[]{:S(2)}) copy-start(bf16[192,576]{1,0:T(8,128)(2,1)} %w_qkv.5) | copy-start | bytes 663556
  12.7 3.8 %copy-start.12 = (bf16[192,192]{1,0:T(8,128)(2,1)S(1)}, bf16[192,192]{1,0:T(8,128)(2,1)}, u32[]{:S(2)}) copy-start(bf16[192,192]{1,0:T(8,128)(2,1)} %w_out.5) | copy-start | bytes 221188
  12.7 3.8 %copy-start.14 = (f32[6,15,15]{2,1,0:T(8,128)S(1)}, f32[6,15,15]{2,1,0:T(8,128)}, u32[]{:S(2)}) copy-start(f32[6,15,15]{2,1,0:T(8,128)} %table.5) | copy-start | bytes 16204
  12.7 3.8 %copy-start.16 = (bf16[3,3,768]{2,1,0:T(4,128)(2,1)S(1)}, bf16[3,3,768]{2,1,0:T(4,128)(2,1)}, u32[]{:S(2)}) copy-start(bf16[3,3,768]{2,1,0:T(4,128)(2,1)} %taps.3) | copy-start | bytes 41476
  12.8 20.5 %collective-permute-start = (bf16[256,128]{1,0:T(8,128)(2,1)S(1)}, bf16[256,128]{1,0:T(8,128)(2,1)S(1)}, u32[]{:S(2)}, u32[]{:S(2)}) collective-permute-start(bf16[256,128]{1,0:T(8,128)(2,1)S(1)} %get-tuple-element.10.top), channel_id=1, source_target_pairs={{0,4},{4,8},{8,12},{12,16},{16,20},{20,24},{24,28},{28,32},{32,36}... | collective-permute-start | bytes 196616 | tf_op jit(solution)/shard_map/ppermute | solution.py:472
  15.2 18.1 %collective-permute-start.1 = (bf16[256,128]{1,0:T(8,128)(2,1)S(1)}, bf16[256,128]{1,0:T(8,128)(2,1)S(1)}, u32[]{:S(2)}, u32[]{:S(2)}) collective-permute-start(bf16[256,128]{1,0:T(8,128)(2,1)S(1)} %get-tuple-element.11.bottom), channel_id=1, source_target_pairs={{4,0},{8,4},{12,8},{16,12},{20,16},{24,20},{28,24},{32,28},{36,32}... | collective-permute-start | bytes 196616 | tf_op jit(solution)/shard_map/ppermute | solution.py:472
  33.3 12.1 %copy-start.17 = (bf16[256,128]{1,0:T(8,128)(2,1)}, bf16[256,128]{1,0:T(8,128)(2,1)S(1)}, u32[]{:S(2)}) copy-start(bf16[256,128]{1,0:T(8,128)(2,1)S(1)} %collective-permute-done.top) | copy-start | bytes 196612
  33.3 12.1 %copy-start.18 = (bf16[256,128]{1,0:T(8,128)(2,1)}, bf16[256,128]{1,0:T(8,128)(2,1)S(1)}, u32[]{:S(2)}) copy-start(bf16[256,128]{1,0:T(8,128)(2,1)S(1)} %collective-permute-done.1.bottom) | copy-start | bytes 196612
  33.3 30.1 %all-to-all-start.2 = ((bf16[32,2,48,128]{3,2,1,0:T(8,128)(2,1)}), bf16[32,2,48,128]{3,2,1,0:T(8,128)(2,1)S(1)}, u32[]{:S(2)}, u32[]{:S(2)}) async-start(bf16[32,2,48,128]{3,2,1,0:T(8,128)(2,1)} %first.2), calls=%async_computation.2 | async-start | bytes 1572864 | tf_op jit(solution)/shard_map/all_to_all | solution.py:501
  63.4 10.0 %copy-start.11 = (bf16[192,576]{1,0:T(8,128)(2,1)S(1)}, bf16[192,576]{1,0:T(8,128)(2,1)}, u32[]{:S(2)}) copy-start(bf16[192,576]{1,0:T(8,128)(2,1)} %w_qkv.7) | copy-start | bytes 663556
  63.4 10.0 %copy-start.13 = (bf16[192,192]{1,0:T(8,128)(2,1)S(1)}, bf16[192,192]{1,0:T(8,128)(2,1)}, u32[]{:S(2)}) copy-start(bf16[192,192]{1,0:T(8,128)(2,1)} %w_out.7) | copy-start | bytes 221188
  63.4 10.0 %copy-start.15 = (f32[6,15,15]{2,1,0:T(8,128)S(1)}, f32[6,15,15]{2,1,0:T(8,128)}, u32[]{:S(2)}) copy-start(f32[6,15,15]{2,1,0:T(8,128)} %table.7) | copy-start | bytes 16204
  63.5 26.9 %all-to-all-start.1 = ((bf16[32,2,48,128]{3,2,1,0:T(8,128)(2,1)}), bf16[32,2,48,128]{3,2,1,0:T(8,128)(2,1)S(1)}, u32[]{:S(2)}, u32[]{:S(2)}) async-start(bf16[32,2,48,128]{3,2,1,0:T(8,128)(2,1)} %first.3), calls=%async_computation.1 | async-start | bytes 1572864 | tf_op jit(solution)/shard_map/all_to_all | solution.py:503
  95.7 28.8 %copy-start.8 = (bf16[192,768]{1,0:T(8,128)(2,1)S(1)}, bf16[192,768]{1,0:T(8,128)(2,1)}, u32[]{:S(2)}) copy-start(bf16[192,768]{1,0:T(8,128)(2,1)} %w_in.5) | copy-start | bytes 884740
  95.7 28.8 %copy-start.9 = (bf16[192,768]{1,0:T(8,128)(2,1)S(1)}, bf16[192,768]{1,0:T(8,128)(2,1)}, u32[]{:S(2)}) copy-start(bf16[192,768]{1,0:T(8,128)(2,1)} %w_back.5) | copy-start | bytes 884740
